TPU v7x, 128 devices: a whole 4x4x4 slice. The times are simulated.
128 devices in a mesh: row: 16 (over z_hi, y, core), col: 8 (over z_lo, x).
Axes of the slice: x: 4, y: 4, z: 4 (z_hi: 2, z_lo: 2; z = z_hi * 2 + z_lo), core: 2. Of those that a mesh axis runs over, the one named last changes fastest.
Arguments:
- blocks: bfloat16 [512, 1024, 128], P('row', 'col'), may hold values from -6 to 6
- block_atom: int32 [512, 8], P('row', 'col'), may hold values from 0 to 63, as said below
- block_col: int32 [512, 8], P('row', 'col'), may hold values from 0 to 7
- block_count: int32 [16, 8], P('row', 'col'), may hold values from 0 to 32, as said below
Outputs:
- sign_step: float32 [8192, 8192], P('row', 'col')
Inputs may be any that keep to these rules, and one draw needn't show every extreme that they name: Entries from block_count on are padding. `block_atom`: used entries of one grid column name distinct blocks; one owner's list names at most 2 blocks of the block rows of any one grid row.
All inputs are finite; a program needn't handle non-finite values.
Results may differ from a plain program's by a relative error of at most 0.0045.
Values may be sent and summed in bfloat16 or wider, within the bound.
No kernel may reach another device: no remote copies, remote signals or barrier semaphores. Data moves between devices by JAX's collectives and lax.ppermute only.
A program may use at most 128 MiB of HBM per device.

v0:
```python
import functools

import jax
import jax.numpy as jnp
from jax import lax
from jax.experimental import pallas as pl
from jax.experimental.pallas import tpu as pltpu
from jax.sharding import PartitionSpec as P

BLOCK = 128
BR = 4
BC = 8
CAP = 2
META = 16
NONE = 64


def pack_kernel(atom, column, count, blocks, send, seen, place):
    groups = send.shape[0]
    slots = blocks.shape[0]
    send[...] = jnp.zeros_like(send)
    for group in range(groups):
        seen[group] = 0
        for turn in range(CAP):
            place[group * CAP + turn] = NONE

    @pl.loop(0, slots)
    def _(slot):
        @pl.when(slot < count[0, 0])
        def _():
            group = atom[slot] // BR
            turn = jnp.minimum(seen[group], CAP - 1)
            seen[group] = turn + 1
            place[group * CAP + turn] = atom[slot] % BR * BC + column[slot]
            start = pl.multiple_of(turn * BLOCK, BLOCK)
            send[group, pl.ds(start, BLOCK), :] = blocks[slot]

    row = lax.broadcasted_iota(jnp.int32, (META, BLOCK), 0)
    for group in range(groups):
        value = jnp.where(row == 0, place[group * CAP], place[group * CAP + 1])
        send[group, CAP * BLOCK :, :] = value.astype(jnp.float32).astype(send.dtype)


def unpack_kernel(received, tile, place_vector, place, sem):
    owners = received.shape[0]
    tile[...] = jnp.zeros_like(tile)
    lane = lax.broadcasted_iota(jnp.int32, (META, BLOCK), 1)
    places = jnp.full((META, BLOCK), NONE, jnp.int32)
    for owner in range(owners):
        value = received[owner, CAP * BLOCK :, :].astype(jnp.float32).astype(jnp.int32)
        places = jnp.where(lane == owner, value, places)
    place_vector[...] = places
    copy = pltpu.make_async_copy(place_vector, place, sem)
    copy.start()
    copy.wait()

    @pl.loop(0, owners)
    def _(owner):
        for turn in range(CAP):
            at = place[turn, owner]

            @pl.when(at < BR * BC)
            def _():
                top = pl.multiple_of(at // BC * BLOCK, BLOCK)
                left = pl.multiple_of(at % BC * BLOCK, BLOCK)
                block = received[owner, turn * BLOCK : (turn + 1) * BLOCK, :]
                tile[pl.ds(top, BLOCK), pl.ds(left, BLOCK)] = block


def local_tile(blocks, block_atom, block_col, block_count):
    owners = lax.axis_size("row")
    vmem = pl.BlockSpec(memory_space=pltpu.VMEM)
    smem = pl.BlockSpec(memory_space=pltpu.SMEM)
    send = pl.pallas_call(
        pack_kernel,
        out_shape=jax.ShapeDtypeStruct((owners, CAP * BLOCK + META, BLOCK), blocks.dtype),
        in_specs=[smem, smem, smem, vmem],
        out_specs=vmem,
        scratch_shapes=[pltpu.SMEM((owners,), jnp.int32), pltpu.SMEM((owners * CAP,), jnp.int32)],
        compiler_params=pltpu.CompilerParams(vmem_limit_bytes=16 << 20),
        name="pack",
    )(block_atom[:, 0], block_col[:, 0], block_count, blocks)
    received = lax.all_to_all(send, "row", 0, 0, tiled=True)
    return pl.pallas_call(
        unpack_kernel,
        out_shape=jax.ShapeDtypeStruct((BR * BLOCK, BC * BLOCK), blocks.dtype),
        in_specs=[vmem],
        out_specs=vmem,
        scratch_shapes=[
            pltpu.VMEM((META, BLOCK), jnp.int32),
            pltpu.SMEM((META, BLOCK), jnp.int32),
            pltpu.SemaphoreType.DMA,
        ],
        compiler_params=pltpu.CompilerParams(vmem_limit_bytes=16 << 20),
        name="unpack",
    )(received)


def product_kernel(factor, left_parts, right_parts, part, first_total, has_base, n_out, left_at, right_at, core, want, *refs):
    lefts, refs = refs[: len(left_parts)], refs[len(left_parts) :]
    n_right = sum(len(pieces) for chunk in right_parts for pieces in chunk)
    rights, refs = list(refs[:n_right]), refs[n_right:]
    if first_total:
        total_in, refs = refs[0], refs[1:]
    if has_base:
        base, refs = refs[0], refs[1:]
    outs, (held, staged, total, base_held, left_sems, right_sems, extra_sems) = refs[:n_out], refs[n_out:]
    places, (slots, depth, _) = held.shape[0], staged.shape
    copies = []
    for index, (left, (source, first, count)) in enumerate(zip(lefts, left_parts)):
        place = left_at[index] % places
        target = held.at[place, pl.ds(first, count)]
        copies.append(pltpu.make_async_copy(left.at[pl.ds(source, count)], target, left_sems.at[place]))
    loads = []
    for index, chunk in enumerate(right_parts):
        load = []
        for step, pieces in enumerate(chunk):
            down = (core[0] + step) % 2 * (depth // 2)
            for first, count in pieces:
                target = staged.at[index % slots, pl.ds(pl.multiple_of(down + first, count), count)]
                sem = right_sems.at[index % slots]
                load.append(pltpu.make_async_copy(rights.pop(0), target, sem))
        loads.append(load)

    def when_wanted(index, act):
        if part:
            pl.when(right_at[index] // places == want[0])(act)
        else:
            act()

    def start(index):
        for load in loads[index]:
            load.start()
        for at, copy in enumerate(copies):
            pl.when(left_at[at] == right_at[index])(copy.start)

    for index in range(slots - 1):
        when_wanted(index, functools.partial(start, index))
    if first_total:
        total_copy = pltpu.make_async_copy(total_in, total, extra_sems.at[0])
        total_copy.start()
    else:
        total[...] = jnp.zeros_like(total)
    if has_base:
        base_copy = pltpu.make_async_copy(base, base_held, extra_sems.at[1])
        base_copy.start()
    if first_total:
        total_copy.wait()

    @pl.loop(0, len(loads))
    def _(index):
        for ahead in range(slots - 1, len(loads)):

            @pl.when(index == ahead - slots + 1)
            def _():
                when_wanted(ahead, functools.partial(start, ahead))

        def add():
            place, slot = right_at[index] % places, index % slots
            pltpu.make_async_copy(held.at[place], held.at[place], left_sems.at[place]).wait()
            pltpu.make_async_copy(staged.at[slot], staged.at[slot], right_sems.at[slot]).wait()
            total[...] += jnp.dot(held[place], staged[slot], preferred_element_type=jnp.float32)

        when_wanted(index, add)

    if has_base:
        base_copy.wait()
    first = 0
    for out in outs:
        count = out.shape[0]
        value = total[first : first + count, :] * factor
        if has_base:
            value = 1.5 * base_held[first : first + count, :].astype(jnp.float32) - value
        out[...] = value.astype(out.dtype)
        first += count


def product(lefts, rights, core, outs, factor, dtype, name, part=None, first_total=None, base=None):
    width = lefts[0][0].shape[1]
    kind = lefts[0][0].dtype
    left_parts = [(source, first, count) for _, _, source, first, count in lefts]
    right_parts = [
        [[(first, array.shape[0]) for array, first in pieces] for pieces in chunk[1:]] for chunk in rights
    ]
    left_at = jnp.stack([chunk for _, chunk, *_ in lefts]).astype(jnp.int32)
    right_at = jnp.stack([chunk for chunk, *_ in rights]).astype(jnp.int32)
    want = jnp.asarray(0 if part is None else part, jnp.int32)[None]
    smem = pl.BlockSpec(memory_space=pltpu.SMEM)
    vmem = pl.BlockSpec(memory_space=pltpu.VMEM)
    hbm = pl.BlockSpec(memory_space=pltpu.HBM)
    arrays = [left for left, *_ in lefts]
    arrays += [array for chunk in rights for pieces in chunk[1:] for array, _ in pieces]
    extra = [value for value in (first_total, base) if value is not None]
    count = len(rights) if part is None else len(rights) // 2
    rows = sum(outs)
    slots = 5 if part is None else 8
    return pl.pallas_call(
        functools.partial(
            product_kernel,
            factor,
            left_parts,
            right_parts,
            part is not None,
            first_total is not None,
            base is not None,
            len(outs),
        ),
        out_shape=[jax.ShapeDtypeStruct((out, width), dtype) for out in outs],
        in_specs=[smem] * 4 + [hbm] * (len(arrays) + len(extra)),
        out_specs=[vmem] * len(outs),
        scratch_shapes=[
            pltpu.VMEM((count, rows, width), kind),
            pltpu.VMEM((slots, width, width), kind),
            pltpu.VMEM((rows, width), jnp.float32),
            pltpu.VMEM((rows, width), kind),
            pltpu.SemaphoreType.DMA((count,)),
            pltpu.SemaphoreType.DMA((slots,)),
            pltpu.SemaphoreType.DMA((2,)),
        ],
        compiler_params=pltpu.CompilerParams(vmem_limit_bytes=58 << 20),
        cost_estimate=pl.CostEstimate(
            flops=2 * rows * width * width * count, bytes_accessed=2 * width * count * (rows + width), transcendentals=0
        ),
        name=name,
    )(left_at, right_at, core.astype(jnp.int32)[None], want, *arrays, *extra)


def over_row(value, z_step, y_step, core_step):
    size = lax.axis_size("row")
    pairs = []
    for source in range(size):
        z, y, core = source // 8, source // 2 % 4, source % 2
        target = ((z + z_step) % 2 * 4 + (y + y_step) % 4) * 2 + (core + core_step) % 2
        pairs.append((source, target))
    return lax.ppermute(value, "row", pairs)


def over_col(value, z_step, x_step):
    size = lax.axis_size("col")
    pairs = []
    for source in range(size):
        z, x = source // 4, source % 4
        pairs.append((source, (z + z_step) % 2 * 4 + (x + x_step) % 4))
    return lax.ppermute(value, "col", pairs)


def x_shift(value, step):
    return over_col(value, 0, step)


def y_shift(value, step):
    return over_row(value, 0, step, 0)


def z_swap(value):
    return over_col(value, 1, 0)


def core_swap(value):
    return over_row(value, 0, 0, 1)


def after(values, *earlier):
    return lax.optimization_barrier((values, earlier))[0]


def near(value, shift):
    return shift(value, 1), shift(value, -1)


def far(below, above, shift):
    half = below.shape[0] // 2
    return shift(below[:half], 1), shift(above[half:], -1)


def local(blocks, block_atom, block_col, block_count):
    matrix = local_tile(blocks, block_atom, block_col, block_count)
    rows = matrix.shape[0]
    half = rows // 2
    quarter = half // 2
    row, col = lax.axis_index("row"), lax.axis_index("col")
    z_hi, y, core = row // 8, row // 2 % 4, row % 2
    z_lo, x = col // 4, col % 4

    def col_chunk(z_step, x_step):
        return (z_lo + z_step) % 2 * 4 + (x + x_step) % 4

    def row_chunk(z_step, y_step):
        return (z_hi + z_step) % 2 * 4 + (y + y_step) % 4

    top, bottom = matrix[:half], matrix[half:]
    other_z = over_row(matrix, 1, 0, 0)
    x_near = near(matrix, x_shift)
    y_near = near(matrix, y_shift)
    top, bottom, matrix_b, other_z, x_near, y_near = after((top, bottom, matrix, other_z, x_near, y_near))
    top_z = z_swap(top)
    x_far = far(*x_near, x_shift)
    y_far = far(*y_near, y_shift)
    swapped = {}
    swapped["own"] = core_swap(matrix_b)
    swapped["near"] = [core_swap(v) for v in y_near]
    bottom, top_z, x_far, y_far, other_z = after((bottom, top_z, x_far, y_far, other_z))
    w1, w2 = other_z[:half], other_z[half:]
    wm1, wp2 = y_shift(w1, 1), y_shift(w2, -1)
    bottom_z = z_swap(bottom)
    top_z_near = near(top_z, x_shift)
    bottom_z, top_z_near, wm1, wp2, w1, w2 = after((bottom_z, top_z_near, wm1, wp2, w1, w2))
    wm2, wp1 = y_shift(w2, 1), y_shift(w1, -1)
    bottom_z_near = near(bottom_z, x_shift)
    cross_top = x_shift(top_z_near[0], 1)
    wm1, wp2, wm2, wp1, bottom_z_near, y_far, other_z = after(
        (wm1, wp2, wm2, wp1, bottom_z_near, y_far, other_z)
    )
    z_far = y_shift(wm1, 1), y_shift(wp2, -1)
    cross_bottom = x_shift(bottom_z_near[1], -1)
    swapped["z"] = core_swap(other_z)
    swapped["far"] = [core_swap(v) for v in y_far]
    z_near = [(wm1, wm2), (wp1, wp2)]
    swapped["z near"] = [[core_swap(v) for v in pair] for pair in z_near]
    z_far, cross_bottom = after((z_far, cross_bottom))
    z_cross = cross_top, cross_bottom
    swapped["z far"] = [core_swap(v) for v in z_far]

    def in_two(pair):
        return [(pair[0], 0), (pair[1], half)]

    pieces = [
        (0, 0, [(matrix, 0)], [(swapped["own"], 0)]),
        (0, -1, [(y_near[0], 0)], [(swapped["near"][0], 0)]),
        (0, 1, [(y_near[1], 0)], [(swapped["near"][1], 0)]),
        (0, 2, [(y_far[0], 0), (y_far[1], half)], [(swapped["far"][0], 0), (swapped["far"][1], half)]),
        (1, 0, [(other_z, 0)], [(swapped["z"], 0)]),
        (1, -1, in_two(z_near[0]), in_two(swapped["z near"][0])),
        (1, 1, in_two(z_near[1]), in_two(swapped["z near"][1])),
        (1, 2, [(z_far[0], 0), (z_far[1], half)], [(swapped["z far"][0], 0), (swapped["z far"][1], half)]),
    ]
    chunks = [(row_chunk(z_step, y_step), mine, others) for z_step, y_step, mine, others in pieces]

    def strip(z_step, own, near_two, far_parts):
        parts = [
            (value, col_chunk(z_step, step), 0, 0, half) for value, step in zip((own, *near_two), (0, -1, 1))
        ]
        count = half // len(far_parts)
        return parts + [
            (value, col_chunk(z_step, 2), 0, index * count, count) for index, value in enumerate(far_parts)
        ]

    factor = 0.5 / (matrix.shape[1] * lax.axis_size("col"))
    kind = matrix.dtype
    def both(z_step, first, second):
        parts = []
        for below, (own, near_two, far_two) in ((0, first), (half, second)):
            for array, chunk, source, row_at, count in strip(z_step, own, near_two, far_two):
                parts.append((array, chunk, source, row_at + below, count))
        return parts

    lefts = [(value, col_chunk(0, step), 0, 0, rows) for value, step in ((matrix, 0), (x_near[0], -1), (x_near[1], 1))]
    lefts += [(value, col_chunk(0, 2), 0, index * half, half) for index, value in enumerate(x_far)]
    for below, own, two, cross in ((0, top_z, top_z_near, z_cross[0]), (half, bottom_z, bottom_z_near, z_cross[1])):
        for value, step in ((own, 0), (two[0], -1), (two[1], 1), (cross, 2)):
            lefts.append((value, col_chunk(1, step), 0, below, half))
    h1, h2 = product(lefts, chunks, core, [half, half], factor, kind, "square")
    h2_z, h1_z = z_swap(h2), z_swap(h1)
    h1_near, h2_near = near(h1, x_shift), near(h2, x_shift)
    h1_near, h2_near, h1_z, h2_z, h1, h2 = after((h1_near, h2_near, h1_z, h2_z, h1, h2))
    h1_far, h2_far = x_shift(h1_near[0], 1), x_shift(h2_near[1], -1)
    h1_z_near = [z_swap(v) for v in h1_near]
    h1_far, h2_far, h2_z = after((h1_far, h2_far, h2_z))
    h2_z_near = near(h2_z, x_shift)
    h1_z_far = z_swap(h1_far)
    h2_z_near, h1_z_near = after((h2_z_near, h1_z_near))
    h2_z_far = far(*h2_z_near, x_shift)
    h1_far, h2_far, h1_z_far = [h1_far], [h2_far], [h1_z_far]

    lefts = both(0, (h1, h1_near, h1_far), (h2, h2_near, h2_far))
    (total,) = product(lefts, chunks, core, [rows], 1.0, jnp.float32, "step_first", z_lo)
    late = (h1_z, h1_z_near, h1_z_far, h2_z, h2_z_near, h2_z_far)
    h1_z, h1_z_near, h1_z_far, h2_z, h2_z_near, h2_z_far = after(late, total)
    lefts = both(1, (h1_z, h1_z_near, h1_z_far), (h2_z, h2_z_near, h2_z_far))
    (out,) = product(lefts, chunks, core, [rows], 1.0, jnp.float32, "step_last", 1 - z_lo, total, matrix)
    return out


def solution(mesh):
    placed = (P("row", "col", None), P("row", "col"), P("row", "col"), P("row", "col"))
    return jax.shard_map(
        local, mesh=mesh, in_specs=placed, out_specs=P("row", "col"), check_vma=False
    )
```

profile of v0, /device:TPU:0, one launch (start us, length us, event | category | flops | bytes accessed | tf_op | source)
XLA Modules:
  0.0 242.6 jit_solution(10411120153045839735)
XLA Ops:
  4.7 26.4 %all_to_all.5.received = bf16[16,272,128]{2,1,0:T(8,128)(2,1)S(1)} all-to-all(bf16[16,272,128]{2,1,0:T(8,128)(2,1)S(1)} %pack.1), channel_id=1, replica_groups=mesh['row'=16,'col'=8] {'row'}, dimensions={0} | all-to-all | bytes 2228224 | tf_op jit(solution)/shard_map/all_to_all | solution.py:83
  34.5 2.9 %collective-permute-start.2 = (bf16[512,1024]{1,0:T(8,128)(2,1)S(1)}, bf16[512,1024]{1,0:T(8,128)(2,1)S(1)}, u32[]{:S(2)}, u32[]{:S(2)}) collective-permute-start(bf16[512,1024]{1,0:T(8,128)(2,1)S(1)} %unpack.1.refs_0_.refs_13_.refs_8_.refs_9_.refs_34_), channel_id=1, source_target_pairs={{0,3},{1,0},{2,1},{3,2},{4,7},{5,4},{6,5},{7,6},{8,11},{9,8},{10,9... | collective-permute-start | bytes 3145736 | tf_op jit(solution)/shard_map/ppermute | solution.py:244
  38.2 19.5 %collective-permute-done.4.refs_17_.refs_12_.refs_13_ = bf16[512,1024]{1,0:T(8,128)(2,1)S(1)} collective-permute-done((bf16[512,1024]{1,0:T(8,128)(2,1)S(1)}, bf16[512,1024]{1,0:T(8,128)(2,1)S(1)}, u32[]{:S(2)}, u32[]{:S(2)}) %collective-permute-start.4) | collective-permute-done | bytes 1048608 | tf_op jit(solution)/shard_map/ppermute | solution.py:235
  57.7 2.2 collective-permute-done.3.refs_15_.refs_10_.refs_11_
  59.9 3.1 %collective-permute-done.1.refs_1_ = bf16[512,1024]{1,0:T(8,128)(2,1)S(1)} collective-permute-done((bf16[512,1024]{1,0:T(8,128)(2,1)S(1)}, bf16[512,1024]{1,0:T(8,128)(2,1)S(1)}, u32[]{:S(2)}, u32[]{:S(2)}) %collective-permute-start.1) | collective-permute-done | bytes 1048608 | tf_op jit(solution)/shard_map/ppermute | solution.py:244
  64.0 2.4 %collective-permute-start.9 = (bf16[256,1024]{1,0:T(8,128)(2,1)S(1)}, bf16[256,1024]{1,0:T(8,128)(2,1)S(1)}, u32[]{:S(2)}, u32[]{:S(2)}) collective-permute-start(bf16[256,1024]{1,0:T(8,128)(2,1)S(1)} %slice.35), channel_id=1, source_target_pairs={{0,48},{8,56},{16,0},{24,8},{32,16},{40,24},{48,32},{56,40},{64,11... | collective-permute-start | bytes 1572872 | tf_op jit(solution)/shard_map/ppermute | solution.py:235
  66.4 2.5 %collective-permute-start.7 = (bf16[256,1024]{1,0:T(8,128)(2,1)S(1)}, bf16[256,1024]{1,0:T(8,128)(2,1)S(1)}, u32[]{:S(2)}, u32[]{:S(2)}) collective-permute-start(bf16[256,1024]{1,0:T(8,128)(2,1)S(1)} %slice.33), channel_id=1, source_target_pairs={{0,3},{1,0},{2,1},{3,2},{4,7},{5,4},{6,5},{7,6},{8,11},{9,8},{10,9... | collective-permute-start | bytes 1572872 | tf_op jit(solution)/shard_map/ppermute | solution.py:244
  69.7 6.5 %collective-permute-done.9.refs_20_.refs_15_.refs_16_ = bf16[256,1024]{1,0:T(8,128)(2,1)S(1)} collective-permute-done((bf16[256,1024]{1,0:T(8,128)(2,1)S(1)}, bf16[256,1024]{1,0:T(8,128)(2,1)S(1)}, u32[]{:S(2)}, u32[]{:S(2)}) %collective-permute-start.9) | collective-permute-done | bytes 524320 | tf_op jit(solution)/shard_map/ppermute | solution.py:235
  76.2 3.3 %collective-permute-done.8.refs_19_.refs_14_.refs_15_ = bf16[256,1024]{1,0:T(8,128)(2,1)S(1)} collective-permute-done((bf16[256,1024]{1,0:T(8,128)(2,1)S(1)}, bf16[256,1024]{1,0:T(8,128)(2,1)S(1)}, u32[]{:S(2)}, u32[]{:S(2)}) %collective-permute-start.8) | collective-permute-done | bytes 524320 | tf_op jit(solution)/shard_map/ppermute | solution.py:235
  79.5 2.0 collective-permute-done.6.refs_3_
  84.5 3.0 %collective-permute-start.14 = (bf16[256,1024]{1,0:T(8,128)(2,1)S(1)}, bf16[256,1024]{1,0:T(8,128)(2,1)}, u32[]{:S(2)}, u32[]{:S(2)}) collective-permute-start(bf16[256,1024]{1,0:T(8,128)(2,1)S(1)} %get-tuple-element.82), channel_id=1, source_target_pairs={{0,48},{8,56},{16,0},{24,8},{32,16},{40,24},{48,32},{56,40},{64,11... | collective-permute-start | bytes 1572872 | tf_op jit(solution)/shard_map/ppermute | solution.py:235
  87.5 5.9 %collective-permute-done.10.refs_9_ = bf16[256,1024]{1,0:T(8,128)(2,1)S(1)} collective-permute-done((bf16[256,1024]{1,0:T(8,128)(2,1)S(1)}, bf16[256,1024]{1,0:T(8,128)(2,1)S(1)}, u32[]{:S(2)}, u32[]{:S(2)}) %collective-permute-start.10) | collective-permute-done | bytes 524320 | tf_op jit(solution)/shard_map/ppermute | solution.py:244
  94.3 5.4 %collective-permute-done.13.refs_25_.refs_20_.refs_21_ = bf16[256,1024]{1,0:T(8,128)(2,1)} collective-permute-done((bf16[256,1024]{1,0:T(8,128)(2,1)S(1)}, bf16[256,1024]{1,0:T(8,128)(2,1)}, u32[]{:S(2)}, u32[]{:S(2)}) %collective-permute-start.13) | collective-permute-done | bytes 524320 | tf_op jit(solution)/shard_map/ppermute | solution.py:235
  99.8 3.2 %collective-permute-start.17 = (bf16[256,1024]{1,0:T(8,128)(2,1)S(1)}, bf16[256,1024]{1,0:T(8,128)(2,1)S(1)}, u32[]{:S(2)}, u32[]{:S(2)}) collective-permute-start(bf16[256,1024]{1,0:T(8,128)(2,1)S(1)} %get-tuple-element.83), channel_id=1, source_target_pairs={{0,48},{8,56},{16,0},{24,8},{32,16},{40,24},{48,32},{56,40},{64,11... | collective-permute-start | bytes 1572872 | tf_op jit(solution)/shard_map/ppermute | solution.py:235
  103.5 3.3 %collective-permute-start.19 = (bf16[256,1024]{1,0:T(8,128)(2,1)S(1)}, bf16[256,1024]{1,0:T(8,128)(2,1)S(1)}, u32[]{:S(2)}, u32[]{:S(2)}) collective-permute-start(bf16[256,1024]{1,0:T(8,128)(2,1)S(1)} %collective-permute-done.10.refs_9_), channel_id=1, source_target_pairs={{0,3},{1,0},{2,1},{3,2},{4,7},{5,4},{6,5},{7,6},{8,11},{9,8},{10,9... | collective-permute-start | bytes 1572872 | tf_op jit(solution)/shard_map/ppermute | solution.py:244
  106.8 3.3 %collective-permute-done.16.refs_26_.refs_21_.refs_22_ = bf16[256,1024]{1,0:T(8,128)(2,1)S(1)} collective-permute-done((bf16[256,1024]{1,0:T(8,128)(2,1)S(1)}, bf16[256,1024]{1,0:T(8,128)(2,1)S(1)}, u32[]{:S(2)}, u32[]{:S(2)}) %collective-permute-start.16) | collective-permute-done | bytes 524320 | tf_op jit(solution)/shard_map/ppermute | solution.py:235
  110.3 8.0 %collective-permute-done.19.refs_11_ = bf16[256,1024]{1,0:T(8,128)(2,1)S(1)} collective-permute-done((bf16[256,1024]{1,0:T(8,128)(2,1)S(1)}, bf16[256,1024]{1,0:T(8,128)(2,1)S(1)}, u32[]{:S(2)}, u32[]{:S(2)}) %collective-permute-start.19) | collective-permute-done | bytes 524320 | tf_op jit(solution)/shard_map/ppermute | solution.py:244
  118.3 3.4 %collective-permute-done.18.refs_10_ = bf16[256,1024]{1,0:T(8,128)(2,1)S(1)} collective-permute-done((bf16[256,1024]{1,0:T(8,128)(2,1)S(1)}, bf16[256,1024]{1,0:T(8,128)(2,1)S(1)}, u32[]{:S(2)}, u32[]{:S(2)}) %collective-permute-start.18) | collective-permute-done | bytes 524320 | tf_op jit(solution)/shard_map/ppermute | solution.py:244
  122.7 3.2 %collective-permute-start.21 = (bf16[256,1024]{1,0:T(8,128)(2,1)}, bf16[256,1024]{1,0:T(8,128)(2,1)}, u32[]{:S(2)}, u32[]{:S(2)}) collective-permute-start(bf16[256,1024]{1,0:T(8,128)(2,1)} %collective-permute-done.14.refs_30_.refs_25_.refs_26_), channel_id=1, source_target_pairs={{0,48},{8,56},{16,0},{24,8},{32,16},{40,24},{48,32},{56,40},{64,11... | collective-permute-start | bytes 1572872 | tf_op jit(solution)/shard_map/ppermute | solution.py:235
  125.9 7.4 %collective-permute-done.15.refs_8_ = bf16[256,1024]{1,0:T(8,128)(2,1)S(1)} collective-permute-done((bf16[256,1024]{1,0:T(8,128)(2,1)S(1)}, bf16[256,1024]{1,0:T(8,128)(2,1)S(1)}, u32[]{:S(2)}, u32[]{:S(2)}) %collective-permute-start.15) | collective-permute-done | bytes 524320 | tf_op jit(solution)/shard_map/ppermute | solution.py:244
  133.8 2.6 %collective-permute-done.20.refs_33_.refs_28_.refs_29_ = bf16[256,1024]{1,0:T(8,128)(2,1)} collective-permute-done((bf16[256,1024]{1,0:T(8,128)(2,1)}, bf16[256,1024]{1,0:T(8,128)(2,1)}, u32[]{:S(2)}, u32[]{:S(2)}) %collective-permute-start.20) | collective-permute-done | bytes 524320 | tf_op jit(solution)/shard_map/ppermute | solution.py:235
  144.1 15.9 %square.1 = (bf16[256,1024]{1,0:T(8,128)(2,1)}, bf16[256,1024]{1,0:T(8,128)(2,1)}) custom-call(s32[13]{0:T(128)} %stack.58.left_at, s32[8]{0:T(128)} %stack.53.right_at, s32[1]{0:T(128)} %bitcast.12.core, s32[1]{0:T(128)} %constant.244.clone.1.want, bf16[512,1024]{1,0:T(8,128)(2,1)} %copy-done, bf16[512,1024]{1,0:T(8,128)(2,1)} %copy-done.28, ...), custom_call_target="tpu_custom_call" | custom-call | flops 8589934592 | bytes 25165824 | tf_op jit(solution)/shard_map/square/pallas_call | solution.py:197
  164.2 3.2 %collective-permute-start.38 = (bf16[256,1024]{1,0:T(8,128)(2,1)}, bf16[256,1024]{1,0:T(8,128)(2,1)S(1)}, u32[]{:S(2)}, u32[]{:S(2)}) collective-permute-start(bf16[256,1024]{1,0:T(8,128)(2,1)} %get-tuple-element.113.refs_4_), channel_id=1, source_target_pairs={{0,3},{1,0},{2,1},{3,2},{4,7},{5,4},{6,5},{7,6},{8,11},{9,8},{10,9... | collective-permute-start | bytes 1572872 | tf_op jit(solution)/shard_map/ppermute | solution.py:244
  167.4 7.7 %collective-permute-done.39.refs_0_ = bf16[256,1024]{1,0:T(8,128)(2,1)S(1)} collective-permute-done((bf16[256,1024]{1,0:T(8,128)(2,1)}, bf16[256,1024]{1,0:T(8,128)(2,1)S(1)}, u32[]{:S(2)}, u32[]{:S(2)}) %collective-permute-start.39) | collective-permute-done | bytes 524320 | tf_op jit(solution)/shard_map/ppermute | solution.py:244
  177.3 8.3 %collective-permute-done.40.refs_4_ = bf16[256,1024]{1,0:T(8,128)(2,1)} collective-permute-done((bf16[256,1024]{1,0:T(8,128)(2,1)}, bf16[256,1024]{1,0:T(8,128)(2,1)}, u32[]{:S(2)}, u32[]{:S(2)}) %collective-permute-start.40) | collective-permute-done | bytes 524320 | tf_op jit(solution)/shard_map/ppermute | solution.py:244
  185.7 3.2 %collective-permute-done.37.refs_5_ = bf16[256,1024]{1,0:T(8,128)(2,1)S(1)} collective-permute-done((bf16[256,1024]{1,0:T(8,128)(2,1)}, bf16[256,1024]{1,0:T(8,128)(2,1)S(1)}, u32[]{:S(2)}, u32[]{:S(2)}) %collective-permute-start.37) | collective-permute-done | bytes 524320 | tf_op jit(solution)/shard_map/ppermute | solution.py:244
  192.9 7.4 %collective-permute-done.42.refs_7_ = bf16[256,1024]{1,0:T(8,128)(2,1)S(1)} collective-permute-done((bf16[256,1024]{1,0:T(8,128)(2,1)S(1)}, bf16[256,1024]{1,0:T(8,128)(2,1)S(1)}, u32[]{:S(2)}, u32[]{:S(2)}) %collective-permute-start.42) | collective-permute-done | bytes 524320 | tf_op jit(solution)/shard_map/ppermute | solution.py:244
  200.3 2.8 %collective-permute-done.41.refs_3_ = bf16[256,1024]{1,0:T(8,128)(2,1)} collective-permute-done((bf16[256,1024]{1,0:T(8,128)(2,1)S(1)}, bf16[256,1024]{1,0:T(8,128)(2,1)}, u32[]{:S(2)}, u32[]{:S(2)}) %collective-permute-start.41) | collective-permute-done | bytes 524320 | tf_op jit(solution)/shard_map/ppermute | solution.py:244
  207.7 9.4 %collective-permute-done.46.refs_2_ = bf16[256,1024]{1,0:T(8,128)(2,1)} collective-permute-done((bf16[256,1024]{1,0:T(8,128)(2,1)S(1)}, bf16[256,1024]{1,0:T(8,128)(2,1)}, u32[]{:S(2)}, u32[]{:S(2)}) %collective-permute-start.46) | collective-permute-done | bytes 524320 | tf_op jit(solution)/shard_map/ppermute | solution.py:244
  217.2 2.1 collective-permute-start.49
  219.3 10.4 %step_first.1.refs_33_ = f32[512,1024]{1,0:T(8,128)} custom-call(s32[8]{0:T(128)} %stack.59.left_at, s32[8]{0:T(128)} %stack.53.right_at, s32[1]{0:T(128)} %bitcast.12.core, s32[1]{0:T(128)} %bitcast.20.want, bf16[256,1024]{1,0:T(8,128)(2,1)} %get-tuple-element.112.refs_0_, bf16[256,1024]{1,0:T(8,128)(2,1)} %copy-done.22, bf16[256,1024]{1,0:T(8,128)(2,1)} %copy-done.21, ...), custom_call_target="tpu_custom_call" | custom-call | flops 4294967296 | bytes 12582912 | tf_op jit(solution)/shard_map/step_first/pallas_call | solution.py:197
  230.6 11.8 %step_last.1 = f32[512,1024]{1,0:T(8,128)} custom-call(s32[9]{0:T(128)} %stack.44.left_at, s32[8]{0:T(128)} %stack.53.right_at, s32[1]{0:T(128)} %bitcast.12.core, s32[1]{0:T(128)} %bitcast.13.want, bf16[256,1024]{1,0:T(8,128)(2,1)} %copy-done.26, bf16[256,1024]{1,0:T(8,128)(2,1)} %collective-permute-done.45.refs_1_, ...), custom_call_target="tpu_custom_call" | custom-call | flops 4294967296 | bytes 12582912 | tf_op jit(solution)/shard_map/step_last/pallas_call | solution.py:197
  (166 shorter events, 39.4 us)
Async XLA Ops:
  32.4 25.2 %collective-permute-start.4 = (bf16[512,1024]{1,0:T(8,128)(2,1)S(1)}, bf16[512,1024]{1,0:T(8,128)(2,1)S(1)}, u32[]{:S(2)}, u32[]{:S(2)}) collective-permute-start(bf16[512,1024]{1,0:T(8,128)(2,1)S(1)} %unpack.1.refs_0_.refs_13_.refs_8_.refs_9_.refs_34_), channel_id=1, source_target_pairs={{0,48},{8,56},{16,0},{24,8},{32,16},{40,24},{48,32},{56,40},{64,11... | collective-permute-start | bytes 3145736 | tf_op jit(solution)/shard_map/ppermute | solution.py:235
  33.7 26.2 %collective-permute-start.3 = (bf16[512,1024]{1,0:T(8,128)(2,1)S(1)}, bf16[512,1024]{1,0:T(8,128)(2,1)S(1)}, u32[]{:S(2)}, u32[]{:S(2)}) collective-permute-start(bf16[512,1024]{1,0:T(8,128)(2,1)S(1)} %unpack.1.refs_0_.refs_13_.refs_8_.refs_9_.refs_34_), channel_id=1, source_target_pairs={{0,16},{8,24},{16,32},{24,40},{32,48},{40,56},{48,0},{56,8},{64,80... | collective-permute-start | bytes 3145736 | tf_op jit(solution)/shard_map/ppermute | solution.py:235
  34.5 25.4 %collective-permute-start.2 = (bf16[512,1024]{1,0:T(8,128)(2,1)S(1)}, bf16[512,1024]{1,0:T(8,128)(2,1)S(1)}, u32[]{:S(2)}, u32[]{:S(2)}) collective-permute-start(bf16[512,1024]{1,0:T(8,128)(2,1)S(1)} %unpack.1.refs_0_.refs_13_.refs_8_.refs_9_.refs_34_), channel_id=1, source_target_pairs={{0,3},{1,0},{2,1},{3,2},{4,7},{5,4},{6,5},{7,6},{8,11},{9,8},{10,9... | collective-permute-start | bytes 3145736 | tf_op jit(solution)/shard_map/ppermute | solution.py:244
  37.4 25.6 %collective-permute-start.1 = (bf16[512,1024]{1,0:T(8,128)(2,1)S(1)}, bf16[512,1024]{1,0:T(8,128)(2,1)S(1)}, u32[]{:S(2)}, u32[]{:S(2)}) collective-permute-start(bf16[512,1024]{1,0:T(8,128)(2,1)S(1)} %unpack.1.refs_0_.refs_13_.refs_8_.refs_9_.refs_34_), channel_id=1, source_target_pairs={{0,1},{1,2},{2,3},{3,0},{4,5},{5,6},{6,7},{7,4},{8,9},{9,10},{10,1... | collective-permute-start | bytes 3145736 | tf_op jit(solution)/shard_map/ppermute | solution.py:244
  37.4 25.9 %collective-permute-start = (bf16[512,1024]{1,0:T(8,128)(2,1)S(1)}, bf16[512,1024]{1,0:T(8,128)(2,1)S(1)}, u32[]{:S(2)}, u32[]{:S(2)}) collective-permute-start(bf16[512,1024]{1,0:T(8,128)(2,1)S(1)} %unpack.1.refs_0_.refs_13_.refs_8_.refs_9_.refs_34_), channel_id=1, source_target_pairs={{0,64},{8,72},{16,80},{24,88},{32,96},{40,104},{48,112},{56,120},{... | collective-permute-start | bytes 3145736 | tf_op jit(solution)/shard_map/ppermute | solution.py:235
  64.0 12.2 %collective-permute-start.9 = (bf16[256,1024]{1,0:T(8,128)(2,1)S(1)}, bf16[256,1024]{1,0:T(8,128)(2,1)S(1)}, u32[]{:S(2)}, u32[]{:S(2)}) collective-permute-start(bf16[256,1024]{1,0:T(8,128)(2,1)S(1)} %slice.35), channel_id=1, source_target_pairs={{0,48},{8,56},{16,0},{24,8},{32,16},{40,24},{48,32},{56,40},{64,11... | collective-permute-start | bytes 1572872 | tf_op jit(solution)/shard_map/ppermute | solution.py:235
  66.4 13.1 %collective-permute-start.8 = (bf16[256,1024]{1,0:T(8,128)(2,1)S(1)}, bf16[256,1024]{1,0:T(8,128)(2,1)S(1)}, u32[]{:S(2)}, u32[]{:S(2)}) collective-permute-start(bf16[256,1024]{1,0:T(8,128)(2,1)S(1)} %slice.34), channel_id=1, source_target_pairs={{0,16},{8,24},{16,32},{24,40},{32,48},{40,56},{48,0},{56,8},{64,80... | collective-permute-start | bytes 1572872 | tf_op jit(solution)/shard_map/ppermute | solution.py:235
  66.4 13.1 %collective-permute-start.7 = (bf16[256,1024]{1,0:T(8,128)(2,1)S(1)}, bf16[256,1024]{1,0:T(8,128)(2,1)S(1)}, u32[]{:S(2)}, u32[]{:S(2)}) collective-permute-start(bf16[256,1024]{1,0:T(8,128)(2,1)S(1)} %slice.33), channel_id=1, source_target_pairs={{0,3},{1,0},{2,1},{3,2},{4,7},{5,4},{6,5},{7,6},{8,11},{9,8},{10,9... | collective-permute-start | bytes 1572872 | tf_op jit(solution)/shard_map/ppermute | solution.py:244
  69.0 12.5 %collective-permute-start.6 = (bf16[256,1024]{1,0:T(8,128)(2,1)S(1)}, bf16[256,1024]{1,0:T(8,128)(2,1)S(1)}, u32[]{:S(2)}, u32[]{:S(2)}) collective-permute-start(bf16[256,1024]{1,0:T(8,128)(2,1)S(1)} %slice.32), channel_id=1, source_target_pairs={{0,1},{1,2},{2,3},{3,0},{4,5},{5,6},{6,7},{7,4},{8,9},{9,10},{10,1... | collective-permute-start | bytes 1572872 | tf_op jit(solution)/shard_map/ppermute | solution.py:244
  69.0 12.5 %collective-permute-start.5 = (bf16[256,1024]{1,0:T(8,128)(2,1)S(1)}, bf16[256,1024]{1,0:T(8,128)(2,1)S(1)}, u32[]{:S(2)}, u32[]{:S(2)}) collective-permute-start(bf16[256,1024]{1,0:T(8,128)(2,1)S(1)} %get-tuple-element.68), channel_id=1, source_target_pairs={{0,4},{1,5},{2,6},{3,7},{4,0},{5,1},{6,2},{7,3},{8,12},{9,13},{10,... | collective-permute-start | bytes 1572872 | tf_op jit(solution)/shard_map/ppermute | solution.py:244
  81.5 11.9 %collective-permute-start.12 = (bf16[256,1024]{1,0:T(8,128)(2,1)S(1)}, bf16[256,1024]{1,0:T(8,128)(2,1)S(1)}, u32[]{:S(2)}, u32[]{:S(2)}) collective-permute-start(bf16[256,1024]{1,0:T(8,128)(2,1)S(1)} %collective-permute-done.5.refs_5_), channel_id=1, source_target_pairs={{0,3},{1,0},{2,1},{3,2},{4,7},{5,4},{6,5},{7,6},{8,11},{9,8},{10,9... | collective-permute-start | bytes 1572872 | tf_op jit(solution)/shard_map/ppermute | solution.py:244
  87.5 12.3 %collective-permute-start.13 = (bf16[256,1024]{1,0:T(8,128)(2,1)S(1)}, bf16[256,1024]{1,0:T(8,128)(2,1)}, u32[]{:S(2)}, u32[]{:S(2)}) collective-permute-start(bf16[256,1024]{1,0:T(8,128)(2,1)S(1)} %get-tuple-element.83), channel_id=1, source_target_pairs={{0,16},{8,24},{16,32},{24,40},{32,48},{40,56},{48,0},{56,8},{64,80... | collective-permute-start | bytes 1572872 | tf_op jit(solution)/shard_map/ppermute | solution.py:235
  103.0 19.7 %collective-permute-start.23 = (bf16[512,1024]{1,0:T(8,128)(2,1)S(1)}, bf16[512,1024]{1,0:T(8,128)(2,1)S(1)}, u32[]{:S(2)}, u32[]{:S(2)}) collective-permute-start(bf16[512,1024]{1,0:T(8,128)(2,1)S(1)} %unpack.1.refs_0_.refs_13_.refs_8_.refs_9_.refs_34_), channel_id=1, source_target_pairs={{0,8},{8,0},{16,24},{24,16},{32,40},{40,32},{48,56},{56,48},{64,72... | collective-permute-start | bytes 3145736 | tf_op jit(solution)/shard_map/ppermute | solution.py:235
  103.0 19.7 %collective-permute-start.24 = (bf16[512,1024]{1,0:T(8,128)(2,1)S(1)}, bf16[512,1024]{1,0:T(8,128)(2,1)S(1)}, u32[]{:S(2)}, u32[]{:S(2)}) collective-permute-start(bf16[512,1024]{1,0:T(8,128)(2,1)S(1)} %collective-permute-done.3.refs_15_.refs_10_.refs_11_), channel_id=1, source_target_pairs={{0,8},{8,0},{16,24},{24,16},{32,40},{40,32},{48,56},{56,48},{64,72... | collective-permute-start | bytes 3145736 | tf_op jit(solution)/shard_map/ppermute | solution.py:235
  103.5 14.8 %collective-permute-start.19 = (bf16[256,1024]{1,0:T(8,128)(2,1)S(1)}, bf16[256,1024]{1,0:T(8,128)(2,1)S(1)}, u32[]{:S(2)}, u32[]{:S(2)}) collective-permute-start(bf16[256,1024]{1,0:T(8,128)(2,1)S(1)} %collective-permute-done.10.refs_9_), channel_id=1, source_target_pairs={{0,3},{1,0},{2,1},{3,2},{4,7},{5,4},{6,5},{7,6},{8,11},{9,8},{10,9... | collective-permute-start | bytes 1572872 | tf_op jit(solution)/shard_map/ppermute | solution.py:244
  110.2 15.7 %collective-permute-start.25 = (bf16[512,1024]{1,0:T(8,128)(2,1)S(1)}, bf16[512,1024]{1,0:T(8,128)(2,1)S(1)}, u32[]{:S(2)}, u32[]{:S(2)}) collective-permute-start(bf16[512,1024]{1,0:T(8,128)(2,1)S(1)} %collective-permute-done.4.refs_17_.refs_12_.refs_13_), channel_id=1, source_target_pairs={{0,8},{8,0},{16,24},{24,16},{32,40},{40,32},{48,56},{56,48},{64,72... | collective-permute-start | bytes 3145736 | tf_op jit(solution)/shard_map/ppermute | solution.py:235
  118.3 15.0 %collective-permute-start.15 = (bf16[256,1024]{1,0:T(8,128)(2,1)S(1)}, bf16[256,1024]{1,0:T(8,128)(2,1)S(1)}, u32[]{:S(2)}, u32[]{:S(2)}) collective-permute-start(bf16[256,1024]{1,0:T(8,128)(2,1)S(1)} %collective-permute-done.11.refs_6_), channel_id=1, source_target_pairs={{0,1},{1,2},{2,3},{3,0},{4,5},{5,6},{6,7},{7,4},{8,9},{9,10},{10,1... | collective-permute-start | bytes 1572872 | tf_op jit(solution)/shard_map/ppermute | solution.py:244
  122.7 13.7 %collective-permute-start.20 = (bf16[256,1024]{1,0:T(8,128)(2,1)}, bf16[256,1024]{1,0:T(8,128)(2,1)}, u32[]{:S(2)}, u32[]{:S(2)}) collective-permute-start(bf16[256,1024]{1,0:T(8,128)(2,1)} %collective-permute-done.13.refs_25_.refs_20_.refs_21_), channel_id=1, source_target_pairs={{0,16},{8,24},{16,32},{24,40},{32,48},{40,56},{48,0},{56,8},{64,80... | collective-permute-start | bytes 1572872 | tf_op jit(solution)/shard_map/ppermute | solution.py:235
  122.7 13.7 %collective-permute-start.21 = (bf16[256,1024]{1,0:T(8,128)(2,1)}, bf16[256,1024]{1,0:T(8,128)(2,1)}, u32[]{:S(2)}, u32[]{:S(2)}) collective-permute-start(bf16[256,1024]{1,0:T(8,128)(2,1)} %collective-permute-done.14.refs_30_.refs_25_.refs_26_), channel_id=1, source_target_pairs={{0,48},{8,56},{16,0},{24,8},{32,16},{40,24},{48,32},{56,40},{64,11... | collective-permute-start | bytes 1572872 | tf_op jit(solution)/shard_map/ppermute | solution.py:235
  160.1 15.1 %collective-permute-start.39 = (bf16[256,1024]{1,0:T(8,128)(2,1)}, bf16[256,1024]{1,0:T(8,128)(2,1)S(1)}, u32[]{:S(2)}, u32[]{:S(2)}) collective-permute-start(bf16[256,1024]{1,0:T(8,128)(2,1)} %get-tuple-element.112.refs_0_), channel_id=1, source_target_pairs={{0,4},{1,5},{2,6},{3,7},{4,0},{5,1},{6,2},{7,3},{8,12},{9,13},{10,... | collective-permute-start | bytes 1572872 | tf_op jit(solution)/shard_map/ppermute | solution.py:244
  160.5 15.0 %collective-permute-start.36 = (bf16[256,1024]{1,0:T(8,128)(2,1)}, bf16[256,1024]{1,0:T(8,128)(2,1)S(1)}, u32[]{:S(2)}, u32[]{:S(2)}) collective-permute-start(bf16[256,1024]{1,0:T(8,128)(2,1)} %get-tuple-element.112.refs_0_), channel_id=1, source_target_pairs={{0,3},{1,0},{2,1},{3,2},{4,7},{5,4},{6,5},{7,6},{8,11},{9,8},{10,9... | collective-permute-start | bytes 1572872 | tf_op jit(solution)/shard_map/ppermute | solution.py:244
  162.2 15.1 %collective-permute-start.35 = (bf16[256,1024]{1,0:T(8,128)(2,1)}, bf16[256,1024]{1,0:T(8,128)(2,1)S(1)}, u32[]{:S(2)}, u32[]{:S(2)}) collective-permute-start(bf16[256,1024]{1,0:T(8,128)(2,1)} %get-tuple-element.112.refs_0_), channel_id=1, source_target_pairs={{0,1},{1,2},{2,3},{3,0},{4,5},{5,6},{6,7},{7,4},{8,9},{9,10},{10,1... | collective-permute-start | bytes 1572872 | tf_op jit(solution)/shard_map/ppermute | solution.py:244
  162.6 23.1 %collective-permute-start.40 = (bf16[256,1024]{1,0:T(8,128)(2,1)}, bf16[256,1024]{1,0:T(8,128)(2,1)}, u32[]{:S(2)}, u32[]{:S(2)}) collective-permute-start(bf16[256,1024]{1,0:T(8,128)(2,1)} %get-tuple-element.113.refs_4_), channel_id=1, source_target_pairs={{0,4},{1,5},{2,6},{3,7},{4,0},{5,1},{6,2},{7,3},{8,12},{9,13},{10,... | collective-permute-start | bytes 1572872 | tf_op jit(solution)/shard_map/ppermute | solution.py:244
  164.2 21.5 %collective-permute-start.38 = (bf16[256,1024]{1,0:T(8,128)(2,1)}, bf16[256,1024]{1,0:T(8,128)(2,1)S(1)}, u32[]{:S(2)}, u32[]{:S(2)}) collective-permute-start(bf16[256,1024]{1,0:T(8,128)(2,1)} %get-tuple-element.113.refs_4_), channel_id=1, source_target_pairs={{0,3},{1,0},{2,1},{3,2},{4,7},{5,4},{6,5},{7,6},{8,11},{9,8},{10,9... | collective-permute-start | bytes 1572872 | tf_op jit(solution)/shard_map/ppermute | solution.py:244
  175.1 13.7 %collective-permute-start.37 = (bf16[256,1024]{1,0:T(8,128)(2,1)}, bf16[256,1024]{1,0:T(8,128)(2,1)S(1)}, u32[]{:S(2)}, u32[]{:S(2)}) collective-permute-start(bf16[256,1024]{1,0:T(8,128)(2,1)} %get-tuple-element.113.refs_4_), channel_id=1, source_target_pairs={{0,1},{1,2},{2,3},{3,0},{4,5},{5,6},{6,7},{7,4},{8,9},{9,10},{10,1... | collective-permute-start | bytes 1572872 | tf_op jit(solution)/shard_map/ppermute | solution.py:244
  189.7 13.4 %collective-permute-start.41 = (bf16[256,1024]{1,0:T(8,128)(2,1)S(1)}, bf16[256,1024]{1,0:T(8,128)(2,1)}, u32[]{:S(2)}, u32[]{:S(2)}) collective-permute-start(bf16[256,1024]{1,0:T(8,128)(2,1)S(1)} %collective-permute-done.35.refs_1_), channel_id=1, source_target_pairs={{0,1},{1,2},{2,3},{3,0},{4,5},{5,6},{6,7},{7,4},{8,9},{9,10},{10,1... | collective-permute-start | bytes 1572872 | tf_op jit(solution)/shard_map/ppermute | solution.py:244
  190.9 26.2 %collective-permute-start.45 = (bf16[256,1024]{1,0:T(8,128)(2,1)S(1)}, bf16[256,1024]{1,0:T(8,128)(2,1)}, u32[]{:S(2)}, u32[]{:S(2)}) collective-permute-start(bf16[256,1024]{1,0:T(8,128)(2,1)S(1)} %collective-permute-done.35.refs_1_), channel_id=1, source_target_pairs={{0,4},{1,5},{2,6},{3,7},{4,0},{5,1},{6,2},{7,3},{8,12},{9,13},{10,... | collective-permute-start | bytes 1572872 | tf_op jit(solution)/shard_map/ppermute | solution.py:244
  192.3 24.8 %collective-permute-start.46 = (bf16[256,1024]{1,0:T(8,128)(2,1)S(1)}, bf16[256,1024]{1,0:T(8,128)(2,1)}, u32[]{:S(2)}, u32[]{:S(2)}) collective-permute-start(bf16[256,1024]{1,0:T(8,128)(2,1)S(1)} %collective-permute-done.36.refs_2_), channel_id=1, source_target_pairs={{0,4},{1,5},{2,6},{3,7},{4,0},{5,1},{6,2},{7,3},{8,12},{9,13},{10,... | collective-permute-start | bytes 1572872 | tf_op jit(solution)/shard_map/ppermute | solution.py:244
  203.1 14.0 %collective-permute-start.44 = (bf16[256,1024]{1,0:T(8,128)(2,1)}, bf16[256,1024]{1,0:T(8,128)(2,1)S(1)}, u32[]{:S(2)}, u32[]{:S(2)}) collective-permute-start(bf16[256,1024]{1,0:T(8,128)(2,1)} %collective-permute-done.40.refs_4_), channel_id=1, source_target_pairs={{0,3},{1,0},{2,1},{3,2},{4,7},{5,4},{6,5},{7,6},{8,11},{9,8},{10,9... | collective-permute-start | bytes 1572872 | tf_op jit(solution)/shard_map/ppermute | solution.py:244
  204.1 13.0 %collective-permute-start.43 = (bf16[256,1024]{1,0:T(8,128)(2,1)}, bf16[256,1024]{1,0:T(8,128)(2,1)S(1)}, u32[]{:S(2)}, u32[]{:S(2)}) collective-permute-start(bf16[256,1024]{1,0:T(8,128)(2,1)} %collective-permute-done.40.refs_4_), channel_id=1, source_target_pairs={{0,1},{1,2},{2,3},{3,0},{4,5},{5,6},{6,7},{7,4},{8,9},{9,10},{10,1... | collective-permute-start | bytes 1572872 | tf_op jit(solution)/shard_map/ppermute | solution.py:244
  205.1 24.6 %collective-permute-start.47 = (bf16[256,1024]{1,0:T(8,128)(2,1)}, bf16[256,1024]{1,0:T(8,128)(2,1)}, u32[]{:S(2)}, u32[]{:S(2)}) collective-permute-start(bf16[256,1024]{1,0:T(8,128)(2,1)} %collective-permute-done.41.refs_3_), channel_id=1, source_target_pairs={{0,4},{1,5},{2,6},{3,7},{4,0},{5,1},{6,2},{7,3},{8,12},{9,13},{10,... | collective-permute-start | bytes 1572872 | tf_op jit(solution)/shard_map/ppermute | solution.py:244
  217.2 12.6 %collective-permute-start.49 = (bf16[128,1024]{1,0:T(8,128)(2,1)S(1)}, bf16[128,1024]{1,0:T(8,128)(2,1)S(1)}, u32[]{:S(2)}, u32[]{:S(2)}) collective-permute-start(bf16[128,1024]{1,0:T(8,128)(2,1)S(1)} %slice.39), channel_id=1, source_target_pairs={{0,3},{1,0},{2,1},{3,2},{4,7},{5,4},{6,5},{7,6},{8,11},{9,8},{10,9... | collective-permute-start | bytes 786440 | tf_op jit(solution)/shard_map/ppermute | solution.py:244
  (58 other events, 1048.7 us)
where the time goes:
time: 243 us
  waiting for transfers between devices  118 us (49%)
  starting transfers between devices  47.6 us (20%)
  Pallas kernels  41 us (17%)
  blocking collectives  26.4 us (11%)
  local copies, waits for them, and re-layouts  8.66 us (4%)
    ppermute x27, waiting for transfers between devices, over_col(): return lax.ppermute(value, 'col', pairs)  71.7 us
    ppermute x23, waiting for transfers between devices, over_row(): return lax.ppermute(value, 'row', pairs)  46 us
    pallas_call x3, Pallas kernels, product(): pl.pallas_call(functools.partial(product_kernel, factor, left_parts, righ...  38.2 us
    ppermute x27, starting transfers between devices, over_col(): return lax.ppermute(value, 'col', pairs)  30.2 us
    all_to_all x1, blocking collectives, local_tile(): received = lax.all_to_all(send, 'row', 0, 0, tiled=True)  26.4 us
    ppermute x23, starting transfers between devices, over_row(): return lax.ppermute(value, 'row', pairs)  17.4 us
    unnamed x80, local copies, waits for them, and re-layouts  5.88 us
  transfers between devices with their start and end apart: 50, of which 28 were waited for; matrix products, arithmetic and copies ran while one was open for 1% of the time, Pallas kernels for 4%

commit v1 on v0

--- a/solution.py
+++ b/solution.py
@@ -368,12 +368,11 @@
     h1_far, h2_far, h2_z = after((h1_far, h2_far, h2_z))
     h2_z_near = near(h2_z, x_shift)
     h1_z_far = z_swap(h1_far)
-    h2_z_near, h1_z_near = after((h2_z_near, h1_z_near))
+    lefts = both(0, (h1, h1_near, [h1_far]), (h2, h2_near, [h2_far]))
+    (total,) = product(lefts, chunks, core, [rows], 1.0, jnp.float32, "step_first", z_lo)
+    h2_z_near, h1_z_near, total = after((h2_z_near, h1_z_near, total))
     h2_z_far = far(*h2_z_near, x_shift)
-    h1_far, h2_far, h1_z_far = [h1_far], [h2_far], [h1_z_far]
-
-    lefts = both(0, (h1, h1_near, h1_far), (h2, h2_near, h2_far))
-    (total,) = product(lefts, chunks, core, [rows], 1.0, jnp.float32, "step_first", z_lo)
+    h1_z_far = [h1_z_far]
     late = (h1_z, h1_z_near, h1_z_far, h2_z, h2_z_near, h2_z_far)
     h1_z, h1_z_near, h1_z_far, h2_z, h2_z_near, h2_z_far = after(late, total)
     lefts = both(1, (h1_z, h1_z_near, h1_z_far), (h2_z, h2_z_near, h2_z_far))

time: 243 us -> 241 us (level)
  waiting for transfers between devices: 118 us -> 115 us
    ppermute x27, waiting for transfers between devices: 71.7 us -> 68.9 us  [over_col(): return lax.ppermute(value, 'col', pairs)]
  transfers between devices with their start and end apart: 50 -> 50, of which waited for: 28 -> 30; matrix products, arithmetic and copies ran while one was open for 1% -> 1% of each run, Pallas kernels for 4% -> 4%
where the time goes in v1:
time: 241 us
  waiting for transfers between devices  115 us (48%)
  starting transfers between devices  47.8 us (20%)
  Pallas kernels  40.8 us (17%)
  blocking collectives  26.5 us (11%)
  local copies, waits for them, and re-layouts  9.44 us (4%)
    ppermute x27, waiting for transfers between devices, over_col(): return lax.ppermute(value, 'col', pairs)  68.9 us
    ppermute x23, waiting for transfers between devices, over_row(): return lax.ppermute(value, 'row', pairs)  46.1 us
    pallas_call x3, Pallas kernels, product(): pl.pallas_call(functools.partial(product_kernel, factor, left_parts, righ...  38.1 us
    ppermute x27, starting transfers between devices, over_col(): return lax.ppermute(value, 'col', pairs)  30.4 us
    all_to_all x1, blocking collectives, local_tile(): received = lax.all_to_all(send, 'row', 0, 0, tiled=True)  26.5 us
    ppermute x23, starting transfers between devices, over_row(): return lax.ppermute(value, 'row', pairs)  17.4 us
    unnamed x80, local copies, waits for them, and re-layouts  6.62 us
  transfers between devices with their start and end apart: 50, of which 30 were waited for; matrix products, arithmetic and copies ran while one was open for 1% of the time, Pallas kernels for 4%

profile of v1, /device:TPU:0, one launch (start us, length us, event | category | flops | bytes accessed | tf_op | source)
XLA Modules:
  0.0 240.7 jit_solution(13316647329414647668)
XLA Ops:
  4.6 26.5 %all_to_all.5.received = bf16[16,272,128]{2,1,0:T(8,128)(2,1)S(1)} all-to-all(bf16[16,272,128]{2,1,0:T(8,128)(2,1)S(1)} %pack.1), channel_id=1, replica_groups=mesh['row'=16,'col'=8] {'row'}, dimensions={0} | all-to-all | bytes 2228224 | tf_op jit(solution)/shard_map/all_to_all | solution.py:83
  34.6 2.9 %collective-permute-start.2 = (bf16[512,1024]{1,0:T(8,128)(2,1)S(1)}, bf16[512,1024]{1,0:T(8,128)(2,1)S(1)}, u32[]{:S(2)}, u32[]{:S(2)}) collective-permute-start(bf16[512,1024]{1,0:T(8,128)(2,1)S(1)} %unpack.1.refs_0_.refs_13_.refs_8_.refs_9_.refs_34_), channel_id=1, source_target_pairs={{0,3},{1,0},{2,1},{3,2},{4,7},{5,4},{6,5},{7,6},{8,11},{9,8},{10,9... | collective-permute-start | bytes 3145736 | tf_op jit(solution)/shard_map/ppermute | solution.py:244
  38.2 19.5 %collective-permute-done.4.refs_17_.refs_12_.refs_13_ = bf16[512,1024]{1,0:T(8,128)(2,1)S(1)} collective-permute-done((bf16[512,1024]{1,0:T(8,128)(2,1)S(1)}, bf16[512,1024]{1,0:T(8,128)(2,1)S(1)}, u32[]{:S(2)}, u32[]{:S(2)}) %collective-permute-start.4) | collective-permute-done | bytes 1048608 | tf_op jit(solution)/shard_map/ppermute | solution.py:235
  57.7 2.2 collective-permute-done.3.refs_15_.refs_10_.refs_11_
  59.9 3.1 %collective-permute-done.1.refs_1_ = bf16[512,1024]{1,0:T(8,128)(2,1)S(1)} collective-permute-done((bf16[512,1024]{1,0:T(8,128)(2,1)S(1)}, bf16[512,1024]{1,0:T(8,128)(2,1)S(1)}, u32[]{:S(2)}, u32[]{:S(2)}) %collective-permute-start.1) | collective-permute-done | bytes 1048608 | tf_op jit(solution)/shard_map/ppermute | solution.py:244
  64.0 2.4 %collective-permute-start.9 = (bf16[256,1024]{1,0:T(8,128)(2,1)S(1)}, bf16[256,1024]{1,0:T(8,128)(2,1)S(1)}, u32[]{:S(2)}, u32[]{:S(2)}) collective-permute-start(bf16[256,1024]{1,0:T(8,128)(2,1)S(1)} %slice.35), channel_id=1, source_target_pairs={{0,48},{8,56},{16,0},{24,8},{32,16},{40,24},{48,32},{56,40},{64,11... | collective-permute-start | bytes 1572872 | tf_op jit(solution)/shard_map/ppermute | solution.py:235
  66.5 2.5 %collective-permute-start.7 = (bf16[256,1024]{1,0:T(8,128)(2,1)S(1)}, bf16[256,1024]{1,0:T(8,128)(2,1)S(1)}, u32[]{:S(2)}, u32[]{:S(2)}) collective-permute-start(bf16[256,1024]{1,0:T(8,128)(2,1)S(1)} %slice.33), channel_id=1, source_target_pairs={{0,3},{1,0},{2,1},{3,2},{4,7},{5,4},{6,5},{7,6},{8,11},{9,8},{10,9... | collective-permute-start | bytes 1572872 | tf_op jit(solution)/shard_map/ppermute | solution.py:244
  69.7 6.5 %collective-permute-done.9.refs_20_.refs_15_.refs_16_ = bf16[256,1024]{1,0:T(8,128)(2,1)S(1)} collective-permute-done((bf16[256,1024]{1,0:T(8,128)(2,1)S(1)}, bf16[256,1024]{1,0:T(8,128)(2,1)S(1)}, u32[]{:S(2)}, u32[]{:S(2)}) %collective-permute-start.9) | collective-permute-done | bytes 524320 | tf_op jit(solution)/shard_map/ppermute | solution.py:235
  76.3 3.4 %collective-permute-done.8.refs_19_.refs_14_.refs_15_ = bf16[256,1024]{1,0:T(8,128)(2,1)S(1)} collective-permute-done((bf16[256,1024]{1,0:T(8,128)(2,1)S(1)}, bf16[256,1024]{1,0:T(8,128)(2,1)S(1)}, u32[]{:S(2)}, u32[]{:S(2)}) %collective-permute-start.8) | collective-permute-done | bytes 524320 | tf_op jit(solution)/shard_map/ppermute | solution.py:235
  84.4 3.0 %collective-permute-start.14 = (bf16[256,1024]{1,0:T(8,128)(2,1)S(1)}, bf16[256,1024]{1,0:T(8,128)(2,1)}, u32[]{:S(2)}, u32[]{:S(2)}) collective-permute-start(bf16[256,1024]{1,0:T(8,128)(2,1)S(1)} %get-tuple-element.83), channel_id=1, source_target_pairs={{0,48},{8,56},{16,0},{24,8},{32,16},{40,24},{48,32},{56,40},{64,11... | collective-permute-start | bytes 1572872 | tf_op jit(solution)/shard_map/ppermute | solution.py:235
  87.5 6.1 %collective-permute-done.10.refs_9_ = bf16[256,1024]{1,0:T(8,128)(2,1)S(1)} collective-permute-done((bf16[256,1024]{1,0:T(8,128)(2,1)S(1)}, bf16[256,1024]{1,0:T(8,128)(2,1)S(1)}, u32[]{:S(2)}, u32[]{:S(2)}) %collective-permute-start.10) | collective-permute-done | bytes 524320 | tf_op jit(solution)/shard_map/ppermute | solution.py:244
  94.4 5.3 %collective-permute-done.13.refs_25_.refs_20_.refs_21_ = bf16[256,1024]{1,0:T(8,128)(2,1)} collective-permute-done((bf16[256,1024]{1,0:T(8,128)(2,1)S(1)}, bf16[256,1024]{1,0:T(8,128)(2,1)}, u32[]{:S(2)}, u32[]{:S(2)}) %collective-permute-start.13) | collective-permute-done | bytes 524320 | tf_op jit(solution)/shard_map/ppermute | solution.py:235
  99.8 3.2 %collective-permute-start.17 = (bf16[256,1024]{1,0:T(8,128)(2,1)S(1)}, bf16[256,1024]{1,0:T(8,128)(2,1)S(1)}, u32[]{:S(2)}, u32[]{:S(2)}) collective-permute-start(bf16[256,1024]{1,0:T(8,128)(2,1)S(1)} %get-tuple-element.84), channel_id=1, source_target_pairs={{0,48},{8,56},{16,0},{24,8},{32,16},{40,24},{48,32},{56,40},{64,11... | collective-permute-start | bytes 1572872 | tf_op jit(solution)/shard_map/ppermute | solution.py:235
  103.5 3.2 %collective-permute-start.19 = (bf16[256,1024]{1,0:T(8,128)(2,1)S(1)}, bf16[256,1024]{1,0:T(8,128)(2,1)S(1)}, u32[]{:S(2)}, u32[]{:S(2)}) collective-permute-start(bf16[256,1024]{1,0:T(8,128)(2,1)S(1)} %collective-permute-done.10.refs_9_), channel_id=1, source_target_pairs={{0,3},{1,0},{2,1},{3,2},{4,7},{5,4},{6,5},{7,6},{8,11},{9,8},{10,9... | collective-permute-start | bytes 1572872 | tf_op jit(solution)/shard_map/ppermute | solution.py:244
  106.7 3.5 %collective-permute-done.16.refs_26_.refs_21_.refs_22_ = bf16[256,1024]{1,0:T(8,128)(2,1)S(1)} collective-permute-done((bf16[256,1024]{1,0:T(8,128)(2,1)S(1)}, bf16[256,1024]{1,0:T(8,128)(2,1)S(1)}, u32[]{:S(2)}, u32[]{:S(2)}) %collective-permute-start.16) | collective-permute-done | bytes 524320 | tf_op jit(solution)/shard_map/ppermute | solution.py:235
  110.3 7.8 %collective-permute-done.19.refs_11_ = bf16[256,1024]{1,0:T(8,128)(2,1)S(1)} collective-permute-done((bf16[256,1024]{1,0:T(8,128)(2,1)S(1)}, bf16[256,1024]{1,0:T(8,128)(2,1)S(1)}, u32[]{:S(2)}, u32[]{:S(2)}) %collective-permute-start.19) | collective-permute-done | bytes 524320 | tf_op jit(solution)/shard_map/ppermute | solution.py:244
  118.1 3.4 %collective-permute-done.18.refs_10_ = bf16[256,1024]{1,0:T(8,128)(2,1)S(1)} collective-permute-done((bf16[256,1024]{1,0:T(8,128)(2,1)S(1)}, bf16[256,1024]{1,0:T(8,128)(2,1)S(1)}, u32[]{:S(2)}, u32[]{:S(2)}) %collective-permute-start.18) | collective-permute-done | bytes 524320 | tf_op jit(solution)/shard_map/ppermute | solution.py:244
  122.5 3.2 %collective-permute-start.21 = (bf16[256,1024]{1,0:T(8,128)(2,1)}, bf16[256,1024]{1,0:T(8,128)(2,1)}, u32[]{:S(2)}, u32[]{:S(2)}) collective-permute-start(bf16[256,1024]{1,0:T(8,128)(2,1)} %collective-permute-done.14.refs_30_.refs_25_.refs_26_), channel_id=1, source_target_pairs={{0,48},{8,56},{16,0},{24,8},{32,16},{40,24},{48,32},{56,40},{64,11... | collective-permute-start | bytes 1572872 | tf_op jit(solution)/shard_map/ppermute | solution.py:235
  125.8 7.4 %collective-permute-done.15.refs_8_ = bf16[256,1024]{1,0:T(8,128)(2,1)S(1)} collective-permute-done((bf16[256,1024]{1,0:T(8,128)(2,1)S(1)}, bf16[256,1024]{1,0:T(8,128)(2,1)S(1)}, u32[]{:S(2)}, u32[]{:S(2)}) %collective-permute-start.15) | collective-permute-done | bytes 524320 | tf_op jit(solution)/shard_map/ppermute | solution.py:244
  133.7 2.6 %collective-permute-done.20.refs_33_.refs_28_.refs_29_ = bf16[256,1024]{1,0:T(8,128)(2,1)} collective-permute-done((bf16[256,1024]{1,0:T(8,128)(2,1)}, bf16[256,1024]{1,0:T(8,128)(2,1)}, u32[]{:S(2)}, u32[]{:S(2)}) %collective-permute-start.20) | collective-permute-done | bytes 524320 | tf_op jit(solution)/shard_map/ppermute | solution.py:235
  144.0 15.9 %square.1 = (bf16[256,1024]{1,0:T(8,128)(2,1)}, bf16[256,1024]{1,0:T(8,128)(2,1)}) custom-call(s32[13]{0:T(128)} %stack.58.left_at, s32[8]{0:T(128)} %stack.53.right_at, s32[1]{0:T(128)} %bitcast.12.core, s32[1]{0:T(128)} %constant.244.clone.1.want, bf16[512,1024]{1,0:T(8,128)(2,1)} %copy-done, bf16[512,1024]{1,0:T(8,128)(2,1)} %copy-done.28, ...), custom_call_target="tpu_custom_call" | custom-call | flops 8589934592 | bytes 25165824 | tf_op jit(solution)/shard_map/square/pallas_call | solution.py:197
  164.0 3.2 %collective-permute-start.38 = (bf16[256,1024]{1,0:T(8,128)(2,1)}, bf16[256,1024]{1,0:T(8,128)(2,1)S(1)}, u32[]{:S(2)}, u32[]{:S(2)}) collective-permute-start(bf16[256,1024]{1,0:T(8,128)(2,1)} %get-tuple-element.110.refs_4_), channel_id=1, source_target_pairs={{0,3},{1,0},{2,1},{3,2},{4,7},{5,4},{6,5},{7,6},{8,11},{9,8},{10,9... | collective-permute-start | bytes 1572872 | tf_op jit(solution)/shard_map/ppermute | solution.py:244
  167.2 7.8 %collective-permute-done.39.refs_0_ = bf16[256,1024]{1,0:T(8,128)(2,1)} collective-permute-done((bf16[256,1024]{1,0:T(8,128)(2,1)}, bf16[256,1024]{1,0:T(8,128)(2,1)}, u32[]{:S(2)}, u32[]{:S(2)}) %collective-permute-start.39) | collective-permute-done | bytes 524320 | tf_op jit(solution)/shard_map/ppermute | solution.py:244
  177.1 8.3 %collective-permute-done.40.refs_4_ = bf16[256,1024]{1,0:T(8,128)(2,1)} collective-permute-done((bf16[256,1024]{1,0:T(8,128)(2,1)}, bf16[256,1024]{1,0:T(8,128)(2,1)}, u32[]{:S(2)}, u32[]{:S(2)}) %collective-permute-start.40) | collective-permute-done | bytes 524320 | tf_op jit(solution)/shard_map/ppermute | solution.py:244
  185.8 3.0 %collective-permute-done.37.refs_5_ = bf16[256,1024]{1,0:T(8,128)(2,1)S(1)} collective-permute-done((bf16[256,1024]{1,0:T(8,128)(2,1)}, bf16[256,1024]{1,0:T(8,128)(2,1)S(1)}, u32[]{:S(2)}, u32[]{:S(2)}) %collective-permute-start.37) | collective-permute-done | bytes 524320 | tf_op jit(solution)/shard_map/ppermute | solution.py:244
  193.6 7.4 %collective-permute-done.42.refs_7_ = bf16[256,1024]{1,0:T(8,128)(2,1)S(1)} collective-permute-done((bf16[256,1024]{1,0:T(8,128)(2,1)S(1)}, bf16[256,1024]{1,0:T(8,128)(2,1)S(1)}, u32[]{:S(2)}, u32[]{:S(2)}) %collective-permute-start.42) | collective-permute-done | bytes 524320 | tf_op jit(solution)/shard_map/ppermute | solution.py:244
  201.0 2.3 collective-permute-done.41.refs_3_
  207.5 10.4 %step_first.1.refs_33_ = f32[512,1024]{1,0:T(8,128)} custom-call(s32[8]{0:T(128)} %stack.59.left_at, s32[8]{0:T(128)} %stack.53.right_at, s32[1]{0:T(128)} %bitcast.12.core, s32[1]{0:T(128)} %bitcast.20.want, bf16[256,1024]{1,0:T(8,128)(2,1)} %get-tuple-element.108.refs_0_, bf16[256,1024]{1,0:T(8,128)(2,1)} %copy-done.22, bf16[256,1024]{1,0:T(8,128)(2,1)} %copy-done.21, ...), custom_call_target="tpu_custom_call" | custom-call | flops 4294967296 | bytes 12582912 | tf_op jit(solution)/shard_map/step_first/pallas_call | solution.py:197
  218.0 2.4 collective-permute-start.49
  221.1 3.9 %collective-permute-done.47.refs_3_ = bf16[256,1024]{1,0:T(8,128)(2,1)} collective-permute-done((bf16[256,1024]{1,0:T(8,128)(2,1)S(1)}, bf16[256,1024]{1,0:T(8,128)(2,1)}, u32[]{:S(2)}, u32[]{:S(2)}) %collective-permute-start.47) | collective-permute-done | bytes 524320 | tf_op jit(solution)/shard_map/ppermute | solution.py:244
  225.0 3.0 %collective-permute-done.48.refs_7_ = bf16[128,1024]{1,0:T(8,128)(2,1)S(1)} collective-permute-done((bf16[128,1024]{1,0:T(8,128)(2,1)S(1)}, bf16[128,1024]{1,0:T(8,128)(2,1)S(1)}, u32[]{:S(2)}, u32[]{:S(2)}) %collective-permute-start.48) | collective-permute-done | bytes 262176 | tf_op jit(solution)/shard_map/ppermute | solution.py:244
  228.7 11.8 %step_last.1 = f32[512,1024]{1,0:T(8,128)} custom-call(s32[9]{0:T(128)} %stack.44.left_at, s32[8]{0:T(128)} %stack.53.right_at, s32[1]{0:T(128)} %bitcast.12.core, s32[1]{0:T(128)} %bitcast.13.want, bf16[256,1024]{1,0:T(8,128)(2,1)} %collective-permute-done.39.refs_0_, bf16[256,1024]{1,0:T(8,128)(2,1)} %collective-permute-done.45.refs_1_, ...), custom_call_target="tpu_custom_call" | custom-call | flops 4294967296 | bytes 12582912 | tf_op jit(solution)/shard_map/step_last/pallas_call | solution.py:197
  (166 shorter events, 42.3 us)
Async XLA Ops:
  32.5 25.2 %collective-permute-start.4 = (bf16[512,1024]{1,0:T(8,128)(2,1)S(1)}, bf16[512,1024]{1,0:T(8,128)(2,1)S(1)}, u32[]{:S(2)}, u32[]{:S(2)}) collective-permute-start(bf16[512,1024]{1,0:T(8,128)(2,1)S(1)} %unpack.1.refs_0_.refs_13_.refs_8_.refs_9_.refs_34_), channel_id=1, source_target_pairs={{0,48},{8,56},{16,0},{24,8},{32,16},{40,24},{48,32},{56,40},{64,11... | collective-permute-start | bytes 3145736 | tf_op jit(solution)/shard_map/ppermute | solution.py:235
  33.8 26.1 %collective-permute-start.3 = (bf16[512,1024]{1,0:T(8,128)(2,1)S(1)}, bf16[512,1024]{1,0:T(8,128)(2,1)S(1)}, u32[]{:S(2)}, u32[]{:S(2)}) collective-permute-start(bf16[512,1024]{1,0:T(8,128)(2,1)S(1)} %unpack.1.refs_0_.refs_13_.refs_8_.refs_9_.refs_34_), channel_id=1, source_target_pairs={{0,16},{8,24},{16,32},{24,40},{32,48},{40,56},{48,0},{56,8},{64,80... | collective-permute-start | bytes 3145736 | tf_op jit(solution)/shard_map/ppermute | solution.py:235
  34.6 25.3 %collective-permute-start.2 = (bf16[512,1024]{1,0:T(8,128)(2,1)S(1)}, bf16[512,1024]{1,0:T(8,128)(2,1)S(1)}, u32[]{:S(2)}, u32[]{:S(2)}) collective-permute-start(bf16[512,1024]{1,0:T(8,128)(2,1)S(1)} %unpack.1.refs_0_.refs_13_.refs_8_.refs_9_.refs_34_), channel_id=1, source_target_pairs={{0,3},{1,0},{2,1},{3,2},{4,7},{5,4},{6,5},{7,6},{8,11},{9,8},{10,9... | collective-permute-start | bytes 3145736 | tf_op jit(solution)/shard_map/ppermute | solution.py:244
  37.5 25.6 %collective-permute-start.1 = (bf16[512,1024]{1,0:T(8,128)(2,1)S(1)}, bf16[512,1024]{1,0:T(8,128)(2,1)S(1)}, u32[]{:S(2)}, u32[]{:S(2)}) collective-permute-start(bf16[512,1024]{1,0:T(8,128)(2,1)S(1)} %unpack.1.refs_0_.refs_13_.refs_8_.refs_9_.refs_34_), channel_id=1, source_target_pairs={{0,1},{1,2},{2,3},{3,0},{4,5},{5,6},{6,7},{7,4},{8,9},{9,10},{10,1... | collective-permute-start | bytes 3145736 | tf_op jit(solution)/shard_map/ppermute | solution.py:244
  37.5 25.9 %collective-permute-start = (bf16[512,1024]{1,0:T(8,128)(2,1)S(1)}, bf16[512,1024]{1,0:T(8,128)(2,1)S(1)}, u32[]{:S(2)}, u32[]{:S(2)}) collective-permute-start(bf16[512,1024]{1,0:T(8,128)(2,1)S(1)} %unpack.1.refs_0_.refs_13_.refs_8_.refs_9_.refs_34_), channel_id=1, source_target_pairs={{0,64},{8,72},{16,80},{24,88},{32,96},{40,104},{48,112},{56,120},{... | collective-permute-start | bytes 3145736 | tf_op jit(solution)/shard_map/ppermute | solution.py:235
  64.0 12.2 %collective-permute-start.9 = (bf16[256,1024]{1,0:T(8,128)(2,1)S(1)}, bf16[256,1024]{1,0:T(8,128)(2,1)S(1)}, u32[]{:S(2)}, u32[]{:S(2)}) collective-permute-start(bf16[256,1024]{1,0:T(8,128)(2,1)S(1)} %slice.35), channel_id=1, source_target_pairs={{0,48},{8,56},{16,0},{24,8},{32,16},{40,24},{48,32},{56,40},{64,11... | collective-permute-start | bytes 1572872 | tf_op jit(solution)/shard_map/ppermute | solution.py:235
  66.5 13.1 %collective-permute-start.8 = (bf16[256,1024]{1,0:T(8,128)(2,1)S(1)}, bf16[256,1024]{1,0:T(8,128)(2,1)S(1)}, u32[]{:S(2)}, u32[]{:S(2)}) collective-permute-start(bf16[256,1024]{1,0:T(8,128)(2,1)S(1)} %slice.34), channel_id=1, source_target_pairs={{0,16},{8,24},{16,32},{24,40},{32,48},{40,56},{48,0},{56,8},{64,80... | collective-permute-start | bytes 1572872 | tf_op jit(solution)/shard_map/ppermute | solution.py:235
  66.5 13.1 %collective-permute-start.7 = (bf16[256,1024]{1,0:T(8,128)(2,1)S(1)}, bf16[256,1024]{1,0:T(8,128)(2,1)S(1)}, u32[]{:S(2)}, u32[]{:S(2)}) collective-permute-start(bf16[256,1024]{1,0:T(8,128)(2,1)S(1)} %slice.33), channel_id=1, source_target_pairs={{0,3},{1,0},{2,1},{3,2},{4,7},{5,4},{6,5},{7,6},{8,11},{9,8},{10,9... | collective-permute-start | bytes 1572872 | tf_op jit(solution)/shard_map/ppermute | solution.py:244
  69.0 12.6 %collective-permute-start.6 = (bf16[256,1024]{1,0:T(8,128)(2,1)S(1)}, bf16[256,1024]{1,0:T(8,128)(2,1)S(1)}, u32[]{:S(2)}, u32[]{:S(2)}) collective-permute-start(bf16[256,1024]{1,0:T(8,128)(2,1)S(1)} %slice.32), channel_id=1, source_target_pairs={{0,1},{1,2},{2,3},{3,0},{4,5},{5,6},{6,7},{7,4},{8,9},{9,10},{10,1... | collective-permute-start | bytes 1572872 | tf_op jit(solution)/shard_map/ppermute | solution.py:244
  69.0 12.6 %collective-permute-start.5 = (bf16[256,1024]{1,0:T(8,128)(2,1)S(1)}, bf16[256,1024]{1,0:T(8,128)(2,1)S(1)}, u32[]{:S(2)}, u32[]{:S(2)}) collective-permute-start(bf16[256,1024]{1,0:T(8,128)(2,1)S(1)} %get-tuple-element.69), channel_id=1, source_target_pairs={{0,4},{1,5},{2,6},{3,7},{4,0},{5,1},{6,2},{7,3},{8,12},{9,13},{10,... | collective-permute-start | bytes 1572872 | tf_op jit(solution)/shard_map/ppermute | solution.py:244
  81.6 12.0 %collective-permute-start.12 = (bf16[256,1024]{1,0:T(8,128)(2,1)S(1)}, bf16[256,1024]{1,0:T(8,128)(2,1)S(1)}, u32[]{:S(2)}, u32[]{:S(2)}) collective-permute-start(bf16[256,1024]{1,0:T(8,128)(2,1)S(1)} %collective-permute-done.5.refs_5_), channel_id=1, source_target_pairs={{0,3},{1,0},{2,1},{3,2},{4,7},{5,4},{6,5},{7,6},{8,11},{9,8},{10,9... | collective-permute-start | bytes 1572872 | tf_op jit(solution)/shard_map/ppermute | solution.py:244
  87.5 12.3 %collective-permute-start.13 = (bf16[256,1024]{1,0:T(8,128)(2,1)S(1)}, bf16[256,1024]{1,0:T(8,128)(2,1)}, u32[]{:S(2)}, u32[]{:S(2)}) collective-permute-start(bf16[256,1024]{1,0:T(8,128)(2,1)S(1)} %get-tuple-element.84), channel_id=1, source_target_pairs={{0,16},{8,24},{16,32},{24,40},{32,48},{40,56},{48,0},{56,8},{64,80... | collective-permute-start | bytes 1572872 | tf_op jit(solution)/shard_map/ppermute | solution.py:235
  103.0 19.5 %collective-permute-start.23 = (bf16[512,1024]{1,0:T(8,128)(2,1)S(1)}, bf16[512,1024]{1,0:T(8,128)(2,1)S(1)}, u32[]{:S(2)}, u32[]{:S(2)}) collective-permute-start(bf16[512,1024]{1,0:T(8,128)(2,1)S(1)} %unpack.1.refs_0_.refs_13_.refs_8_.refs_9_.refs_34_), channel_id=1, source_target_pairs={{0,8},{8,0},{16,24},{24,16},{32,40},{40,32},{48,56},{56,48},{64,72... | collective-permute-start | bytes 3145736 | tf_op jit(solution)/shard_map/ppermute | solution.py:235
  103.0 19.5 %collective-permute-start.24 = (bf16[512,1024]{1,0:T(8,128)(2,1)S(1)}, bf16[512,1024]{1,0:T(8,128)(2,1)S(1)}, u32[]{:S(2)}, u32[]{:S(2)}) collective-permute-start(bf16[512,1024]{1,0:T(8,128)(2,1)S(1)} %collective-permute-done.3.refs_15_.refs_10_.refs_11_), channel_id=1, source_target_pairs={{0,8},{8,0},{16,24},{24,16},{32,40},{40,32},{48,56},{56,48},{64,72... | collective-permute-start | bytes 3145736 | tf_op jit(solution)/shard_map/ppermute | solution.py:235
  103.5 14.6 %collective-permute-start.19 = (bf16[256,1024]{1,0:T(8,128)(2,1)S(1)}, bf16[256,1024]{1,0:T(8,128)(2,1)S(1)}, u32[]{:S(2)}, u32[]{:S(2)}) collective-permute-start(bf16[256,1024]{1,0:T(8,128)(2,1)S(1)} %collective-permute-done.10.refs_9_), channel_id=1, source_target_pairs={{0,3},{1,0},{2,1},{3,2},{4,7},{5,4},{6,5},{7,6},{8,11},{9,8},{10,9... | collective-permute-start | bytes 1572872 | tf_op jit(solution)/shard_map/ppermute | solution.py:244
  110.2 15.6 %collective-permute-start.25 = (bf16[512,1024]{1,0:T(8,128)(2,1)S(1)}, bf16[512,1024]{1,0:T(8,128)(2,1)S(1)}, u32[]{:S(2)}, u32[]{:S(2)}) collective-permute-start(bf16[512,1024]{1,0:T(8,128)(2,1)S(1)} %collective-permute-done.4.refs_17_.refs_12_.refs_13_), channel_id=1, source_target_pairs={{0,8},{8,0},{16,24},{24,16},{32,40},{40,32},{48,56},{56,48},{64,72... | collective-permute-start | bytes 3145736 | tf_op jit(solution)/shard_map/ppermute | solution.py:235
  118.1 15.0 %collective-permute-start.15 = (bf16[256,1024]{1,0:T(8,128)(2,1)S(1)}, bf16[256,1024]{1,0:T(8,128)(2,1)S(1)}, u32[]{:S(2)}, u32[]{:S(2)}) collective-permute-start(bf16[256,1024]{1,0:T(8,128)(2,1)S(1)} %collective-permute-done.11.refs_6_), channel_id=1, source_target_pairs={{0,1},{1,2},{2,3},{3,0},{4,5},{5,6},{6,7},{7,4},{8,9},{9,10},{10,1... | collective-permute-start | bytes 1572872 | tf_op jit(solution)/shard_map/ppermute | solution.py:244
  121.5 11.6 %collective-permute-start.22 = (bf16[256,1024]{1,0:T(8,128)(2,1)S(1)}, bf16[256,1024]{1,0:T(8,128)(2,1)}, u32[]{:S(2)}, u32[]{:S(2)}) collective-permute-start(bf16[256,1024]{1,0:T(8,128)(2,1)S(1)} %collective-permute-done.19.refs_11_), channel_id=1, source_target_pairs={{0,3},{1,0},{2,1},{3,2},{4,7},{5,4},{6,5},{7,6},{8,11},{9,8},{10,9... | collective-permute-start | bytes 1572872 | tf_op jit(solution)/shard_map/ppermute | solution.py:244
  122.5 13.7 %collective-permute-start.20 = (bf16[256,1024]{1,0:T(8,128)(2,1)}, bf16[256,1024]{1,0:T(8,128)(2,1)}, u32[]{:S(2)}, u32[]{:S(2)}) collective-permute-start(bf16[256,1024]{1,0:T(8,128)(2,1)} %collective-permute-done.13.refs_25_.refs_20_.refs_21_), channel_id=1, source_target_pairs={{0,16},{8,24},{16,32},{24,40},{32,48},{40,56},{48,0},{56,8},{64,80... | collective-permute-start | bytes 1572872 | tf_op jit(solution)/shard_map/ppermute | solution.py:235
  122.5 13.7 %collective-permute-start.21 = (bf16[256,1024]{1,0:T(8,128)(2,1)}, bf16[256,1024]{1,0:T(8,128)(2,1)}, u32[]{:S(2)}, u32[]{:S(2)}) collective-permute-start(bf16[256,1024]{1,0:T(8,128)(2,1)} %collective-permute-done.14.refs_30_.refs_25_.refs_26_), channel_id=1, source_target_pairs={{0,48},{8,56},{16,0},{24,8},{32,16},{40,24},{48,32},{56,40},{64,11... | collective-permute-start | bytes 1572872 | tf_op jit(solution)/shard_map/ppermute | solution.py:235
  159.8 15.2 %collective-permute-start.39 = (bf16[256,1024]{1,0:T(8,128)(2,1)}, bf16[256,1024]{1,0:T(8,128)(2,1)}, u32[]{:S(2)}, u32[]{:S(2)}) collective-permute-start(bf16[256,1024]{1,0:T(8,128)(2,1)} %get-tuple-element.108.refs_0_), channel_id=1, source_target_pairs={{0,4},{1,5},{2,6},{3,7},{4,0},{5,1},{6,2},{7,3},{8,12},{9,13},{10,... | collective-permute-start | bytes 1572872 | tf_op jit(solution)/shard_map/ppermute | solution.py:244
  160.6 15.0 %collective-permute-start.36 = (bf16[256,1024]{1,0:T(8,128)(2,1)}, bf16[256,1024]{1,0:T(8,128)(2,1)S(1)}, u32[]{:S(2)}, u32[]{:S(2)}) collective-permute-start(bf16[256,1024]{1,0:T(8,128)(2,1)} %get-tuple-element.108.refs_0_), channel_id=1, source_target_pairs={{0,3},{1,0},{2,1},{3,2},{4,7},{5,4},{6,5},{7,6},{8,11},{9,8},{10,9... | collective-permute-start | bytes 1572872 | tf_op jit(solution)/shard_map/ppermute | solution.py:244
  162.2 14.9 %collective-permute-start.35 = (bf16[256,1024]{1,0:T(8,128)(2,1)}, bf16[256,1024]{1,0:T(8,128)(2,1)S(1)}, u32[]{:S(2)}, u32[]{:S(2)}) collective-permute-start(bf16[256,1024]{1,0:T(8,128)(2,1)} %get-tuple-element.108.refs_0_), channel_id=1, source_target_pairs={{0,1},{1,2},{2,3},{3,0},{4,5},{5,6},{6,7},{7,4},{8,9},{9,10},{10,1... | collective-permute-start | bytes 1572872 | tf_op jit(solution)/shard_map/ppermute | solution.py:244
  162.7 22.7 %collective-permute-start.40 = (bf16[256,1024]{1,0:T(8,128)(2,1)}, bf16[256,1024]{1,0:T(8,128)(2,1)}, u32[]{:S(2)}, u32[]{:S(2)}) collective-permute-start(bf16[256,1024]{1,0:T(8,128)(2,1)} %get-tuple-element.110.refs_4_), channel_id=1, source_target_pairs={{0,4},{1,5},{2,6},{3,7},{4,0},{5,1},{6,2},{7,3},{8,12},{9,13},{10,... | collective-permute-start | bytes 1572872 | tf_op jit(solution)/shard_map/ppermute | solution.py:244
  164.0 21.8 %collective-permute-start.38 = (bf16[256,1024]{1,0:T(8,128)(2,1)}, bf16[256,1024]{1,0:T(8,128)(2,1)S(1)}, u32[]{:S(2)}, u32[]{:S(2)}) collective-permute-start(bf16[256,1024]{1,0:T(8,128)(2,1)} %get-tuple-element.110.refs_4_), channel_id=1, source_target_pairs={{0,3},{1,0},{2,1},{3,2},{4,7},{5,4},{6,5},{7,6},{8,11},{9,8},{10,9... | collective-permute-start | bytes 1572872 | tf_op jit(solution)/shard_map/ppermute | solution.py:244
  175.0 13.8 %collective-permute-start.37 = (bf16[256,1024]{1,0:T(8,128)(2,1)}, bf16[256,1024]{1,0:T(8,128)(2,1)S(1)}, u32[]{:S(2)}, u32[]{:S(2)}) collective-permute-start(bf16[256,1024]{1,0:T(8,128)(2,1)} %get-tuple-element.110.refs_4_), channel_id=1, source_target_pairs={{0,1},{1,2},{2,3},{3,0},{4,5},{5,6},{6,7},{7,4},{8,9},{9,10},{10,1... | collective-permute-start | bytes 1572872 | tf_op jit(solution)/shard_map/ppermute | solution.py:244
  190.4 13.0 %collective-permute-start.41 = (bf16[256,1024]{1,0:T(8,128)(2,1)S(1)}, bf16[256,1024]{1,0:T(8,128)(2,1)S(1)}, u32[]{:S(2)}, u32[]{:S(2)}) collective-permute-start(bf16[256,1024]{1,0:T(8,128)(2,1)S(1)} %collective-permute-done.35.refs_1_), channel_id=1, source_target_pairs={{0,1},{1,2},{2,3},{3,0},{4,5},{5,6},{6,7},{7,4},{8,9},{9,10},{10,1... | collective-permute-start | bytes 1572872 | tf_op jit(solution)/shard_map/ppermute | solution.py:244
  191.6 26.4 %collective-permute-start.45 = (bf16[256,1024]{1,0:T(8,128)(2,1)S(1)}, bf16[256,1024]{1,0:T(8,128)(2,1)}, u32[]{:S(2)}, u32[]{:S(2)}) collective-permute-start(bf16[256,1024]{1,0:T(8,128)(2,1)S(1)} %collective-permute-done.35.refs_1_), channel_id=1, source_target_pairs={{0,4},{1,5},{2,6},{3,7},{4,0},{5,1},{6,2},{7,3},{8,12},{9,13},{10,... | collective-permute-start | bytes 1572872 | tf_op jit(solution)/shard_map/ppermute | solution.py:244
  192.8 25.1 %collective-permute-start.46 = (bf16[256,1024]{1,0:T(8,128)(2,1)S(1)}, bf16[256,1024]{1,0:T(8,128)(2,1)}, u32[]{:S(2)}, u32[]{:S(2)}) collective-permute-start(bf16[256,1024]{1,0:T(8,128)(2,1)S(1)} %collective-permute-done.36.refs_2_), channel_id=1, source_target_pairs={{0,4},{1,5},{2,6},{3,7},{4,0},{5,1},{6,2},{7,3},{8,12},{9,13},{10,... | collective-permute-start | bytes 1572872 | tf_op jit(solution)/shard_map/ppermute | solution.py:244
  203.3 14.6 %collective-permute-start.44 = (bf16[256,1024]{1,0:T(8,128)(2,1)}, bf16[256,1024]{1,0:T(8,128)(2,1)S(1)}, u32[]{:S(2)}, u32[]{:S(2)}) collective-permute-start(bf16[256,1024]{1,0:T(8,128)(2,1)} %collective-permute-done.40.refs_4_), channel_id=1, source_target_pairs={{0,3},{1,0},{2,1},{3,2},{4,7},{5,4},{6,5},{7,6},{8,11},{9,8},{10,9... | collective-permute-start | bytes 1572872 | tf_op jit(solution)/shard_map/ppermute | solution.py:244
  204.4 13.6 %collective-permute-start.43 = (bf16[256,1024]{1,0:T(8,128)(2,1)}, bf16[256,1024]{1,0:T(8,128)(2,1)S(1)}, u32[]{:S(2)}, u32[]{:S(2)}) collective-permute-start(bf16[256,1024]{1,0:T(8,128)(2,1)} %collective-permute-done.40.refs_4_), channel_id=1, source_target_pairs={{0,1},{1,2},{2,3},{3,0},{4,5},{5,6},{6,7},{7,4},{8,9},{9,10},{10,1... | collective-permute-start | bytes 1572872 | tf_op jit(solution)/shard_map/ppermute | solution.py:244
  206.0 19.1 %collective-permute-start.47 = (bf16[256,1024]{1,0:T(8,128)(2,1)S(1)}, bf16[256,1024]{1,0:T(8,128)(2,1)}, u32[]{:S(2)}, u32[]{:S(2)}) collective-permute-start(bf16[256,1024]{1,0:T(8,128)(2,1)S(1)} %collective-permute-done.41.refs_3_), channel_id=1, source_target_pairs={{0,4},{1,5},{2,6},{3,7},{4,0},{5,1},{6,2},{7,3},{8,12},{9,13},{10,... | collective-permute-start | bytes 1572872 | tf_op jit(solution)/shard_map/ppermute | solution.py:244
  (58 other events, 964.5 us)

commit v2 on v1

--- a/solution.py
+++ b/solution.py
@@ -104,7 +104,7 @@
         total_in, refs = refs[0], refs[1:]
     if has_base:
         base, refs = refs[0], refs[1:]
-    outs, (held, staged, total, base_held, left_sems, right_sems, extra_sems) = refs[:n_out], refs[n_out:]
+    outs, (held, staged, total, total_held, base_held, left_sems, right_sems, extra_sems) = refs[:n_out], refs[n_out:]
     places, (slots, depth, _) = held.shape[0], staged.shape
     copies = []
     for index, (left, (source, first, count)) in enumerate(zip(lefts, left_parts)):
@@ -136,16 +136,13 @@
 
     for index in range(slots - 1):
         when_wanted(index, functools.partial(start, index))
+    total[...] = jnp.zeros_like(total)
     if first_total:
-        total_copy = pltpu.make_async_copy(total_in, total, extra_sems.at[0])
+        total_copy = pltpu.make_async_copy(total_in, total_held, extra_sems.at[0])
         total_copy.start()
-    else:
-        total[...] = jnp.zeros_like(total)
     if has_base:
         base_copy = pltpu.make_async_copy(base, base_held, extra_sems.at[1])
         base_copy.start()
-    if first_total:
-        total_copy.wait()
 
     @pl.loop(0, len(loads))
     def _(index):
@@ -163,12 +160,17 @@
 
         when_wanted(index, add)
 
+    if first_total:
+        total_copy.wait()
     if has_base:
         base_copy.wait()
     first = 0
     for out in outs:
         count = out.shape[0]
-        value = total[first : first + count, :] * factor
+        value = total[first : first + count, :]
+        if first_total:
+            value += total_held[first : first + count, :]
+        value *= factor
         if has_base:
             value = 1.5 * base_held[first : first + count, :].astype(jnp.float32) - value
         out[...] = value.astype(out.dtype)
@@ -193,7 +195,7 @@
     extra = [value for value in (first_total, base) if value is not None]
     count = len(rights) if part is None else len(rights) // 2
     rows = sum(outs)
-    slots = 5 if part is None else 8
+    slots = 3
     return pl.pallas_call(
         functools.partial(
             product_kernel,
@@ -211,6 +213,7 @@
         scratch_shapes=[
             pltpu.VMEM((count, rows, width), kind),
             pltpu.VMEM((slots, width, width), kind),
+            pltpu.VMEM((rows, width), jnp.float32),
             pltpu.VMEM((rows, width), jnp.float32),
             pltpu.VMEM((rows, width), kind),
             pltpu.SemaphoreType.DMA((count,)),

time: 241 us -> 238 us (0.988)
  transfers between devices with their start and end apart: 50 -> 50, of which waited for: 30 -> 32; matrix products, arithmetic and copies ran while one was open for 1% -> 1% of each run, Pallas kernels for 4% -> 4%
where the time goes in v2:
time: 238 us
  waiting for transfers between devices  115 us (48%)
  starting transfers between devices  48.2 us (20%)
  Pallas kernels  38.4 us (16%)
  blocking collectives  26.4 us (11%)
  local copies, waits for them, and re-layouts  9.44 us (4%)
    ppermute x27, waiting for transfers between devices, over_col(): return lax.ppermute(value, 'col', pairs)  68.5 us
    ppermute x23, waiting for transfers between devices, over_row(): return lax.ppermute(value, 'row', pairs)  46.2 us
    pallas_call x3, Pallas kernels, product(): pl.pallas_call(functools.partial(product_kernel, factor, left_parts, righ...  35.7 us
    ppermute x27, starting transfers between devices, over_col(): return lax.ppermute(value, 'col', pairs)  30.8 us
    all_to_all x1, blocking collectives, local_tile(): received = lax.all_to_all(send, 'row', 0, 0, tiled=True)  26.4 us
    ppermute x23, starting transfers between devices, over_row(): return lax.ppermute(value, 'row', pairs)  17.4 us
    unnamed x80, local copies, waits for them, and re-layouts  6.62 us
  transfers between devices with their start and end apart: 50, of which 32 were waited for; matrix products, arithmetic and copies ran while one was open for 1% of the time, Pallas kernels for 4%

profile of v2, /device:TPU:0, one launch (start us, length us, event | category | flops | bytes accessed | tf_op | source)
XLA Modules:
  0.0 238.4 jit_solution(2579002594396377459)
XLA Ops:
  4.6 26.4 %all_to_all.5.received = bf16[16,272,128]{2,1,0:T(8,128)(2,1)S(1)} all-to-all(bf16[16,272,128]{2,1,0:T(8,128)(2,1)S(1)} %pack.1), channel_id=1, replica_groups=mesh['row'=16,'col'=8] {'row'}, dimensions={0} | all-to-all | bytes 2228224 | tf_op jit(solution)/shard_map/all_to_all | solution.py:83
  34.4 2.8 %collective-permute-start.2 = (bf16[512,1024]{1,0:T(8,128)(2,1)S(1)}, bf16[512,1024]{1,0:T(8,128)(2,1)S(1)}, u32[]{:S(2)}, u32[]{:S(2)}) collective-permute-start(bf16[512,1024]{1,0:T(8,128)(2,1)S(1)} %unpack.1.refs_0_.refs_13_.refs_8_.refs_9_.refs_34_), channel_id=1, source_target_pairs={{0,3},{1,0},{2,1},{3,2},{4,7},{5,4},{6,5},{7,6},{8,11},{9,8},{10,9... | collective-permute-start | bytes 3145736 | tf_op jit(solution)/shard_map/ppermute | solution.py:247
  37.8 19.8 %collective-permute-done.4.refs_17_.refs_12_.refs_13_ = bf16[512,1024]{1,0:T(8,128)(2,1)S(1)} collective-permute-done((bf16[512,1024]{1,0:T(8,128)(2,1)S(1)}, bf16[512,1024]{1,0:T(8,128)(2,1)S(1)}, u32[]{:S(2)}, u32[]{:S(2)}) %collective-permute-start.4) | collective-permute-done | bytes 1048608 | tf_op jit(solution)/shard_map/ppermute | solution.py:238
  57.6 2.2 collective-permute-done.3.refs_15_.refs_10_.refs_11_
  59.8 2.9 %collective-permute-done.1.refs_1_ = bf16[512,1024]{1,0:T(8,128)(2,1)S(1)} collective-permute-done((bf16[512,1024]{1,0:T(8,128)(2,1)S(1)}, bf16[512,1024]{1,0:T(8,128)(2,1)S(1)}, u32[]{:S(2)}, u32[]{:S(2)}) %collective-permute-start.1) | collective-permute-done | bytes 1048608 | tf_op jit(solution)/shard_map/ppermute | solution.py:247
  63.6 2.5 %collective-permute-start.9 = (bf16[256,1024]{1,0:T(8,128)(2,1)S(1)}, bf16[256,1024]{1,0:T(8,128)(2,1)S(1)}, u32[]{:S(2)}, u32[]{:S(2)}) collective-permute-start(bf16[256,1024]{1,0:T(8,128)(2,1)S(1)} %slice.35), channel_id=1, source_target_pairs={{0,48},{8,56},{16,0},{24,8},{32,16},{40,24},{48,32},{56,40},{64,11... | collective-permute-start | bytes 1572872 | tf_op jit(solution)/shard_map/ppermute | solution.py:238
  66.1 2.5 %collective-permute-start.7 = (bf16[256,1024]{1,0:T(8,128)(2,1)S(1)}, bf16[256,1024]{1,0:T(8,128)(2,1)S(1)}, u32[]{:S(2)}, u32[]{:S(2)}) collective-permute-start(bf16[256,1024]{1,0:T(8,128)(2,1)S(1)} %slice.33), channel_id=1, source_target_pairs={{0,3},{1,0},{2,1},{3,2},{4,7},{5,4},{6,5},{7,6},{8,11},{9,8},{10,9... | collective-permute-start | bytes 1572872 | tf_op jit(solution)/shard_map/ppermute | solution.py:247
  69.7 6.0 %collective-permute-done.9.refs_20_.refs_15_.refs_16_ = bf16[256,1024]{1,0:T(8,128)(2,1)S(1)} collective-permute-done((bf16[256,1024]{1,0:T(8,128)(2,1)S(1)}, bf16[256,1024]{1,0:T(8,128)(2,1)S(1)}, u32[]{:S(2)}, u32[]{:S(2)}) %collective-permute-start.9) | collective-permute-done | bytes 524320 | tf_op jit(solution)/shard_map/ppermute | solution.py:238
  75.7 3.4 %collective-permute-done.8.refs_19_.refs_14_.refs_15_ = bf16[256,1024]{1,0:T(8,128)(2,1)S(1)} collective-permute-done((bf16[256,1024]{1,0:T(8,128)(2,1)S(1)}, bf16[256,1024]{1,0:T(8,128)(2,1)S(1)}, u32[]{:S(2)}, u32[]{:S(2)}) %collective-permute-start.8) | collective-permute-done | bytes 524320 | tf_op jit(solution)/shard_map/ppermute | solution.py:238
  84.5 3.0 %collective-permute-start.14 = (bf16[256,1024]{1,0:T(8,128)(2,1)S(1)}, bf16[256,1024]{1,0:T(8,128)(2,1)}, u32[]{:S(2)}, u32[]{:S(2)}) collective-permute-start(bf16[256,1024]{1,0:T(8,128)(2,1)S(1)} %get-tuple-element.83), channel_id=1, source_target_pairs={{0,48},{8,56},{16,0},{24,8},{32,16},{40,24},{48,32},{56,40},{64,11... | collective-permute-start | bytes 1572872 | tf_op jit(solution)/shard_map/ppermute | solution.py:238
  87.5 5.5 %collective-permute-done.10.refs_9_ = bf16[256,1024]{1,0:T(8,128)(2,1)S(1)} collective-permute-done((bf16[256,1024]{1,0:T(8,128)(2,1)S(1)}, bf16[256,1024]{1,0:T(8,128)(2,1)S(1)}, u32[]{:S(2)}, u32[]{:S(2)}) %collective-permute-start.10) | collective-permute-done | bytes 524320 | tf_op jit(solution)/shard_map/ppermute | solution.py:247
  94.3 5.5 %collective-permute-done.13.refs_25_.refs_20_.refs_21_ = bf16[256,1024]{1,0:T(8,128)(2,1)} collective-permute-done((bf16[256,1024]{1,0:T(8,128)(2,1)S(1)}, bf16[256,1024]{1,0:T(8,128)(2,1)}, u32[]{:S(2)}, u32[]{:S(2)}) %collective-permute-start.13) | collective-permute-done | bytes 524320 | tf_op jit(solution)/shard_map/ppermute | solution.py:238
  99.8 3.2 %collective-permute-start.17 = (bf16[256,1024]{1,0:T(8,128)(2,1)S(1)}, bf16[256,1024]{1,0:T(8,128)(2,1)S(1)}, u32[]{:S(2)}, u32[]{:S(2)}) collective-permute-start(bf16[256,1024]{1,0:T(8,128)(2,1)S(1)} %get-tuple-element.84), channel_id=1, source_target_pairs={{0,48},{8,56},{16,0},{24,8},{32,16},{40,24},{48,32},{56,40},{64,11... | collective-permute-start | bytes 1572872 | tf_op jit(solution)/shard_map/ppermute | solution.py:238
  103.5 3.4 %collective-permute-start.19 = (bf16[256,1024]{1,0:T(8,128)(2,1)S(1)}, bf16[256,1024]{1,0:T(8,128)(2,1)S(1)}, u32[]{:S(2)}, u32[]{:S(2)}) collective-permute-start(bf16[256,1024]{1,0:T(8,128)(2,1)S(1)} %collective-permute-done.10.refs_9_), channel_id=1, source_target_pairs={{0,3},{1,0},{2,1},{3,2},{4,7},{5,4},{6,5},{7,6},{8,11},{9,8},{10,9... | collective-permute-start | bytes 1572872 | tf_op jit(solution)/shard_map/ppermute | solution.py:247
  106.9 3.3 %collective-permute-done.16.refs_26_.refs_21_.refs_22_ = bf16[256,1024]{1,0:T(8,128)(2,1)S(1)} collective-permute-done((bf16[256,1024]{1,0:T(8,128)(2,1)S(1)}, bf16[256,1024]{1,0:T(8,128)(2,1)S(1)}, u32[]{:S(2)}, u32[]{:S(2)}) %collective-permute-start.16) | collective-permute-done | bytes 524320 | tf_op jit(solution)/shard_map/ppermute | solution.py:238
  110.3 8.0 %collective-permute-done.19.refs_11_ = bf16[256,1024]{1,0:T(8,128)(2,1)S(1)} collective-permute-done((bf16[256,1024]{1,0:T(8,128)(2,1)S(1)}, bf16[256,1024]{1,0:T(8,128)(2,1)S(1)}, u32[]{:S(2)}, u32[]{:S(2)}) %collective-permute-start.19) | collective-permute-done | bytes 524320 | tf_op jit(solution)/shard_map/ppermute | solution.py:247
  118.3 3.4 %collective-permute-done.18.refs_10_ = bf16[256,1024]{1,0:T(8,128)(2,1)S(1)} collective-permute-done((bf16[256,1024]{1,0:T(8,128)(2,1)S(1)}, bf16[256,1024]{1,0:T(8,128)(2,1)S(1)}, u32[]{:S(2)}, u32[]{:S(2)}) %collective-permute-start.18) | collective-permute-done | bytes 524320 | tf_op jit(solution)/shard_map/ppermute | solution.py:247
  122.7 3.2 %collective-permute-start.21 = (bf16[256,1024]{1,0:T(8,128)(2,1)}, bf16[256,1024]{1,0:T(8,128)(2,1)}, u32[]{:S(2)}, u32[]{:S(2)}) collective-permute-start(bf16[256,1024]{1,0:T(8,128)(2,1)} %collective-permute-done.14.refs_30_.refs_25_.refs_26_), channel_id=1, source_target_pairs={{0,48},{8,56},{16,0},{24,8},{32,16},{40,24},{48,32},{56,40},{64,11... | collective-permute-start | bytes 1572872 | tf_op jit(solution)/shard_map/ppermute | solution.py:238
  126.0 7.4 %collective-permute-done.15.refs_8_ = bf16[256,1024]{1,0:T(8,128)(2,1)S(1)} collective-permute-done((bf16[256,1024]{1,0:T(8,128)(2,1)S(1)}, bf16[256,1024]{1,0:T(8,128)(2,1)S(1)}, u32[]{:S(2)}, u32[]{:S(2)}) %collective-permute-start.15) | collective-permute-done | bytes 524320 | tf_op jit(solution)/shard_map/ppermute | solution.py:247
  133.8 2.6 %collective-permute-done.20.refs_33_.refs_28_.refs_29_ = bf16[256,1024]{1,0:T(8,128)(2,1)} collective-permute-done((bf16[256,1024]{1,0:T(8,128)(2,1)}, bf16[256,1024]{1,0:T(8,128)(2,1)}, u32[]{:S(2)}, u32[]{:S(2)}) %collective-permute-start.20) | collective-permute-done | bytes 524320 | tf_op jit(solution)/shard_map/ppermute | solution.py:238
  144.1 15.1 %square.1 = (bf16[256,1024]{1,0:T(8,128)(2,1)}, bf16[256,1024]{1,0:T(8,128)(2,1)}) custom-call(s32[13]{0:T(128)} %stack.58.left_at, s32[8]{0:T(128)} %stack.53.right_at, s32[1]{0:T(128)} %bitcast.12.core, s32[1]{0:T(128)} %constant.244.clone.1.want, bf16[512,1024]{1,0:T(8,128)(2,1)} %copy-done, bf16[512,1024]{1,0:T(8,128)(2,1)} %copy-done.28, ...), custom_call_target="tpu_custom_call" | custom-call | flops 8589934592 | bytes 25165824 | tf_op jit(solution)/shard_map/square/pallas_call | solution.py:199
  163.3 3.0 %collective-permute-start.38 = (bf16[256,1024]{1,0:T(8,128)(2,1)}, bf16[256,1024]{1,0:T(8,128)(2,1)S(1)}, u32[]{:S(2)}, u32[]{:S(2)}) collective-permute-start(bf16[256,1024]{1,0:T(8,128)(2,1)} %get-tuple-element.110.refs_4_), channel_id=1, source_target_pairs={{0,3},{1,0},{2,1},{3,2},{4,7},{5,4},{6,5},{7,6},{8,11},{9,8},{10,9... | collective-permute-start | bytes 1572872 | tf_op jit(solution)/shard_map/ppermute | solution.py:247
  166.3 8.1 %collective-permute-done.39.refs_0_ = bf16[256,1024]{1,0:T(8,128)(2,1)} collective-permute-done((bf16[256,1024]{1,0:T(8,128)(2,1)}, bf16[256,1024]{1,0:T(8,128)(2,1)}, u32[]{:S(2)}, u32[]{:S(2)}) %collective-permute-start.39) | collective-permute-done | bytes 524320 | tf_op jit(solution)/shard_map/ppermute | solution.py:247
  176.3 8.5 %collective-permute-done.40.refs_4_ = bf16[256,1024]{1,0:T(8,128)(2,1)} collective-permute-done((bf16[256,1024]{1,0:T(8,128)(2,1)}, bf16[256,1024]{1,0:T(8,128)(2,1)}, u32[]{:S(2)}, u32[]{:S(2)}) %collective-permute-start.40) | collective-permute-done | bytes 524320 | tf_op jit(solution)/shard_map/ppermute | solution.py:247
  184.9 3.2 %collective-permute-done.37.refs_5_ = bf16[256,1024]{1,0:T(8,128)(2,1)S(1)} collective-permute-done((bf16[256,1024]{1,0:T(8,128)(2,1)}, bf16[256,1024]{1,0:T(8,128)(2,1)S(1)}, u32[]{:S(2)}, u32[]{:S(2)}) %collective-permute-start.37) | collective-permute-done | bytes 524320 | tf_op jit(solution)/shard_map/ppermute | solution.py:247
  193.0 7.4 %collective-permute-done.42.refs_7_ = bf16[256,1024]{1,0:T(8,128)(2,1)S(1)} collective-permute-done((bf16[256,1024]{1,0:T(8,128)(2,1)S(1)}, bf16[256,1024]{1,0:T(8,128)(2,1)S(1)}, u32[]{:S(2)}, u32[]{:S(2)}) %collective-permute-start.42) | collective-permute-done | bytes 524320 | tf_op jit(solution)/shard_map/ppermute | solution.py:247
  200.4 2.0 collective-permute-done.41.refs_3_
  206.7 10.1 %step_first.1.refs_33_ = f32[512,1024]{1,0:T(8,128)} custom-call(s32[8]{0:T(128)} %stack.59.left_at, s32[8]{0:T(128)} %stack.53.right_at, s32[1]{0:T(128)} %bitcast.12.core, s32[1]{0:T(128)} %bitcast.20.want, bf16[256,1024]{1,0:T(8,128)(2,1)} %get-tuple-element.108.refs_0_, bf16[256,1024]{1,0:T(8,128)(2,1)} %copy-done.22, bf16[256,1024]{1,0:T(8,128)(2,1)} %copy-done.21, ...), custom_call_target="tpu_custom_call" | custom-call | flops 4294967296 | bytes 12582912 | tf_op jit(solution)/shard_map/step_first/pallas_call | solution.py:199
  217.3 2.1 collective-permute-start.49
  220.0 4.4 %collective-permute-done.47.refs_3_ = bf16[256,1024]{1,0:T(8,128)(2,1)} collective-permute-done((bf16[256,1024]{1,0:T(8,128)(2,1)S(1)}, bf16[256,1024]{1,0:T(8,128)(2,1)}, u32[]{:S(2)}, u32[]{:S(2)}) %collective-permute-start.47) | collective-permute-done | bytes 524320 | tf_op jit(solution)/shard_map/ppermute | solution.py:247
  224.4 2.5 %collective-permute-done.48.refs_7_ = bf16[128,1024]{1,0:T(8,128)(2,1)S(1)} collective-permute-done((bf16[128,1024]{1,0:T(8,128)(2,1)S(1)}, bf16[128,1024]{1,0:T(8,128)(2,1)S(1)}, u32[]{:S(2)}, u32[]{:S(2)}) %collective-permute-start.48) | collective-permute-done | bytes 262176 | tf_op jit(solution)/shard_map/ppermute | solution.py:247
  227.6 10.6 %step_last.1 = f32[512,1024]{1,0:T(8,128)} custom-call(s32[9]{0:T(128)} %stack.44.left_at, s32[8]{0:T(128)} %stack.53.right_at, s32[1]{0:T(128)} %bitcast.12.core, s32[1]{0:T(128)} %bitcast.13.want, bf16[256,1024]{1,0:T(8,128)(2,1)} %collective-permute-done.39.refs_0_, bf16[256,1024]{1,0:T(8,128)(2,1)} %collective-permute-done.45.refs_1_, ...), custom_call_target="tpu_custom_call" | custom-call | flops 4294967296 | bytes 12582912 | tf_op jit(solution)/shard_map/step_last/pallas_call | solution.py:199
  (166 shorter events, 43.6 us)
Async XLA Ops:
  32.3 25.3 %collective-permute-start.4 = (bf16[512,1024]{1,0:T(8,128)(2,1)S(1)}, bf16[512,1024]{1,0:T(8,128)(2,1)S(1)}, u32[]{:S(2)}, u32[]{:S(2)}) collective-permute-start(bf16[512,1024]{1,0:T(8,128)(2,1)S(1)} %unpack.1.refs_0_.refs_13_.refs_8_.refs_9_.refs_34_), channel_id=1, source_target_pairs={{0,48},{8,56},{16,0},{24,8},{32,16},{40,24},{48,32},{56,40},{64,11... | collective-permute-start | bytes 3145736 | tf_op jit(solution)/shard_map/ppermute | solution.py:238
  33.6 26.2 %collective-permute-start.3 = (bf16[512,1024]{1,0:T(8,128)(2,1)S(1)}, bf16[512,1024]{1,0:T(8,128)(2,1)S(1)}, u32[]{:S(2)}, u32[]{:S(2)}) collective-permute-start(bf16[512,1024]{1,0:T(8,128)(2,1)S(1)} %unpack.1.refs_0_.refs_13_.refs_8_.refs_9_.refs_34_), channel_id=1, source_target_pairs={{0,16},{8,24},{16,32},{24,40},{32,48},{40,56},{48,0},{56,8},{64,80... | collective-permute-start | bytes 3145736 | tf_op jit(solution)/shard_map/ppermute | solution.py:238
  34.4 25.4 %collective-permute-start.2 = (bf16[512,1024]{1,0:T(8,128)(2,1)S(1)}, bf16[512,1024]{1,0:T(8,128)(2,1)S(1)}, u32[]{:S(2)}, u32[]{:S(2)}) collective-permute-start(bf16[512,1024]{1,0:T(8,128)(2,1)S(1)} %unpack.1.refs_0_.refs_13_.refs_8_.refs_9_.refs_34_), channel_id=1, source_target_pairs={{0,3},{1,0},{2,1},{3,2},{4,7},{5,4},{6,5},{7,6},{8,11},{9,8},{10,9... | collective-permute-start | bytes 3145736 | tf_op jit(solution)/shard_map/ppermute | solution.py:247
  37.2 25.5 %collective-permute-start.1 = (bf16[512,1024]{1,0:T(8,128)(2,1)S(1)}, bf16[512,1024]{1,0:T(8,128)(2,1)S(1)}, u32[]{:S(2)}, u32[]{:S(2)}) collective-permute-start(bf16[512,1024]{1,0:T(8,128)(2,1)S(1)} %unpack.1.refs_0_.refs_13_.refs_8_.refs_9_.refs_34_), channel_id=1, source_target_pairs={{0,1},{1,2},{2,3},{3,0},{4,5},{5,6},{6,7},{7,4},{8,9},{9,10},{10,1... | collective-permute-start | bytes 3145736 | tf_op jit(solution)/shard_map/ppermute | solution.py:247
  37.2 25.8 %collective-permute-start = (bf16[512,1024]{1,0:T(8,128)(2,1)S(1)}, bf16[512,1024]{1,0:T(8,128)(2,1)S(1)}, u32[]{:S(2)}, u32[]{:S(2)}) collective-permute-start(bf16[512,1024]{1,0:T(8,128)(2,1)S(1)} %unpack.1.refs_0_.refs_13_.refs_8_.refs_9_.refs_34_), channel_id=1, source_target_pairs={{0,64},{8,72},{16,80},{24,88},{32,96},{40,104},{48,112},{56,120},{... | collective-permute-start | bytes 3145736 | tf_op jit(solution)/shard_map/ppermute | solution.py:238
  63.6 12.1 %collective-permute-start.9 = (bf16[256,1024]{1,0:T(8,128)(2,1)S(1)}, bf16[256,1024]{1,0:T(8,128)(2,1)S(1)}, u32[]{:S(2)}, u32[]{:S(2)}) collective-permute-start(bf16[256,1024]{1,0:T(8,128)(2,1)S(1)} %slice.35), channel_id=1, source_target_pairs={{0,48},{8,56},{16,0},{24,8},{32,16},{40,24},{48,32},{56,40},{64,11... | collective-permute-start | bytes 1572872 | tf_op jit(solution)/shard_map/ppermute | solution.py:238
  66.1 13.0 %collective-permute-start.8 = (bf16[256,1024]{1,0:T(8,128)(2,1)S(1)}, bf16[256,1024]{1,0:T(8,128)(2,1)S(1)}, u32[]{:S(2)}, u32[]{:S(2)}) collective-permute-start(bf16[256,1024]{1,0:T(8,128)(2,1)S(1)} %slice.34), channel_id=1, source_target_pairs={{0,16},{8,24},{16,32},{24,40},{32,48},{40,56},{48,0},{56,8},{64,80... | collective-permute-start | bytes 1572872 | tf_op jit(solution)/shard_map/ppermute | solution.py:238
  66.1 13.0 %collective-permute-start.7 = (bf16[256,1024]{1,0:T(8,128)(2,1)S(1)}, bf16[256,1024]{1,0:T(8,128)(2,1)S(1)}, u32[]{:S(2)}, u32[]{:S(2)}) collective-permute-start(bf16[256,1024]{1,0:T(8,128)(2,1)S(1)} %slice.33), channel_id=1, source_target_pairs={{0,3},{1,0},{2,1},{3,2},{4,7},{5,4},{6,5},{7,6},{8,11},{9,8},{10,9... | collective-permute-start | bytes 1572872 | tf_op jit(solution)/shard_map/ppermute | solution.py:247
  68.6 12.5 %collective-permute-start.6 = (bf16[256,1024]{1,0:T(8,128)(2,1)S(1)}, bf16[256,1024]{1,0:T(8,128)(2,1)S(1)}, u32[]{:S(2)}, u32[]{:S(2)}) collective-permute-start(bf16[256,1024]{1,0:T(8,128)(2,1)S(1)} %slice.32), channel_id=1, source_target_pairs={{0,1},{1,2},{2,3},{3,0},{4,5},{5,6},{6,7},{7,4},{8,9},{9,10},{10,1... | collective-permute-start | bytes 1572872 | tf_op jit(solution)/shard_map/ppermute | solution.py:247
  68.6 12.5 %collective-permute-start.5 = (bf16[256,1024]{1,0:T(8,128)(2,1)S(1)}, bf16[256,1024]{1,0:T(8,128)(2,1)S(1)}, u32[]{:S(2)}, u32[]{:S(2)}) collective-permute-start(bf16[256,1024]{1,0:T(8,128)(2,1)S(1)} %get-tuple-element.69), channel_id=1, source_target_pairs={{0,4},{1,5},{2,6},{3,7},{4,0},{5,1},{6,2},{7,3},{8,12},{9,13},{10,... | collective-permute-start | bytes 1572872 | tf_op jit(solution)/shard_map/ppermute | solution.py:247
  81.1 11.9 %collective-permute-start.12 = (bf16[256,1024]{1,0:T(8,128)(2,1)S(1)}, bf16[256,1024]{1,0:T(8,128)(2,1)S(1)}, u32[]{:S(2)}, u32[]{:S(2)}) collective-permute-start(bf16[256,1024]{1,0:T(8,128)(2,1)S(1)} %collective-permute-done.5.refs_5_), channel_id=1, source_target_pairs={{0,3},{1,0},{2,1},{3,2},{4,7},{5,4},{6,5},{7,6},{8,11},{9,8},{10,9... | collective-permute-start | bytes 1572872 | tf_op jit(solution)/shard_map/ppermute | solution.py:247
  87.5 12.3 %collective-permute-start.13 = (bf16[256,1024]{1,0:T(8,128)(2,1)S(1)}, bf16[256,1024]{1,0:T(8,128)(2,1)}, u32[]{:S(2)}, u32[]{:S(2)}) collective-permute-start(bf16[256,1024]{1,0:T(8,128)(2,1)S(1)} %get-tuple-element.84), channel_id=1, source_target_pairs={{0,16},{8,24},{16,32},{24,40},{32,48},{40,56},{48,0},{56,8},{64,80... | collective-permute-start | bytes 1572872 | tf_op jit(solution)/shard_map/ppermute | solution.py:238
  103.0 19.7 %collective-permute-start.23 = (bf16[512,1024]{1,0:T(8,128)(2,1)S(1)}, bf16[512,1024]{1,0:T(8,128)(2,1)S(1)}, u32[]{:S(2)}, u32[]{:S(2)}) collective-permute-start(bf16[512,1024]{1,0:T(8,128)(2,1)S(1)} %unpack.1.refs_0_.refs_13_.refs_8_.refs_9_.refs_34_), channel_id=1, source_target_pairs={{0,8},{8,0},{16,24},{24,16},{32,40},{40,32},{48,56},{56,48},{64,72... | collective-permute-start | bytes 3145736 | tf_op jit(solution)/shard_map/ppermute | solution.py:238
  103.0 19.7 %collective-permute-start.24 = (bf16[512,1024]{1,0:T(8,128)(2,1)S(1)}, bf16[512,1024]{1,0:T(8,128)(2,1)S(1)}, u32[]{:S(2)}, u32[]{:S(2)}) collective-permute-start(bf16[512,1024]{1,0:T(8,128)(2,1)S(1)} %collective-permute-done.3.refs_15_.refs_10_.refs_11_), channel_id=1, source_target_pairs={{0,8},{8,0},{16,24},{24,16},{32,40},{40,32},{48,56},{56,48},{64,72... | collective-permute-start | bytes 3145736 | tf_op jit(solution)/shard_map/ppermute | solution.py:238
  103.5 14.8 %collective-permute-start.19 = (bf16[256,1024]{1,0:T(8,128)(2,1)S(1)}, bf16[256,1024]{1,0:T(8,128)(2,1)S(1)}, u32[]{:S(2)}, u32[]{:S(2)}) collective-permute-start(bf16[256,1024]{1,0:T(8,128)(2,1)S(1)} %collective-permute-done.10.refs_9_), channel_id=1, source_target_pairs={{0,3},{1,0},{2,1},{3,2},{4,7},{5,4},{6,5},{7,6},{8,11},{9,8},{10,9... | collective-permute-start | bytes 1572872 | tf_op jit(solution)/shard_map/ppermute | solution.py:247
  110.2 15.8 %collective-permute-start.25 = (bf16[512,1024]{1,0:T(8,128)(2,1)S(1)}, bf16[512,1024]{1,0:T(8,128)(2,1)S(1)}, u32[]{:S(2)}, u32[]{:S(2)}) collective-permute-start(bf16[512,1024]{1,0:T(8,128)(2,1)S(1)} %collective-permute-done.4.refs_17_.refs_12_.refs_13_), channel_id=1, source_target_pairs={{0,8},{8,0},{16,24},{24,16},{32,40},{40,32},{48,56},{56,48},{64,72... | collective-permute-start | bytes 3145736 | tf_op jit(solution)/shard_map/ppermute | solution.py:238
  118.3 15.0 %collective-permute-start.15 = (bf16[256,1024]{1,0:T(8,128)(2,1)S(1)}, bf16[256,1024]{1,0:T(8,128)(2,1)S(1)}, u32[]{:S(2)}, u32[]{:S(2)}) collective-permute-start(bf16[256,1024]{1,0:T(8,128)(2,1)S(1)} %collective-permute-done.11.refs_6_), channel_id=1, source_target_pairs={{0,1},{1,2},{2,3},{3,0},{4,5},{5,6},{6,7},{7,4},{8,9},{9,10},{10,1... | collective-permute-start | bytes 1572872 | tf_op jit(solution)/shard_map/ppermute | solution.py:247
  121.7 11.6 %collective-permute-start.22 = (bf16[256,1024]{1,0:T(8,128)(2,1)S(1)}, bf16[256,1024]{1,0:T(8,128)(2,1)}, u32[]{:S(2)}, u32[]{:S(2)}) collective-permute-start(bf16[256,1024]{1,0:T(8,128)(2,1)S(1)} %collective-permute-done.19.refs_11_), channel_id=1, source_target_pairs={{0,3},{1,0},{2,1},{3,2},{4,7},{5,4},{6,5},{7,6},{8,11},{9,8},{10,9... | collective-permute-start | bytes 1572872 | tf_op jit(solution)/shard_map/ppermute | solution.py:247
  122.7 13.7 %collective-permute-start.20 = (bf16[256,1024]{1,0:T(8,128)(2,1)}, bf16[256,1024]{1,0:T(8,128)(2,1)}, u32[]{:S(2)}, u32[]{:S(2)}) collective-permute-start(bf16[256,1024]{1,0:T(8,128)(2,1)} %collective-permute-done.13.refs_25_.refs_20_.refs_21_), channel_id=1, source_target_pairs={{0,16},{8,24},{16,32},{24,40},{32,48},{40,56},{48,0},{56,8},{64,80... | collective-permute-start | bytes 1572872 | tf_op jit(solution)/shard_map/ppermute | solution.py:238
  122.7 13.7 %collective-permute-start.21 = (bf16[256,1024]{1,0:T(8,128)(2,1)}, bf16[256,1024]{1,0:T(8,128)(2,1)}, u32[]{:S(2)}, u32[]{:S(2)}) collective-permute-start(bf16[256,1024]{1,0:T(8,128)(2,1)} %collective-permute-done.14.refs_30_.refs_25_.refs_26_), channel_id=1, source_target_pairs={{0,48},{8,56},{16,0},{24,8},{32,16},{40,24},{48,32},{56,40},{64,11... | collective-permute-start | bytes 1572872 | tf_op jit(solution)/shard_map/ppermute | solution.py:238
  159.2 15.2 %collective-permute-start.39 = (bf16[256,1024]{1,0:T(8,128)(2,1)}, bf16[256,1024]{1,0:T(8,128)(2,1)}, u32[]{:S(2)}, u32[]{:S(2)}) collective-permute-start(bf16[256,1024]{1,0:T(8,128)(2,1)} %get-tuple-element.108.refs_0_), channel_id=1, source_target_pairs={{0,4},{1,5},{2,6},{3,7},{4,0},{5,1},{6,2},{7,3},{8,12},{9,13},{10,... | collective-permute-start | bytes 1572872 | tf_op jit(solution)/shard_map/ppermute | solution.py:247
  159.8 15.0 %collective-permute-start.36 = (bf16[256,1024]{1,0:T(8,128)(2,1)}, bf16[256,1024]{1,0:T(8,128)(2,1)S(1)}, u32[]{:S(2)}, u32[]{:S(2)}) collective-permute-start(bf16[256,1024]{1,0:T(8,128)(2,1)} %get-tuple-element.108.refs_0_), channel_id=1, source_target_pairs={{0,3},{1,0},{2,1},{3,2},{4,7},{5,4},{6,5},{7,6},{8,11},{9,8},{10,9... | collective-permute-start | bytes 1572872 | tf_op jit(solution)/shard_map/ppermute | solution.py:247
  161.5 14.8 %collective-permute-start.35 = (bf16[256,1024]{1,0:T(8,128)(2,1)}, bf16[256,1024]{1,0:T(8,128)(2,1)S(1)}, u32[]{:S(2)}, u32[]{:S(2)}) collective-permute-start(bf16[256,1024]{1,0:T(8,128)(2,1)} %get-tuple-element.108.refs_0_), channel_id=1, source_target_pairs={{0,1},{1,2},{2,3},{3,0},{4,5},{5,6},{6,7},{7,4},{8,9},{9,10},{10,1... | collective-permute-start | bytes 1572872 | tf_op jit(solution)/shard_map/ppermute | solution.py:247
  161.8 23.0 %collective-permute-start.40 = (bf16[256,1024]{1,0:T(8,128)(2,1)}, bf16[256,1024]{1,0:T(8,128)(2,1)}, u32[]{:S(2)}, u32[]{:S(2)}) collective-permute-start(bf16[256,1024]{1,0:T(8,128)(2,1)} %get-tuple-element.110.refs_4_), channel_id=1, source_target_pairs={{0,4},{1,5},{2,6},{3,7},{4,0},{5,1},{6,2},{7,3},{8,12},{9,13},{10,... | collective-permute-start | bytes 1572872 | tf_op jit(solution)/shard_map/ppermute | solution.py:247
  163.3 21.6 %collective-permute-start.38 = (bf16[256,1024]{1,0:T(8,128)(2,1)}, bf16[256,1024]{1,0:T(8,128)(2,1)S(1)}, u32[]{:S(2)}, u32[]{:S(2)}) collective-permute-start(bf16[256,1024]{1,0:T(8,128)(2,1)} %get-tuple-element.110.refs_4_), channel_id=1, source_target_pairs={{0,3},{1,0},{2,1},{3,2},{4,7},{5,4},{6,5},{7,6},{8,11},{9,8},{10,9... | collective-permute-start | bytes 1572872 | tf_op jit(solution)/shard_map/ppermute | solution.py:247
  174.4 13.8 %collective-permute-start.37 = (bf16[256,1024]{1,0:T(8,128)(2,1)}, bf16[256,1024]{1,0:T(8,128)(2,1)S(1)}, u32[]{:S(2)}, u32[]{:S(2)}) collective-permute-start(bf16[256,1024]{1,0:T(8,128)(2,1)} %get-tuple-element.110.refs_4_), channel_id=1, source_target_pairs={{0,1},{1,2},{2,3},{3,0},{4,5},{5,6},{6,7},{7,4},{8,9},{9,10},{10,1... | collective-permute-start | bytes 1572872 | tf_op jit(solution)/shard_map/ppermute | solution.py:247
  189.5 12.9 %collective-permute-start.41 = (bf16[256,1024]{1,0:T(8,128)(2,1)S(1)}, bf16[256,1024]{1,0:T(8,128)(2,1)S(1)}, u32[]{:S(2)}, u32[]{:S(2)}) collective-permute-start(bf16[256,1024]{1,0:T(8,128)(2,1)S(1)} %collective-permute-done.35.refs_1_), channel_id=1, source_target_pairs={{0,1},{1,2},{2,3},{3,0},{4,5},{5,6},{6,7},{7,4},{8,9},{9,10},{10,1... | collective-permute-start | bytes 1572872 | tf_op jit(solution)/shard_map/ppermute | solution.py:247
  191.0 26.2 %collective-permute-start.45 = (bf16[256,1024]{1,0:T(8,128)(2,1)S(1)}, bf16[256,1024]{1,0:T(8,128)(2,1)}, u32[]{:S(2)}, u32[]{:S(2)}) collective-permute-start(bf16[256,1024]{1,0:T(8,128)(2,1)S(1)} %collective-permute-done.35.refs_1_), channel_id=1, source_target_pairs={{0,4},{1,5},{2,6},{3,7},{4,0},{5,1},{6,2},{7,3},{8,12},{9,13},{10,... | collective-permute-start | bytes 1572872 | tf_op jit(solution)/shard_map/ppermute | solution.py:247
  192.0 25.2 %collective-permute-start.46 = (bf16[256,1024]{1,0:T(8,128)(2,1)S(1)}, bf16[256,1024]{1,0:T(8,128)(2,1)}, u32[]{:S(2)}, u32[]{:S(2)}) collective-permute-start(bf16[256,1024]{1,0:T(8,128)(2,1)S(1)} %collective-permute-done.36.refs_2_), channel_id=1, source_target_pairs={{0,4},{1,5},{2,6},{3,7},{4,0},{5,1},{6,2},{7,3},{8,12},{9,13},{10,... | collective-permute-start | bytes 1572872 | tf_op jit(solution)/shard_map/ppermute | solution.py:247
  202.4 14.8 %collective-permute-start.44 = (bf16[256,1024]{1,0:T(8,128)(2,1)}, bf16[256,1024]{1,0:T(8,128)(2,1)S(1)}, u32[]{:S(2)}, u32[]{:S(2)}) collective-permute-start(bf16[256,1024]{1,0:T(8,128)(2,1)} %collective-permute-done.40.refs_4_), channel_id=1, source_target_pairs={{0,3},{1,0},{2,1},{3,2},{4,7},{5,4},{6,5},{7,6},{8,11},{9,8},{10,9... | collective-permute-start | bytes 1572872 | tf_op jit(solution)/shard_map/ppermute | solution.py:247
  203.5 13.7 %collective-permute-start.43 = (bf16[256,1024]{1,0:T(8,128)(2,1)}, bf16[256,1024]{1,0:T(8,128)(2,1)S(1)}, u32[]{:S(2)}, u32[]{:S(2)}) collective-permute-start(bf16[256,1024]{1,0:T(8,128)(2,1)} %collective-permute-done.40.refs_4_), channel_id=1, source_target_pairs={{0,1},{1,2},{2,3},{3,0},{4,5},{5,6},{6,7},{7,4},{8,9},{9,10},{10,1... | collective-permute-start | bytes 1572872 | tf_op jit(solution)/shard_map/ppermute | solution.py:247
  205.1 19.4 %collective-permute-start.47 = (bf16[256,1024]{1,0:T(8,128)(2,1)S(1)}, bf16[256,1024]{1,0:T(8,128)(2,1)}, u32[]{:S(2)}, u32[]{:S(2)}) collective-permute-start(bf16[256,1024]{1,0:T(8,128)(2,1)S(1)} %collective-permute-done.41.refs_3_), channel_id=1, source_target_pairs={{0,4},{1,5},{2,6},{3,7},{4,0},{5,1},{6,2},{7,3},{8,12},{9,13},{10,... | collective-permute-start | bytes 1572872 | tf_op jit(solution)/shard_map/ppermute | solution.py:247
  (58 other events, 968.6 us)

commit v3 on v2

--- a/solution.py
+++ b/solution.py
@@ -365,10 +365,10 @@
     h1, h2 = product(lefts, chunks, core, [half, half], factor, kind, "square")
     h2_z, h1_z = z_swap(h2), z_swap(h1)
     h1_near, h2_near = near(h1, x_shift), near(h2, x_shift)
-    h1_near, h2_near, h1_z, h2_z, h1, h2 = after((h1_near, h2_near, h1_z, h2_z, h1, h2))
+    h1_near, h2_near, h1, h2 = after((h1_near, h2_near, h1, h2))
     h1_far, h2_far = x_shift(h1_near[0], 1), x_shift(h2_near[1], -1)
     h1_z_near = [z_swap(v) for v in h1_near]
-    h1_far, h2_far, h2_z = after((h1_far, h2_far, h2_z))
+    h1_far, h2_far, h1_z, h2_z = after((h1_far, h2_far, h1_z, h2_z))
     h2_z_near = near(h2_z, x_shift)
     h1_z_far = z_swap(h1_far)
     lefts = both(0, (h1, h1_near, [h1_far]), (h2, h2_near, [h2_far]))

time: 238 us -> 238 us (level)
    unnamed x80 -> x82, local copies, waits for them, and re-layouts: 6.62 us -> 6.61 us
  transfers between devices with their start and end apart: 50 -> 50, of which waited for: 32 -> 30; matrix products, arithmetic and copies ran while one was open for 1% -> 1% of each run, Pallas kernels for 4% -> 4%
where the time goes in v3:
time: 238 us
  waiting for transfers between devices  115 us (48%)
  starting transfers between devices  46.8 us (20%)
  Pallas kernels  38.5 us (16%)
  blocking collectives  26.4 us (11%)
  local copies, waits for them, and re-layouts  9.48 us (4%)
    ppermute x27, waiting for transfers between devices, over_col(): return lax.ppermute(value, 'col', pairs)  69.4 us
    ppermute x23, waiting for transfers between devices, over_row(): return lax.ppermute(value, 'row', pairs)  46 us
    pallas_call x3, Pallas kernels, product(): pl.pallas_call(functools.partial(product_kernel, factor, left_parts, righ...  35.7 us
    ppermute x27, starting transfers between devices, over_col(): return lax.ppermute(value, 'col', pairs)  29.3 us
    all_to_all x1, blocking collectives, local_tile(): received = lax.all_to_all(send, 'row', 0, 0, tiled=True)  26.4 us
    ppermute x23, starting transfers between devices, over_row(): return lax.ppermute(value, 'row', pairs)  17.5 us
    unnamed x82, local copies, waits for them, and re-layouts  6.61 us
  transfers between devices with their start and end apart: 50, of which 30 were waited for; matrix products, arithmetic and copies ran while one was open for 1% of the time, Pallas kernels for 4%

profile of v3, /device:TPU:0, one launch (start us, length us, event | category | flops | bytes accessed | tf_op | source)
XLA Modules:
  0.0 237.7 jit_solution(5938867391090539781)
XLA Ops:
  4.6 26.4 %all_to_all.5.received = bf16[16,272,128]{2,1,0:T(8,128)(2,1)S(1)} all-to-all(bf16[16,272,128]{2,1,0:T(8,128)(2,1)S(1)} %pack.1), channel_id=1, replica_groups=mesh['row'=16,'col'=8] {'row'}, dimensions={0} | all-to-all | bytes 2228224 | tf_op jit(solution)/shard_map/all_to_all | solution.py:83
  34.5 2.8 %collective-permute-start.2 = (bf16[512,1024]{1,0:T(8,128)(2,1)S(1)}, bf16[512,1024]{1,0:T(8,128)(2,1)S(1)}, u32[]{:S(2)}, u32[]{:S(2)}) collective-permute-start(bf16[512,1024]{1,0:T(8,128)(2,1)S(1)} %unpack.1.refs_0_.refs_13_.refs_8_.refs_9_.refs_34_), channel_id=1, source_target_pairs={{0,3},{1,0},{2,1},{3,2},{4,7},{5,4},{6,5},{7,6},{8,11},{9,8},{10,9... | collective-permute-start | bytes 3145736 | tf_op jit(solution)/shard_map/ppermute | solution.py:247
  38.0 19.7 %collective-permute-done.4.refs_17_.refs_12_.refs_13_ = bf16[512,1024]{1,0:T(8,128)(2,1)S(1)} collective-permute-done((bf16[512,1024]{1,0:T(8,128)(2,1)S(1)}, bf16[512,1024]{1,0:T(8,128)(2,1)S(1)}, u32[]{:S(2)}, u32[]{:S(2)}) %collective-permute-start.4) | collective-permute-done | bytes 1048608 | tf_op jit(solution)/shard_map/ppermute | solution.py:238
  57.6 2.1 collective-permute-done.3.refs_15_.refs_10_.refs_11_
  59.8 3.0 %collective-permute-done.1.refs_1_ = bf16[512,1024]{1,0:T(8,128)(2,1)S(1)} collective-permute-done((bf16[512,1024]{1,0:T(8,128)(2,1)S(1)}, bf16[512,1024]{1,0:T(8,128)(2,1)S(1)}, u32[]{:S(2)}, u32[]{:S(2)}) %collective-permute-start.1) | collective-permute-done | bytes 1048608 | tf_op jit(solution)/shard_map/ppermute | solution.py:247
  63.8 2.5 %collective-permute-start.9 = (bf16[256,1024]{1,0:T(8,128)(2,1)S(1)}, bf16[256,1024]{1,0:T(8,128)(2,1)S(1)}, u32[]{:S(2)}, u32[]{:S(2)}) collective-permute-start(bf16[256,1024]{1,0:T(8,128)(2,1)S(1)} %slice.35), channel_id=1, source_target_pairs={{0,48},{8,56},{16,0},{24,8},{32,16},{40,24},{48,32},{56,40},{64,11... | collective-permute-start | bytes 1572872 | tf_op jit(solution)/shard_map/ppermute | solution.py:238
  66.3 2.5 %collective-permute-start.7 = (bf16[256,1024]{1,0:T(8,128)(2,1)S(1)}, bf16[256,1024]{1,0:T(8,128)(2,1)S(1)}, u32[]{:S(2)}, u32[]{:S(2)}) collective-permute-start(bf16[256,1024]{1,0:T(8,128)(2,1)S(1)} %slice.33), channel_id=1, source_target_pairs={{0,3},{1,0},{2,1},{3,2},{4,7},{5,4},{6,5},{7,6},{8,11},{9,8},{10,9... | collective-permute-start | bytes 1572872 | tf_op jit(solution)/shard_map/ppermute | solution.py:247
  69.8 6.4 %collective-permute-done.9.refs_20_.refs_15_.refs_16_ = bf16[256,1024]{1,0:T(8,128)(2,1)S(1)} collective-permute-done((bf16[256,1024]{1,0:T(8,128)(2,1)S(1)}, bf16[256,1024]{1,0:T(8,128)(2,1)S(1)}, u32[]{:S(2)}, u32[]{:S(2)}) %collective-permute-start.9) | collective-permute-done | bytes 524320 | tf_op jit(solution)/shard_map/ppermute | solution.py:238
  76.1 3.4 %collective-permute-done.8.refs_19_.refs_14_.refs_15_ = bf16[256,1024]{1,0:T(8,128)(2,1)S(1)} collective-permute-done((bf16[256,1024]{1,0:T(8,128)(2,1)S(1)}, bf16[256,1024]{1,0:T(8,128)(2,1)S(1)}, u32[]{:S(2)}, u32[]{:S(2)}) %collective-permute-start.8) | collective-permute-done | bytes 524320 | tf_op jit(solution)/shard_map/ppermute | solution.py:238
  79.5 2.0 collective-permute-done.6.refs_3_
  84.5 3.0 %collective-permute-start.14 = (bf16[256,1024]{1,0:T(8,128)(2,1)S(1)}, bf16[256,1024]{1,0:T(8,128)(2,1)}, u32[]{:S(2)}, u32[]{:S(2)}) collective-permute-start(bf16[256,1024]{1,0:T(8,128)(2,1)S(1)} %get-tuple-element.82), channel_id=1, source_target_pairs={{0,48},{8,56},{16,0},{24,8},{32,16},{40,24},{48,32},{56,40},{64,11... | collective-permute-start | bytes 1572872 | tf_op jit(solution)/shard_map/ppermute | solution.py:238
  87.5 6.1 %collective-permute-done.10.refs_9_ = bf16[256,1024]{1,0:T(8,128)(2,1)S(1)} collective-permute-done((bf16[256,1024]{1,0:T(8,128)(2,1)S(1)}, bf16[256,1024]{1,0:T(8,128)(2,1)S(1)}, u32[]{:S(2)}, u32[]{:S(2)}) %collective-permute-start.10) | collective-permute-done | bytes 524320 | tf_op jit(solution)/shard_map/ppermute | solution.py:247
  94.5 5.3 %collective-permute-done.13.refs_25_.refs_20_.refs_21_ = bf16[256,1024]{1,0:T(8,128)(2,1)} collective-permute-done((bf16[256,1024]{1,0:T(8,128)(2,1)S(1)}, bf16[256,1024]{1,0:T(8,128)(2,1)}, u32[]{:S(2)}, u32[]{:S(2)}) %collective-permute-start.13) | collective-permute-done | bytes 524320 | tf_op jit(solution)/shard_map/ppermute | solution.py:238
  99.8 3.2 %collective-permute-start.17 = (bf16[256,1024]{1,0:T(8,128)(2,1)S(1)}, bf16[256,1024]{1,0:T(8,128)(2,1)S(1)}, u32[]{:S(2)}, u32[]{:S(2)}) collective-permute-start(bf16[256,1024]{1,0:T(8,128)(2,1)S(1)} %get-tuple-element.83), channel_id=1, source_target_pairs={{0,48},{8,56},{16,0},{24,8},{32,16},{40,24},{48,32},{56,40},{64,11... | collective-permute-start | bytes 1572872 | tf_op jit(solution)/shard_map/ppermute | solution.py:238
  103.6 3.2 %collective-permute-start.19 = (bf16[256,1024]{1,0:T(8,128)(2,1)S(1)}, bf16[256,1024]{1,0:T(8,128)(2,1)S(1)}, u32[]{:S(2)}, u32[]{:S(2)}) collective-permute-start(bf16[256,1024]{1,0:T(8,128)(2,1)S(1)} %collective-permute-done.10.refs_9_), channel_id=1, source_target_pairs={{0,3},{1,0},{2,1},{3,2},{4,7},{5,4},{6,5},{7,6},{8,11},{9,8},{10,9... | collective-permute-start | bytes 1572872 | tf_op jit(solution)/shard_map/ppermute | solution.py:247
  106.7 3.5 %collective-permute-done.16.refs_26_.refs_21_.refs_22_ = bf16[256,1024]{1,0:T(8,128)(2,1)S(1)} collective-permute-done((bf16[256,1024]{1,0:T(8,128)(2,1)S(1)}, bf16[256,1024]{1,0:T(8,128)(2,1)S(1)}, u32[]{:S(2)}, u32[]{:S(2)}) %collective-permute-start.16) | collective-permute-done | bytes 524320 | tf_op jit(solution)/shard_map/ppermute | solution.py:238
  110.3 7.8 %collective-permute-done.19.refs_11_ = bf16[256,1024]{1,0:T(8,128)(2,1)S(1)} collective-permute-done((bf16[256,1024]{1,0:T(8,128)(2,1)S(1)}, bf16[256,1024]{1,0:T(8,128)(2,1)S(1)}, u32[]{:S(2)}, u32[]{:S(2)}) %collective-permute-start.19) | collective-permute-done | bytes 524320 | tf_op jit(solution)/shard_map/ppermute | solution.py:247
  118.2 3.4 %collective-permute-done.18.refs_10_ = bf16[256,1024]{1,0:T(8,128)(2,1)S(1)} collective-permute-done((bf16[256,1024]{1,0:T(8,128)(2,1)S(1)}, bf16[256,1024]{1,0:T(8,128)(2,1)S(1)}, u32[]{:S(2)}, u32[]{:S(2)}) %collective-permute-start.18) | collective-permute-done | bytes 524320 | tf_op jit(solution)/shard_map/ppermute | solution.py:247
  122.6 3.2 %collective-permute-start.21 = (bf16[256,1024]{1,0:T(8,128)(2,1)}, bf16[256,1024]{1,0:T(8,128)(2,1)}, u32[]{:S(2)}, u32[]{:S(2)}) collective-permute-start(bf16[256,1024]{1,0:T(8,128)(2,1)} %collective-permute-done.14.refs_30_.refs_25_.refs_26_), channel_id=1, source_target_pairs={{0,48},{8,56},{16,0},{24,8},{32,16},{40,24},{48,32},{56,40},{64,11... | collective-permute-start | bytes 1572872 | tf_op jit(solution)/shard_map/ppermute | solution.py:238
  125.8 7.4 %collective-permute-done.15.refs_8_ = bf16[256,1024]{1,0:T(8,128)(2,1)S(1)} collective-permute-done((bf16[256,1024]{1,0:T(8,128)(2,1)S(1)}, bf16[256,1024]{1,0:T(8,128)(2,1)S(1)}, u32[]{:S(2)}, u32[]{:S(2)}) %collective-permute-start.15) | collective-permute-done | bytes 524320 | tf_op jit(solution)/shard_map/ppermute | solution.py:247
  133.7 2.6 %collective-permute-done.20.refs_33_.refs_28_.refs_29_ = bf16[256,1024]{1,0:T(8,128)(2,1)} collective-permute-done((bf16[256,1024]{1,0:T(8,128)(2,1)}, bf16[256,1024]{1,0:T(8,128)(2,1)}, u32[]{:S(2)}, u32[]{:S(2)}) %collective-permute-start.20) | collective-permute-done | bytes 524320 | tf_op jit(solution)/shard_map/ppermute | solution.py:238
  144.0 15.1 %square.1 = (bf16[256,1024]{1,0:T(8,128)(2,1)}, bf16[256,1024]{1,0:T(8,128)(2,1)}) custom-call(s32[13]{0:T(128)} %stack.58.left_at, s32[8]{0:T(128)} %stack.53.right_at, s32[1]{0:T(128)} %bitcast.12.core, s32[1]{0:T(128)} %constant.244.clone.1.want, bf16[512,1024]{1,0:T(8,128)(2,1)} %copy-done, bf16[512,1024]{1,0:T(8,128)(2,1)} %copy-done.29, ...), custom_call_target="tpu_custom_call" | custom-call | flops 8589934592 | bytes 25165824 | tf_op jit(solution)/shard_map/square/pallas_call | solution.py:199
  161.2 3.0 %collective-permute-start.38 = (bf16[256,1024]{1,0:T(8,128)(2,1)}, bf16[256,1024]{1,0:T(8,128)(2,1)S(1)}, u32[]{:S(2)}, u32[]{:S(2)}) collective-permute-start(bf16[256,1024]{1,0:T(8,128)(2,1)} %get-tuple-element.108.refs_4_), channel_id=1, source_target_pairs={{0,3},{1,0},{2,1},{3,2},{4,7},{5,4},{6,5},{7,6},{8,11},{9,8},{10,9... | collective-permute-start | bytes 1572872 | tf_op jit(solution)/shard_map/ppermute | solution.py:247
  165.0 9.1 %collective-permute-done.36.refs_2_ = bf16[256,1024]{1,0:T(8,128)(2,1)S(1)} collective-permute-done((bf16[256,1024]{1,0:T(8,128)(2,1)}, bf16[256,1024]{1,0:T(8,128)(2,1)S(1)}, u32[]{:S(2)}, u32[]{:S(2)}) %collective-permute-start.36) | collective-permute-done | bytes 524320 | tf_op jit(solution)/shard_map/ppermute | solution.py:247
  175.1 2.0 collective-permute-done.35.refs_1_
  177.1 7.4 %collective-permute-done.38.refs_6_ = bf16[256,1024]{1,0:T(8,128)(2,1)S(1)} collective-permute-done((bf16[256,1024]{1,0:T(8,128)(2,1)}, bf16[256,1024]{1,0:T(8,128)(2,1)S(1)}, u32[]{:S(2)}, u32[]{:S(2)}) %collective-permute-start.38) | collective-permute-done | bytes 524320 | tf_op jit(solution)/shard_map/ppermute | solution.py:247
  184.5 2.7 %collective-permute-done.37.refs_5_ = bf16[256,1024]{1,0:T(8,128)(2,1)S(1)} collective-permute-done((bf16[256,1024]{1,0:T(8,128)(2,1)}, bf16[256,1024]{1,0:T(8,128)(2,1)S(1)}, u32[]{:S(2)}, u32[]{:S(2)}) %collective-permute-start.37) | collective-permute-done | bytes 524320 | tf_op jit(solution)/shard_map/ppermute | solution.py:247
  192.1 8.8 %collective-permute-done.40.refs_7_ = bf16[256,1024]{1,0:T(8,128)(2,1)S(1)} collective-permute-done((bf16[256,1024]{1,0:T(8,128)(2,1)S(1)}, bf16[256,1024]{1,0:T(8,128)(2,1)S(1)}, u32[]{:S(2)}, u32[]{:S(2)}) %collective-permute-start.40) | collective-permute-done | bytes 524320 | tf_op jit(solution)/shard_map/ppermute | solution.py:247
  206.1 10.1 %step_first.1.refs_33_ = f32[512,1024]{1,0:T(8,128)} custom-call(s32[8]{0:T(128)} %stack.59.left_at, s32[8]{0:T(128)} %stack.53.right_at, s32[1]{0:T(128)} %bitcast.12.core, s32[1]{0:T(128)} %bitcast.20.want, bf16[256,1024]{1,0:T(8,128)(2,1)} %get-tuple-element.106.refs_0_, bf16[256,1024]{1,0:T(8,128)(2,1)} %copy-done.22, bf16[256,1024]{1,0:T(8,128)(2,1)} %copy-done.21, ...), custom_call_target="tpu_custom_call" | custom-call | flops 4294967296 | bytes 12582912 | tf_op jit(solution)/shard_map/step_first/pallas_call | solution.py:199
  216.9 1.8 collective-permute-start.49
  219.6 5.3 %collective-permute-done.47.refs_3_ = bf16[256,1024]{1,0:T(8,128)(2,1)} collective-permute-done((bf16[256,1024]{1,0:T(8,128)(2,1)S(1)}, bf16[256,1024]{1,0:T(8,128)(2,1)}, u32[]{:S(2)}, u32[]{:S(2)}) %collective-permute-start.47) | collective-permute-done | bytes 524320 | tf_op jit(solution)/shard_map/ppermute | solution.py:247
  227.0 10.6 %step_last.1 = f32[512,1024]{1,0:T(8,128)} custom-call(s32[9]{0:T(128)} %stack.44.left_at, s32[8]{0:T(128)} %stack.53.right_at, s32[1]{0:T(128)} %bitcast.12.core, s32[1]{0:T(128)} %bitcast.13.want, bf16[256,1024]{1,0:T(8,128)(2,1)} %copy-done.27, bf16[256,1024]{1,0:T(8,128)(2,1)} %collective-permute-done.45.refs_1_, ...), custom_call_target="tpu_custom_call" | custom-call | flops 4294967296 | bytes 12582912 | tf_op jit(solution)/shard_map/step_last/pallas_call | solution.py:199
  (168 shorter events, 41.3 us)
Async XLA Ops:
  32.4 25.3 %collective-permute-start.4 = (bf16[512,1024]{1,0:T(8,128)(2,1)S(1)}, bf16[512,1024]{1,0:T(8,128)(2,1)S(1)}, u32[]{:S(2)}, u32[]{:S(2)}) collective-permute-start(bf16[512,1024]{1,0:T(8,128)(2,1)S(1)} %unpack.1.refs_0_.refs_13_.refs_8_.refs_9_.refs_34_), channel_id=1, source_target_pairs={{0,48},{8,56},{16,0},{24,8},{32,16},{40,24},{48,32},{56,40},{64,11... | collective-permute-start | bytes 3145736 | tf_op jit(solution)/shard_map/ppermute | solution.py:238
  33.7 26.1 %collective-permute-start.3 = (bf16[512,1024]{1,0:T(8,128)(2,1)S(1)}, bf16[512,1024]{1,0:T(8,128)(2,1)S(1)}, u32[]{:S(2)}, u32[]{:S(2)}) collective-permute-start(bf16[512,1024]{1,0:T(8,128)(2,1)S(1)} %unpack.1.refs_0_.refs_13_.refs_8_.refs_9_.refs_34_), channel_id=1, source_target_pairs={{0,16},{8,24},{16,32},{24,40},{32,48},{40,56},{48,0},{56,8},{64,80... | collective-permute-start | bytes 3145736 | tf_op jit(solution)/shard_map/ppermute | solution.py:238
  34.5 25.3 %collective-permute-start.2 = (bf16[512,1024]{1,0:T(8,128)(2,1)S(1)}, bf16[512,1024]{1,0:T(8,128)(2,1)S(1)}, u32[]{:S(2)}, u32[]{:S(2)}) collective-permute-start(bf16[512,1024]{1,0:T(8,128)(2,1)S(1)} %unpack.1.refs_0_.refs_13_.refs_8_.refs_9_.refs_34_), channel_id=1, source_target_pairs={{0,3},{1,0},{2,1},{3,2},{4,7},{5,4},{6,5},{7,6},{8,11},{9,8},{10,9... | collective-permute-start | bytes 3145736 | tf_op jit(solution)/shard_map/ppermute | solution.py:247
  37.2 25.6 %collective-permute-start.1 = (bf16[512,1024]{1,0:T(8,128)(2,1)S(1)}, bf16[512,1024]{1,0:T(8,128)(2,1)S(1)}, u32[]{:S(2)}, u32[]{:S(2)}) collective-permute-start(bf16[512,1024]{1,0:T(8,128)(2,1)S(1)} %unpack.1.refs_0_.refs_13_.refs_8_.refs_9_.refs_34_), channel_id=1, source_target_pairs={{0,1},{1,2},{2,3},{3,0},{4,5},{5,6},{6,7},{7,4},{8,9},{9,10},{10,1... | collective-permute-start | bytes 3145736 | tf_op jit(solution)/shard_map/ppermute | solution.py:247
  37.2 25.9 %collective-permute-start = (bf16[512,1024]{1,0:T(8,128)(2,1)S(1)}, bf16[512,1024]{1,0:T(8,128)(2,1)S(1)}, u32[]{:S(2)}, u32[]{:S(2)}) collective-permute-start(bf16[512,1024]{1,0:T(8,128)(2,1)S(1)} %unpack.1.refs_0_.refs_13_.refs_8_.refs_9_.refs_34_), channel_id=1, source_target_pairs={{0,64},{8,72},{16,80},{24,88},{32,96},{40,104},{48,112},{56,120},{... | collective-permute-start | bytes 3145736 | tf_op jit(solution)/shard_map/ppermute | solution.py:238
  63.8 12.4 %collective-permute-start.9 = (bf16[256,1024]{1,0:T(8,128)(2,1)S(1)}, bf16[256,1024]{1,0:T(8,128)(2,1)S(1)}, u32[]{:S(2)}, u32[]{:S(2)}) collective-permute-start(bf16[256,1024]{1,0:T(8,128)(2,1)S(1)} %slice.35), channel_id=1, source_target_pairs={{0,48},{8,56},{16,0},{24,8},{32,16},{40,24},{48,32},{56,40},{64,11... | collective-permute-start | bytes 1572872 | tf_op jit(solution)/shard_map/ppermute | solution.py:238
  66.3 13.2 %collective-permute-start.8 = (bf16[256,1024]{1,0:T(8,128)(2,1)S(1)}, bf16[256,1024]{1,0:T(8,128)(2,1)S(1)}, u32[]{:S(2)}, u32[]{:S(2)}) collective-permute-start(bf16[256,1024]{1,0:T(8,128)(2,1)S(1)} %slice.34), channel_id=1, source_target_pairs={{0,16},{8,24},{16,32},{24,40},{32,48},{40,56},{48,0},{56,8},{64,80... | collective-permute-start | bytes 1572872 | tf_op jit(solution)/shard_map/ppermute | solution.py:238
  66.3 13.2 %collective-permute-start.7 = (bf16[256,1024]{1,0:T(8,128)(2,1)S(1)}, bf16[256,1024]{1,0:T(8,128)(2,1)S(1)}, u32[]{:S(2)}, u32[]{:S(2)}) collective-permute-start(bf16[256,1024]{1,0:T(8,128)(2,1)S(1)} %slice.33), channel_id=1, source_target_pairs={{0,3},{1,0},{2,1},{3,2},{4,7},{5,4},{6,5},{7,6},{8,11},{9,8},{10,9... | collective-permute-start | bytes 1572872 | tf_op jit(solution)/shard_map/ppermute | solution.py:247
  68.8 12.7 %collective-permute-start.6 = (bf16[256,1024]{1,0:T(8,128)(2,1)S(1)}, bf16[256,1024]{1,0:T(8,128)(2,1)S(1)}, u32[]{:S(2)}, u32[]{:S(2)}) collective-permute-start(bf16[256,1024]{1,0:T(8,128)(2,1)S(1)} %slice.32), channel_id=1, source_target_pairs={{0,1},{1,2},{2,3},{3,0},{4,5},{5,6},{6,7},{7,4},{8,9},{9,10},{10,1... | collective-permute-start | bytes 1572872 | tf_op jit(solution)/shard_map/ppermute | solution.py:247
  68.8 12.7 %collective-permute-start.5 = (bf16[256,1024]{1,0:T(8,128)(2,1)S(1)}, bf16[256,1024]{1,0:T(8,128)(2,1)S(1)}, u32[]{:S(2)}, u32[]{:S(2)}) collective-permute-start(bf16[256,1024]{1,0:T(8,128)(2,1)S(1)} %get-tuple-element.68), channel_id=1, source_target_pairs={{0,4},{1,5},{2,6},{3,7},{4,0},{5,1},{6,2},{7,3},{8,12},{9,13},{10,... | collective-permute-start | bytes 1572872 | tf_op jit(solution)/shard_map/ppermute | solution.py:247
  81.5 12.1 %collective-permute-start.12 = (bf16[256,1024]{1,0:T(8,128)(2,1)S(1)}, bf16[256,1024]{1,0:T(8,128)(2,1)S(1)}, u32[]{:S(2)}, u32[]{:S(2)}) collective-permute-start(bf16[256,1024]{1,0:T(8,128)(2,1)S(1)} %collective-permute-done.5.refs_5_), channel_id=1, source_target_pairs={{0,3},{1,0},{2,1},{3,2},{4,7},{5,4},{6,5},{7,6},{8,11},{9,8},{10,9... | collective-permute-start | bytes 1572872 | tf_op jit(solution)/shard_map/ppermute | solution.py:247
  87.5 12.3 %collective-permute-start.13 = (bf16[256,1024]{1,0:T(8,128)(2,1)S(1)}, bf16[256,1024]{1,0:T(8,128)(2,1)}, u32[]{:S(2)}, u32[]{:S(2)}) collective-permute-start(bf16[256,1024]{1,0:T(8,128)(2,1)S(1)} %get-tuple-element.83), channel_id=1, source_target_pairs={{0,16},{8,24},{16,32},{24,40},{32,48},{40,56},{48,0},{56,8},{64,80... | collective-permute-start | bytes 1572872 | tf_op jit(solution)/shard_map/ppermute | solution.py:238
  103.0 19.5 %collective-permute-start.23 = (bf16[512,1024]{1,0:T(8,128)(2,1)S(1)}, bf16[512,1024]{1,0:T(8,128)(2,1)S(1)}, u32[]{:S(2)}, u32[]{:S(2)}) collective-permute-start(bf16[512,1024]{1,0:T(8,128)(2,1)S(1)} %unpack.1.refs_0_.refs_13_.refs_8_.refs_9_.refs_34_), channel_id=1, source_target_pairs={{0,8},{8,0},{16,24},{24,16},{32,40},{40,32},{48,56},{56,48},{64,72... | collective-permute-start | bytes 3145736 | tf_op jit(solution)/shard_map/ppermute | solution.py:238
  103.0 19.5 %collective-permute-start.24 = (bf16[512,1024]{1,0:T(8,128)(2,1)S(1)}, bf16[512,1024]{1,0:T(8,128)(2,1)S(1)}, u32[]{:S(2)}, u32[]{:S(2)}) collective-permute-start(bf16[512,1024]{1,0:T(8,128)(2,1)S(1)} %collective-permute-done.3.refs_15_.refs_10_.refs_11_), channel_id=1, source_target_pairs={{0,8},{8,0},{16,24},{24,16},{32,40},{40,32},{48,56},{56,48},{64,72... | collective-permute-start | bytes 3145736 | tf_op jit(solution)/shard_map/ppermute | solution.py:238
  103.6 14.6 %collective-permute-start.19 = (bf16[256,1024]{1,0:T(8,128)(2,1)S(1)}, bf16[256,1024]{1,0:T(8,128)(2,1)S(1)}, u32[]{:S(2)}, u32[]{:S(2)}) collective-permute-start(bf16[256,1024]{1,0:T(8,128)(2,1)S(1)} %collective-permute-done.10.refs_9_), channel_id=1, source_target_pairs={{0,3},{1,0},{2,1},{3,2},{4,7},{5,4},{6,5},{7,6},{8,11},{9,8},{10,9... | collective-permute-start | bytes 1572872 | tf_op jit(solution)/shard_map/ppermute | solution.py:247
  110.2 15.6 %collective-permute-start.25 = (bf16[512,1024]{1,0:T(8,128)(2,1)S(1)}, bf16[512,1024]{1,0:T(8,128)(2,1)S(1)}, u32[]{:S(2)}, u32[]{:S(2)}) collective-permute-start(bf16[512,1024]{1,0:T(8,128)(2,1)S(1)} %collective-permute-done.4.refs_17_.refs_12_.refs_13_), channel_id=1, source_target_pairs={{0,8},{8,0},{16,24},{24,16},{32,40},{40,32},{48,56},{56,48},{64,72... | collective-permute-start | bytes 3145736 | tf_op jit(solution)/shard_map/ppermute | solution.py:238
  118.2 15.0 %collective-permute-start.15 = (bf16[256,1024]{1,0:T(8,128)(2,1)S(1)}, bf16[256,1024]{1,0:T(8,128)(2,1)S(1)}, u32[]{:S(2)}, u32[]{:S(2)}) collective-permute-start(bf16[256,1024]{1,0:T(8,128)(2,1)S(1)} %collective-permute-done.11.refs_6_), channel_id=1, source_target_pairs={{0,1},{1,2},{2,3},{3,0},{4,5},{5,6},{6,7},{7,4},{8,9},{9,10},{10,1... | collective-permute-start | bytes 1572872 | tf_op jit(solution)/shard_map/ppermute | solution.py:247
  122.5 13.7 %collective-permute-start.20 = (bf16[256,1024]{1,0:T(8,128)(2,1)}, bf16[256,1024]{1,0:T(8,128)(2,1)}, u32[]{:S(2)}, u32[]{:S(2)}) collective-permute-start(bf16[256,1024]{1,0:T(8,128)(2,1)} %collective-permute-done.13.refs_25_.refs_20_.refs_21_), channel_id=1, source_target_pairs={{0,16},{8,24},{16,32},{24,40},{32,48},{40,56},{48,0},{56,8},{64,80... | collective-permute-start | bytes 1572872 | tf_op jit(solution)/shard_map/ppermute | solution.py:238
  122.6 13.7 %collective-permute-start.21 = (bf16[256,1024]{1,0:T(8,128)(2,1)}, bf16[256,1024]{1,0:T(8,128)(2,1)}, u32[]{:S(2)}, u32[]{:S(2)}) collective-permute-start(bf16[256,1024]{1,0:T(8,128)(2,1)} %collective-permute-done.14.refs_30_.refs_25_.refs_26_), channel_id=1, source_target_pairs={{0,48},{8,56},{16,0},{24,8},{32,16},{40,24},{48,32},{56,40},{64,11... | collective-permute-start | bytes 1572872 | tf_op jit(solution)/shard_map/ppermute | solution.py:238
  159.1 15.0 %collective-permute-start.36 = (bf16[256,1024]{1,0:T(8,128)(2,1)}, bf16[256,1024]{1,0:T(8,128)(2,1)S(1)}, u32[]{:S(2)}, u32[]{:S(2)}) collective-permute-start(bf16[256,1024]{1,0:T(8,128)(2,1)} %get-tuple-element.106.refs_0_), channel_id=1, source_target_pairs={{0,3},{1,0},{2,1},{3,2},{4,7},{5,4},{6,5},{7,6},{8,11},{9,8},{10,9... | collective-permute-start | bytes 1572872 | tf_op jit(solution)/shard_map/ppermute | solution.py:247
  160.9 16.2 %collective-permute-start.35 = (bf16[256,1024]{1,0:T(8,128)(2,1)}, bf16[256,1024]{1,0:T(8,128)(2,1)S(1)}, u32[]{:S(2)}, u32[]{:S(2)}) collective-permute-start(bf16[256,1024]{1,0:T(8,128)(2,1)} %get-tuple-element.106.refs_0_), channel_id=1, source_target_pairs={{0,1},{1,2},{2,3},{3,0},{4,5},{5,6},{6,7},{7,4},{8,9},{9,10},{10,1... | collective-permute-start | bytes 1572872 | tf_op jit(solution)/shard_map/ppermute | solution.py:247
  161.2 23.4 %collective-permute-start.38 = (bf16[256,1024]{1,0:T(8,128)(2,1)}, bf16[256,1024]{1,0:T(8,128)(2,1)S(1)}, u32[]{:S(2)}, u32[]{:S(2)}) collective-permute-start(bf16[256,1024]{1,0:T(8,128)(2,1)} %get-tuple-element.108.refs_4_), channel_id=1, source_target_pairs={{0,3},{1,0},{2,1},{3,2},{4,7},{5,4},{6,5},{7,6},{8,11},{9,8},{10,9... | collective-permute-start | bytes 1572872 | tf_op jit(solution)/shard_map/ppermute | solution.py:247
  164.1 23.1 %collective-permute-start.37 = (bf16[256,1024]{1,0:T(8,128)(2,1)}, bf16[256,1024]{1,0:T(8,128)(2,1)S(1)}, u32[]{:S(2)}, u32[]{:S(2)}) collective-permute-start(bf16[256,1024]{1,0:T(8,128)(2,1)} %get-tuple-element.108.refs_4_), channel_id=1, source_target_pairs={{0,1},{1,2},{2,3},{3,0},{4,5},{5,6},{6,7},{7,4},{8,9},{9,10},{10,1... | collective-permute-start | bytes 1572872 | tf_op jit(solution)/shard_map/ppermute | solution.py:247
  164.1 26.9 %collective-permute-start.41 = (bf16[256,1024]{1,0:T(8,128)(2,1)}, bf16[256,1024]{1,0:T(8,128)(2,1)S(1)}, u32[]{:S(2)}, u32[]{:S(2)}) collective-permute-start(bf16[256,1024]{1,0:T(8,128)(2,1)} %get-tuple-element.106.refs_0_), channel_id=1, source_target_pairs={{0,4},{1,5},{2,6},{3,7},{4,0},{5,1},{6,2},{7,3},{8,12},{9,13},{10,... | collective-permute-start | bytes 1572872 | tf_op jit(solution)/shard_map/ppermute | solution.py:247
  174.1 18.0 %collective-permute-start.42 = (bf16[256,1024]{1,0:T(8,128)(2,1)}, bf16[256,1024]{1,0:T(8,128)(2,1)}, u32[]{:S(2)}, u32[]{:S(2)}) collective-permute-start(bf16[256,1024]{1,0:T(8,128)(2,1)} %get-tuple-element.108.refs_4_), channel_id=1, source_target_pairs={{0,4},{1,5},{2,6},{3,7},{4,0},{5,1},{6,2},{7,3},{8,12},{9,13},{10,... | collective-permute-start | bytes 1572872 | tf_op jit(solution)/shard_map/ppermute | solution.py:247
  188.0 12.8 %collective-permute-start.40 = (bf16[256,1024]{1,0:T(8,128)(2,1)S(1)}, bf16[256,1024]{1,0:T(8,128)(2,1)S(1)}, u32[]{:S(2)}, u32[]{:S(2)}) collective-permute-start(bf16[256,1024]{1,0:T(8,128)(2,1)S(1)} %collective-permute-done.38.refs_6_), channel_id=1, source_target_pairs={{0,3},{1,0},{2,1},{3,2},{4,7},{5,4},{6,5},{7,6},{8,11},{9,8},{10,9... | collective-permute-start | bytes 1572872 | tf_op jit(solution)/shard_map/ppermute | solution.py:247
  188.3 14.1 %collective-permute-start.39 = (bf16[256,1024]{1,0:T(8,128)(2,1)S(1)}, bf16[256,1024]{1,0:T(8,128)(2,1)S(1)}, u32[]{:S(2)}, u32[]{:S(2)}) collective-permute-start(bf16[256,1024]{1,0:T(8,128)(2,1)S(1)} %collective-permute-done.35.refs_1_), channel_id=1, source_target_pairs={{0,1},{1,2},{2,3},{3,0},{4,5},{5,6},{6,7},{7,4},{8,9},{9,10},{10,1... | collective-permute-start | bytes 1572872 | tf_op jit(solution)/shard_map/ppermute | solution.py:247
  190.0 26.2 %collective-permute-start.45 = (bf16[256,1024]{1,0:T(8,128)(2,1)S(1)}, bf16[256,1024]{1,0:T(8,128)(2,1)}, u32[]{:S(2)}, u32[]{:S(2)}) collective-permute-start(bf16[256,1024]{1,0:T(8,128)(2,1)S(1)} %collective-permute-done.35.refs_1_), channel_id=1, source_target_pairs={{0,4},{1,5},{2,6},{3,7},{4,0},{5,1},{6,2},{7,3},{8,12},{9,13},{10,... | collective-permute-start | bytes 1572872 | tf_op jit(solution)/shard_map/ppermute | solution.py:247
  191.0 25.3 %collective-permute-start.46 = (bf16[256,1024]{1,0:T(8,128)(2,1)S(1)}, bf16[256,1024]{1,0:T(8,128)(2,1)}, u32[]{:S(2)}, u32[]{:S(2)}) collective-permute-start(bf16[256,1024]{1,0:T(8,128)(2,1)S(1)} %collective-permute-done.36.refs_2_), channel_id=1, source_target_pairs={{0,4},{1,5},{2,6},{3,7},{4,0},{5,1},{6,2},{7,3},{8,12},{9,13},{10,... | collective-permute-start | bytes 1572872 | tf_op jit(solution)/shard_map/ppermute | solution.py:247
  202.4 13.8 %collective-permute-start.44 = (bf16[256,1024]{1,0:T(8,128)(2,1)}, bf16[256,1024]{1,0:T(8,128)(2,1)S(1)}, u32[]{:S(2)}, u32[]{:S(2)}) collective-permute-start(bf16[256,1024]{1,0:T(8,128)(2,1)} %collective-permute-done.42.refs_4_), channel_id=1, source_target_pairs={{0,3},{1,0},{2,1},{3,2},{4,7},{5,4},{6,5},{7,6},{8,11},{9,8},{10,9... | collective-permute-start | bytes 1572872 | tf_op jit(solution)/shard_map/ppermute | solution.py:247
  203.5 13.4 %collective-permute-start.43 = (bf16[256,1024]{1,0:T(8,128)(2,1)}, bf16[256,1024]{1,0:T(8,128)(2,1)S(1)}, u32[]{:S(2)}, u32[]{:S(2)}) collective-permute-start(bf16[256,1024]{1,0:T(8,128)(2,1)} %collective-permute-done.42.refs_4_), channel_id=1, source_target_pairs={{0,1},{1,2},{2,3},{3,0},{4,5},{5,6},{6,7},{7,4},{8,9},{9,10},{10,1... | collective-permute-start | bytes 1572872 | tf_op jit(solution)/shard_map/ppermute | solution.py:247
  205.1 19.8 %collective-permute-start.47 = (bf16[256,1024]{1,0:T(8,128)(2,1)S(1)}, bf16[256,1024]{1,0:T(8,128)(2,1)}, u32[]{:S(2)}, u32[]{:S(2)}) collective-permute-start(bf16[256,1024]{1,0:T(8,128)(2,1)S(1)} %collective-permute-done.39.refs_3_), channel_id=1, source_target_pairs={{0,4},{1,5},{2,6},{3,7},{4,0},{5,1},{6,2},{7,3},{8,12},{9,13},{10,... | collective-permute-start | bytes 1572872 | tf_op jit(solution)/shard_map/ppermute | solution.py:247
  (59 other events, 974.3 us)

commit v4 on v3

--- a/solution.py
+++ b/solution.py
@@ -15,7 +15,7 @@
 NONE = 64
 
 
-def pack_kernel(atom, column, count, blocks, send, seen, place):
+def pack_kernel(atom, column, count, blocks, send, seen, place, sems):
     groups = send.shape[0]
     slots = blocks.shape[0]
     send[...] = jnp.zeros_like(send)
@@ -33,12 +33,19 @@
             seen[group] = turn + 1
             place[group * CAP + turn] = atom[slot] % BR * BC + column[slot]
             start = pl.multiple_of(turn * BLOCK, BLOCK)
-            send[group, pl.ds(start, BLOCK), :] = blocks[slot]
+            target = send.at[group, pl.ds(start, BLOCK)]
+            pltpu.make_async_copy(blocks.at[slot], target, sems.at[slot]).start()
 
     row = lax.broadcasted_iota(jnp.int32, (META, BLOCK), 0)
     for group in range(groups):
         value = jnp.where(row == 0, place[group * CAP], place[group * CAP + 1])
         send[group, CAP * BLOCK :, :] = value.astype(jnp.float32).astype(send.dtype)
+
+    @pl.loop(0, slots)
+    def _(slot):
+        @pl.when(slot < count[0, 0])
+        def _():
+            pltpu.make_async_copy(blocks.at[slot], send.at[0, pl.ds(0, BLOCK)], sems.at[slot]).wait()
 
 
 def unpack_kernel(received, tile, place_vector, place, sem):
@@ -74,10 +81,10 @@
     send = pl.pallas_call(
         pack_kernel,
         out_shape=jax.ShapeDtypeStruct((owners, CAP * BLOCK + META, BLOCK), blocks.dtype),
-        in_specs=[smem, smem, smem, vmem],
+        in_specs=[smem, smem, smem, pl.BlockSpec(memory_space=pltpu.HBM)],
         out_specs=vmem,
-        scratch_shapes=[pltpu.SMEM((owners,), jnp.int32), pltpu.SMEM((owners * CAP,), jnp.int32)],
-        compiler_params=pltpu.CompilerParams(vmem_limit_bytes=16 << 20),
+        scratch_shapes=[pltpu.SMEM((owners,), jnp.int32), pltpu.SMEM((owners * CAP,), jnp.int32), pltpu.SemaphoreType.DMA((blocks.shape[0],))],
+        compiler_params=pltpu.CompilerParams(vmem_limit_bytes=58 << 20),
         name="pack",
     )(block_atom[:, 0], block_col[:, 0], block_count, blocks)
     received = lax.all_to_all(send, "row", 0, 0, tiled=True)

time: 238 us -> 237 us (level)
  local copies, waits for them, and re-layouts: 9.48 us -> 6.52 us
    unnamed x82 -> x74, local copies, waits for them, and re-layouts: 6.61 us -> 3.5 us
  transfers between devices with their start and end apart: 50 -> 50, of which waited for: 30 -> 31; matrix products, arithmetic and copies ran while one was open for 1% -> 1% of each run, Pallas kernels for 4% -> 4%
where the time goes in v4:
time: 237 us; the launch traced here: 236 us
  waiting for transfers between devices  115 us (49%)
  starting transfers between devices  45.9 us (19%)
  Pallas kernels  40.4 us (17%)
  blocking collectives  27.1 us (11%)
  local copies, waits for them, and re-layouts  6.52 us (3%)
    ppermute x27, waiting for transfers between devices, over_col(): return lax.ppermute(value, 'col', pairs)  68.8 us
    ppermute x23, waiting for transfers between devices, over_row(): return lax.ppermute(value, 'row', pairs)  46.5 us
    pallas_call x3, Pallas kernels, product(): pl.pallas_call(functools.partial(product_kernel, factor, left_parts, righ...  35.8 us
    ppermute x27, starting transfers between devices, over_col(): return lax.ppermute(value, 'col', pairs)  28.4 us
    all_to_all x1, blocking collectives, local_tile(): received = lax.all_to_all(send, 'row', 0, 0, tiled=True)  27.1 us
    ppermute x23, starting transfers between devices, over_row(): return lax.ppermute(value, 'row', pairs)  17.6 us
  transfers between devices with their start and end apart: 50, of which 31 were waited for; matrix products, arithmetic and copies ran while one was open for 1% of the time, Pallas kernels for 4%

profile of v4, /device:TPU:0, one launch (start us, length us, event | category | flops | bytes accessed | tf_op | source)
XLA Modules:
  0.0 236.4 jit_solution(1309862649621398277)
XLA Ops:
  0.7 3.3 %pack.1 = bf16[16,272,128]{2,1,0:T(8,128)(2,1)} custom-call(s32[32]{0:T(128)} %bitcast.21, s32[32]{0:T(128)} %bitcast.22, s32[1,1]{1,0:T(1,128)S(6)} %copy.5.count, bf16[32,128,128]{2,1,0:T(8,128)(2,1)} %blocks.1), custom_call_target="tpu_custom_call" | custom-call | tf_op jit(solution)/shard_map/pack/pallas_call | solution.py:81
  4.0 27.1 %all_to_all.5.received = bf16[16,272,128]{2,1,0:T(8,128)(2,1)S(1)} all-to-all(bf16[16,272,128]{2,1,0:T(8,128)(2,1)} %pack.1), channel_id=1, replica_groups=mesh['row'=16,'col'=8] {'row'}, dimensions={0} | all-to-all | bytes 2228224 | tf_op jit(solution)/shard_map/all_to_all | solution.py:90
  34.5 2.3 collective-permute-start.2
  37.6 20.1 %collective-permute-done.4.refs_17_.refs_12_.refs_13_ = bf16[512,1024]{1,0:T(8,128)(2,1)S(1)} collective-permute-done((bf16[512,1024]{1,0:T(8,128)(2,1)S(1)}, bf16[512,1024]{1,0:T(8,128)(2,1)S(1)}, u32[]{:S(2)}, u32[]{:S(2)}) %collective-permute-start.4) | collective-permute-done | bytes 1048608 | tf_op jit(solution)/shard_map/ppermute | solution.py:245
  57.6 2.1 collective-permute-done.3.refs_15_.refs_10_.refs_11_
  59.8 2.6 %collective-permute-done.1.refs_1_ = bf16[512,1024]{1,0:T(8,128)(2,1)S(1)} collective-permute-done((bf16[512,1024]{1,0:T(8,128)(2,1)S(1)}, bf16[512,1024]{1,0:T(8,128)(2,1)S(1)}, u32[]{:S(2)}, u32[]{:S(2)}) %collective-permute-start.1) | collective-permute-done | bytes 1048608 | tf_op jit(solution)/shard_map/ppermute | solution.py:254
  63.3 2.5 %collective-permute-start.9 = (bf16[256,1024]{1,0:T(8,128)(2,1)S(1)}, bf16[256,1024]{1,0:T(8,128)(2,1)S(1)}, u32[]{:S(2)}, u32[]{:S(2)}) collective-permute-start(bf16[256,1024]{1,0:T(8,128)(2,1)S(1)} %slice.35), channel_id=1, source_target_pairs={{0,48},{8,56},{16,0},{24,8},{32,16},{40,24},{48,32},{56,40},{64,11... | collective-permute-start | bytes 1572872 | tf_op jit(solution)/shard_map/ppermute | solution.py:245
  65.9 2.5 %collective-permute-start.7 = (bf16[256,1024]{1,0:T(8,128)(2,1)S(1)}, bf16[256,1024]{1,0:T(8,128)(2,1)S(1)}, u32[]{:S(2)}, u32[]{:S(2)}) collective-permute-start(bf16[256,1024]{1,0:T(8,128)(2,1)S(1)} %slice.33), channel_id=1, source_target_pairs={{0,3},{1,0},{2,1},{3,2},{4,7},{5,4},{6,5},{7,6},{8,11},{9,8},{10,9... | collective-permute-start | bytes 1572872 | tf_op jit(solution)/shard_map/ppermute | solution.py:254
  69.5 6.1 %collective-permute-done.9.refs_20_.refs_15_.refs_16_ = bf16[256,1024]{1,0:T(8,128)(2,1)S(1)} collective-permute-done((bf16[256,1024]{1,0:T(8,128)(2,1)S(1)}, bf16[256,1024]{1,0:T(8,128)(2,1)S(1)}, u32[]{:S(2)}, u32[]{:S(2)}) %collective-permute-start.9) | collective-permute-done | bytes 524320 | tf_op jit(solution)/shard_map/ppermute | solution.py:245
  75.6 3.4 %collective-permute-done.8.refs_19_.refs_14_.refs_15_ = bf16[256,1024]{1,0:T(8,128)(2,1)S(1)} collective-permute-done((bf16[256,1024]{1,0:T(8,128)(2,1)S(1)}, bf16[256,1024]{1,0:T(8,128)(2,1)S(1)}, u32[]{:S(2)}, u32[]{:S(2)}) %collective-permute-start.8) | collective-permute-done | bytes 524320 | tf_op jit(solution)/shard_map/ppermute | solution.py:245
  79.0 2.0 collective-permute-done.6.refs_3_
  84.2 3.0 %collective-permute-start.14 = (bf16[256,1024]{1,0:T(8,128)(2,1)S(1)}, bf16[256,1024]{1,0:T(8,128)(2,1)}, u32[]{:S(2)}, u32[]{:S(2)}) collective-permute-start(bf16[256,1024]{1,0:T(8,128)(2,1)S(1)} %get-tuple-element.82), channel_id=1, source_target_pairs={{0,48},{8,56},{16,0},{24,8},{32,16},{40,24},{48,32},{56,40},{64,11... | collective-permute-start | bytes 1572872 | tf_op jit(solution)/shard_map/ppermute | solution.py:245
  87.2 5.8 %collective-permute-done.10.refs_9_ = bf16[256,1024]{1,0:T(8,128)(2,1)S(1)} collective-permute-done((bf16[256,1024]{1,0:T(8,128)(2,1)S(1)}, bf16[256,1024]{1,0:T(8,128)(2,1)S(1)}, u32[]{:S(2)}, u32[]{:S(2)}) %collective-permute-start.10) | collective-permute-done | bytes 524320 | tf_op jit(solution)/shard_map/ppermute | solution.py:254
  94.0 5.5 %collective-permute-done.13.refs_25_.refs_20_.refs_21_ = bf16[256,1024]{1,0:T(8,128)(2,1)} collective-permute-done((bf16[256,1024]{1,0:T(8,128)(2,1)S(1)}, bf16[256,1024]{1,0:T(8,128)(2,1)}, u32[]{:S(2)}, u32[]{:S(2)}) %collective-permute-start.13) | collective-permute-done | bytes 524320 | tf_op jit(solution)/shard_map/ppermute | solution.py:245
  99.5 3.2 %collective-permute-start.17 = (bf16[256,1024]{1,0:T(8,128)(2,1)S(1)}, bf16[256,1024]{1,0:T(8,128)(2,1)S(1)}, u32[]{:S(2)}, u32[]{:S(2)}) collective-permute-start(bf16[256,1024]{1,0:T(8,128)(2,1)S(1)} %get-tuple-element.83), channel_id=1, source_target_pairs={{0,48},{8,56},{16,0},{24,8},{32,16},{40,24},{48,32},{56,40},{64,11... | collective-permute-start | bytes 1572872 | tf_op jit(solution)/shard_map/ppermute | solution.py:245
  103.3 3.4 %collective-permute-start.19 = (bf16[256,1024]{1,0:T(8,128)(2,1)S(1)}, bf16[256,1024]{1,0:T(8,128)(2,1)S(1)}, u32[]{:S(2)}, u32[]{:S(2)}) collective-permute-start(bf16[256,1024]{1,0:T(8,128)(2,1)S(1)} %collective-permute-done.10.refs_9_), channel_id=1, source_target_pairs={{0,3},{1,0},{2,1},{3,2},{4,7},{5,4},{6,5},{7,6},{8,11},{9,8},{10,9... | collective-permute-start | bytes 1572872 | tf_op jit(solution)/shard_map/ppermute | solution.py:254
  106.6 3.3 %collective-permute-done.16.refs_26_.refs_21_.refs_22_ = bf16[256,1024]{1,0:T(8,128)(2,1)S(1)} collective-permute-done((bf16[256,1024]{1,0:T(8,128)(2,1)S(1)}, bf16[256,1024]{1,0:T(8,128)(2,1)S(1)}, u32[]{:S(2)}, u32[]{:S(2)}) %collective-permute-start.16) | collective-permute-done | bytes 524320 | tf_op jit(solution)/shard_map/ppermute | solution.py:245
  110.0 8.0 %collective-permute-done.19.refs_11_ = bf16[256,1024]{1,0:T(8,128)(2,1)S(1)} collective-permute-done((bf16[256,1024]{1,0:T(8,128)(2,1)S(1)}, bf16[256,1024]{1,0:T(8,128)(2,1)S(1)}, u32[]{:S(2)}, u32[]{:S(2)}) %collective-permute-start.19) | collective-permute-done | bytes 524320 | tf_op jit(solution)/shard_map/ppermute | solution.py:254
  118.1 3.4 %collective-permute-done.18.refs_10_ = bf16[256,1024]{1,0:T(8,128)(2,1)S(1)} collective-permute-done((bf16[256,1024]{1,0:T(8,128)(2,1)S(1)}, bf16[256,1024]{1,0:T(8,128)(2,1)S(1)}, u32[]{:S(2)}, u32[]{:S(2)}) %collective-permute-start.18) | collective-permute-done | bytes 524320 | tf_op jit(solution)/shard_map/ppermute | solution.py:254
  122.5 3.2 %collective-permute-start.21 = (bf16[256,1024]{1,0:T(8,128)(2,1)}, bf16[256,1024]{1,0:T(8,128)(2,1)}, u32[]{:S(2)}, u32[]{:S(2)}) collective-permute-start(bf16[256,1024]{1,0:T(8,128)(2,1)} %collective-permute-done.14.refs_30_.refs_25_.refs_26_), channel_id=1, source_target_pairs={{0,48},{8,56},{16,0},{24,8},{32,16},{40,24},{48,32},{56,40},{64,11... | collective-permute-start | bytes 1572872 | tf_op jit(solution)/shard_map/ppermute | solution.py:245
  125.7 7.4 %collective-permute-done.15.refs_8_ = bf16[256,1024]{1,0:T(8,128)(2,1)S(1)} collective-permute-done((bf16[256,1024]{1,0:T(8,128)(2,1)S(1)}, bf16[256,1024]{1,0:T(8,128)(2,1)S(1)}, u32[]{:S(2)}, u32[]{:S(2)}) %collective-permute-start.15) | collective-permute-done | bytes 524320 | tf_op jit(solution)/shard_map/ppermute | solution.py:254
  133.6 2.6 %collective-permute-done.20.refs_33_.refs_28_.refs_29_ = bf16[256,1024]{1,0:T(8,128)(2,1)} collective-permute-done((bf16[256,1024]{1,0:T(8,128)(2,1)}, bf16[256,1024]{1,0:T(8,128)(2,1)}, u32[]{:S(2)}, u32[]{:S(2)}) %collective-permute-start.20) | collective-permute-done | bytes 524320 | tf_op jit(solution)/shard_map/ppermute | solution.py:245
  142.9 15.1 %square.1 = (bf16[256,1024]{1,0:T(8,128)(2,1)}, bf16[256,1024]{1,0:T(8,128)(2,1)}) custom-call(s32[13]{0:T(128)} %stack.58.left_at, s32[8]{0:T(128)} %stack.53.right_at, s32[1]{0:T(128)} %bitcast.12.core, s32[1]{0:T(128)} %constant.244.clone.1.want, bf16[512,1024]{1,0:T(8,128)(2,1)} %copy-done, bf16[512,1024]{1,0:T(8,128)(2,1)} %copy-done.25, ...), custom_call_target="tpu_custom_call" | custom-call | flops 8589934592 | bytes 25165824 | tf_op jit(solution)/shard_map/square/pallas_call | solution.py:206
  160.2 3.0 %collective-permute-start.38 = (bf16[256,1024]{1,0:T(8,128)(2,1)}, bf16[256,1024]{1,0:T(8,128)(2,1)S(1)}, u32[]{:S(2)}, u32[]{:S(2)}) collective-permute-start(bf16[256,1024]{1,0:T(8,128)(2,1)} %get-tuple-element.108.refs_4_), channel_id=1, source_target_pairs={{0,3},{1,0},{2,1},{3,2},{4,7},{5,4},{6,5},{7,6},{8,11},{9,8},{10,9... | collective-permute-start | bytes 1572872 | tf_op jit(solution)/shard_map/ppermute | solution.py:254
  163.7 9.4 %collective-permute-done.36.refs_2_ = bf16[256,1024]{1,0:T(8,128)(2,1)S(1)} collective-permute-done((bf16[256,1024]{1,0:T(8,128)(2,1)}, bf16[256,1024]{1,0:T(8,128)(2,1)S(1)}, u32[]{:S(2)}, u32[]{:S(2)}) %collective-permute-start.36) | collective-permute-done | bytes 524320 | tf_op jit(solution)/shard_map/ppermute | solution.py:254
  173.8 2.4 %collective-permute-done.35.refs_1_ = bf16[256,1024]{1,0:T(8,128)(2,1)S(1)} collective-permute-done((bf16[256,1024]{1,0:T(8,128)(2,1)}, bf16[256,1024]{1,0:T(8,128)(2,1)S(1)}, u32[]{:S(2)}, u32[]{:S(2)}) %collective-permute-start.35) | collective-permute-done | bytes 524320 | tf_op jit(solution)/shard_map/ppermute | solution.py:254
  176.1 7.4 %collective-permute-done.38.refs_6_ = bf16[256,1024]{1,0:T(8,128)(2,1)S(1)} collective-permute-done((bf16[256,1024]{1,0:T(8,128)(2,1)}, bf16[256,1024]{1,0:T(8,128)(2,1)S(1)}, u32[]{:S(2)}, u32[]{:S(2)}) %collective-permute-start.38) | collective-permute-done | bytes 524320 | tf_op jit(solution)/shard_map/ppermute | solution.py:254
  183.5 2.7 %collective-permute-done.37.refs_5_ = bf16[256,1024]{1,0:T(8,128)(2,1)S(1)} collective-permute-done((bf16[256,1024]{1,0:T(8,128)(2,1)}, bf16[256,1024]{1,0:T(8,128)(2,1)S(1)}, u32[]{:S(2)}, u32[]{:S(2)}) %collective-permute-start.37) | collective-permute-done | bytes 524320 | tf_op jit(solution)/shard_map/ppermute | solution.py:254
  191.1 8.7 %collective-permute-done.40.refs_7_ = bf16[256,1024]{1,0:T(8,128)(2,1)S(1)} collective-permute-done((bf16[256,1024]{1,0:T(8,128)(2,1)S(1)}, bf16[256,1024]{1,0:T(8,128)(2,1)S(1)}, u32[]{:S(2)}, u32[]{:S(2)}) %collective-permute-start.40) | collective-permute-done | bytes 524320 | tf_op jit(solution)/shard_map/ppermute | solution.py:254
  204.7 10.1 %step_first.1.refs_33_ = f32[512,1024]{1,0:T(8,128)} custom-call(s32[8]{0:T(128)} %stack.59.left_at, s32[8]{0:T(128)} %stack.53.right_at, s32[1]{0:T(128)} %bitcast.12.core, s32[1]{0:T(128)} %bitcast.20.want, bf16[256,1024]{1,0:T(8,128)(2,1)} %get-tuple-element.106.refs_0_, bf16[256,1024]{1,0:T(8,128)(2,1)} %copy-done.18, bf16[256,1024]{1,0:T(8,128)(2,1)} %copy-done.17, ...), custom_call_target="tpu_custom_call" | custom-call | flops 4294967296 | bytes 12582912 | tf_op jit(solution)/shard_map/step_first/pallas_call | solution.py:206
  218.7 5.2 %collective-permute-done.47.refs_3_ = bf16[256,1024]{1,0:T(8,128)(2,1)} collective-permute-done((bf16[256,1024]{1,0:T(8,128)(2,1)S(1)}, bf16[256,1024]{1,0:T(8,128)(2,1)}, u32[]{:S(2)}, u32[]{:S(2)}) %collective-permute-start.47) | collective-permute-done | bytes 524320 | tf_op jit(solution)/shard_map/ppermute | solution.py:254
  225.6 10.6 %step_last.1 = f32[512,1024]{1,0:T(8,128)} custom-call(s32[9]{0:T(128)} %stack.44.left_at, s32[8]{0:T(128)} %stack.53.right_at, s32[1]{0:T(128)} %bitcast.12.core, s32[1]{0:T(128)} %bitcast.13.want, bf16[256,1024]{1,0:T(8,128)(2,1)} %copy-done.23, bf16[256,1024]{1,0:T(8,128)(2,1)} %collective-permute-done.45.refs_1_, ...), custom_call_target="tpu_custom_call" | custom-call | flops 4294967296 | bytes 12582912 | tf_op jit(solution)/shard_map/step_last/pallas_call | solution.py:206
  (160 shorter events, 37.7 us)
Async XLA Ops:
  32.4 25.2 %collective-permute-start.4 = (bf16[512,1024]{1,0:T(8,128)(2,1)S(1)}, bf16[512,1024]{1,0:T(8,128)(2,1)S(1)}, u32[]{:S(2)}, u32[]{:S(2)}) collective-permute-start(bf16[512,1024]{1,0:T(8,128)(2,1)S(1)} %unpack.1.refs_0_.refs_13_.refs_8_.refs_9_.refs_34_), channel_id=1, source_target_pairs={{0,48},{8,56},{16,0},{24,8},{32,16},{40,24},{48,32},{56,40},{64,11... | collective-permute-start | bytes 3145736 | tf_op jit(solution)/shard_map/ppermute | solution.py:245
  33.7 26.1 %collective-permute-start.3 = (bf16[512,1024]{1,0:T(8,128)(2,1)S(1)}, bf16[512,1024]{1,0:T(8,128)(2,1)S(1)}, u32[]{:S(2)}, u32[]{:S(2)}) collective-permute-start(bf16[512,1024]{1,0:T(8,128)(2,1)S(1)} %unpack.1.refs_0_.refs_13_.refs_8_.refs_9_.refs_34_), channel_id=1, source_target_pairs={{0,16},{8,24},{16,32},{24,40},{32,48},{40,56},{48,0},{56,8},{64,80... | collective-permute-start | bytes 3145736 | tf_op jit(solution)/shard_map/ppermute | solution.py:245
  34.5 25.3 %collective-permute-start.2 = (bf16[512,1024]{1,0:T(8,128)(2,1)S(1)}, bf16[512,1024]{1,0:T(8,128)(2,1)S(1)}, u32[]{:S(2)}, u32[]{:S(2)}) collective-permute-start(bf16[512,1024]{1,0:T(8,128)(2,1)S(1)} %unpack.1.refs_0_.refs_13_.refs_8_.refs_9_.refs_34_), channel_id=1, source_target_pairs={{0,3},{1,0},{2,1},{3,2},{4,7},{5,4},{6,5},{7,6},{8,11},{9,8},{10,9... | collective-permute-start | bytes 3145736 | tf_op jit(solution)/shard_map/ppermute | solution.py:254
  36.8 25.5 %collective-permute-start.1 = (bf16[512,1024]{1,0:T(8,128)(2,1)S(1)}, bf16[512,1024]{1,0:T(8,128)(2,1)S(1)}, u32[]{:S(2)}, u32[]{:S(2)}) collective-permute-start(bf16[512,1024]{1,0:T(8,128)(2,1)S(1)} %unpack.1.refs_0_.refs_13_.refs_8_.refs_9_.refs_34_), channel_id=1, source_target_pairs={{0,1},{1,2},{2,3},{3,0},{4,5},{5,6},{6,7},{7,4},{8,9},{9,10},{10,1... | collective-permute-start | bytes 3145736 | tf_op jit(solution)/shard_map/ppermute | solution.py:254
  36.8 25.8 %collective-permute-start = (bf16[512,1024]{1,0:T(8,128)(2,1)S(1)}, bf16[512,1024]{1,0:T(8,128)(2,1)S(1)}, u32[]{:S(2)}, u32[]{:S(2)}) collective-permute-start(bf16[512,1024]{1,0:T(8,128)(2,1)S(1)} %unpack.1.refs_0_.refs_13_.refs_8_.refs_9_.refs_34_), channel_id=1, source_target_pairs={{0,64},{8,72},{16,80},{24,88},{32,96},{40,104},{48,112},{56,120},{... | collective-permute-start | bytes 3145736 | tf_op jit(solution)/shard_map/ppermute | solution.py:245
  63.3 12.3 %collective-permute-start.9 = (bf16[256,1024]{1,0:T(8,128)(2,1)S(1)}, bf16[256,1024]{1,0:T(8,128)(2,1)S(1)}, u32[]{:S(2)}, u32[]{:S(2)}) collective-permute-start(bf16[256,1024]{1,0:T(8,128)(2,1)S(1)} %slice.35), channel_id=1, source_target_pairs={{0,48},{8,56},{16,0},{24,8},{32,16},{40,24},{48,32},{56,40},{64,11... | collective-permute-start | bytes 1572872 | tf_op jit(solution)/shard_map/ppermute | solution.py:245
  65.9 13.2 %collective-permute-start.8 = (bf16[256,1024]{1,0:T(8,128)(2,1)S(1)}, bf16[256,1024]{1,0:T(8,128)(2,1)S(1)}, u32[]{:S(2)}, u32[]{:S(2)}) collective-permute-start(bf16[256,1024]{1,0:T(8,128)(2,1)S(1)} %slice.34), channel_id=1, source_target_pairs={{0,16},{8,24},{16,32},{24,40},{32,48},{40,56},{48,0},{56,8},{64,80... | collective-permute-start | bytes 1572872 | tf_op jit(solution)/shard_map/ppermute | solution.py:245
  65.9 13.2 %collective-permute-start.7 = (bf16[256,1024]{1,0:T(8,128)(2,1)S(1)}, bf16[256,1024]{1,0:T(8,128)(2,1)S(1)}, u32[]{:S(2)}, u32[]{:S(2)}) collective-permute-start(bf16[256,1024]{1,0:T(8,128)(2,1)S(1)} %slice.33), channel_id=1, source_target_pairs={{0,3},{1,0},{2,1},{3,2},{4,7},{5,4},{6,5},{7,6},{8,11},{9,8},{10,9... | collective-permute-start | bytes 1572872 | tf_op jit(solution)/shard_map/ppermute | solution.py:254
  68.4 12.6 %collective-permute-start.6 = (bf16[256,1024]{1,0:T(8,128)(2,1)S(1)}, bf16[256,1024]{1,0:T(8,128)(2,1)S(1)}, u32[]{:S(2)}, u32[]{:S(2)}) collective-permute-start(bf16[256,1024]{1,0:T(8,128)(2,1)S(1)} %slice.32), channel_id=1, source_target_pairs={{0,1},{1,2},{2,3},{3,0},{4,5},{5,6},{6,7},{7,4},{8,9},{9,10},{10,1... | collective-permute-start | bytes 1572872 | tf_op jit(solution)/shard_map/ppermute | solution.py:254
  68.4 12.6 %collective-permute-start.5 = (bf16[256,1024]{1,0:T(8,128)(2,1)S(1)}, bf16[256,1024]{1,0:T(8,128)(2,1)S(1)}, u32[]{:S(2)}, u32[]{:S(2)}) collective-permute-start(bf16[256,1024]{1,0:T(8,128)(2,1)S(1)} %get-tuple-element.68), channel_id=1, source_target_pairs={{0,4},{1,5},{2,6},{3,7},{4,0},{5,1},{6,2},{7,3},{8,12},{9,13},{10,... | collective-permute-start | bytes 1572872 | tf_op jit(solution)/shard_map/ppermute | solution.py:254
  81.0 12.0 %collective-permute-start.12 = (bf16[256,1024]{1,0:T(8,128)(2,1)S(1)}, bf16[256,1024]{1,0:T(8,128)(2,1)S(1)}, u32[]{:S(2)}, u32[]{:S(2)}) collective-permute-start(bf16[256,1024]{1,0:T(8,128)(2,1)S(1)} %collective-permute-done.5.refs_5_), channel_id=1, source_target_pairs={{0,3},{1,0},{2,1},{3,2},{4,7},{5,4},{6,5},{7,6},{8,11},{9,8},{10,9... | collective-permute-start | bytes 1572872 | tf_op jit(solution)/shard_map/ppermute | solution.py:254
  87.2 12.3 %collective-permute-start.13 = (bf16[256,1024]{1,0:T(8,128)(2,1)S(1)}, bf16[256,1024]{1,0:T(8,128)(2,1)}, u32[]{:S(2)}, u32[]{:S(2)}) collective-permute-start(bf16[256,1024]{1,0:T(8,128)(2,1)S(1)} %get-tuple-element.83), channel_id=1, source_target_pairs={{0,16},{8,24},{16,32},{24,40},{32,48},{40,56},{48,0},{56,8},{64,80... | collective-permute-start | bytes 1572872 | tf_op jit(solution)/shard_map/ppermute | solution.py:245
  102.8 19.7 %collective-permute-start.23 = (bf16[512,1024]{1,0:T(8,128)(2,1)S(1)}, bf16[512,1024]{1,0:T(8,128)(2,1)S(1)}, u32[]{:S(2)}, u32[]{:S(2)}) collective-permute-start(bf16[512,1024]{1,0:T(8,128)(2,1)S(1)} %unpack.1.refs_0_.refs_13_.refs_8_.refs_9_.refs_34_), channel_id=1, source_target_pairs={{0,8},{8,0},{16,24},{24,16},{32,40},{40,32},{48,56},{56,48},{64,72... | collective-permute-start | bytes 3145736 | tf_op jit(solution)/shard_map/ppermute | solution.py:245
  102.8 19.7 %collective-permute-start.24 = (bf16[512,1024]{1,0:T(8,128)(2,1)S(1)}, bf16[512,1024]{1,0:T(8,128)(2,1)S(1)}, u32[]{:S(2)}, u32[]{:S(2)}) collective-permute-start(bf16[512,1024]{1,0:T(8,128)(2,1)S(1)} %collective-permute-done.3.refs_15_.refs_10_.refs_11_), channel_id=1, source_target_pairs={{0,8},{8,0},{16,24},{24,16},{32,40},{40,32},{48,56},{56,48},{64,72... | collective-permute-start | bytes 3145736 | tf_op jit(solution)/shard_map/ppermute | solution.py:245
  103.3 14.8 %collective-permute-start.19 = (bf16[256,1024]{1,0:T(8,128)(2,1)S(1)}, bf16[256,1024]{1,0:T(8,128)(2,1)S(1)}, u32[]{:S(2)}, u32[]{:S(2)}) collective-permute-start(bf16[256,1024]{1,0:T(8,128)(2,1)S(1)} %collective-permute-done.10.refs_9_), channel_id=1, source_target_pairs={{0,3},{1,0},{2,1},{3,2},{4,7},{5,4},{6,5},{7,6},{8,11},{9,8},{10,9... | collective-permute-start | bytes 1572872 | tf_op jit(solution)/shard_map/ppermute | solution.py:254
  109.9 15.8 %collective-permute-start.25 = (bf16[512,1024]{1,0:T(8,128)(2,1)S(1)}, bf16[512,1024]{1,0:T(8,128)(2,1)S(1)}, u32[]{:S(2)}, u32[]{:S(2)}) collective-permute-start(bf16[512,1024]{1,0:T(8,128)(2,1)S(1)} %collective-permute-done.4.refs_17_.refs_12_.refs_13_), channel_id=1, source_target_pairs={{0,8},{8,0},{16,24},{24,16},{32,40},{40,32},{48,56},{56,48},{64,72... | collective-permute-start | bytes 3145736 | tf_op jit(solution)/shard_map/ppermute | solution.py:245
  118.1 15.0 %collective-permute-start.15 = (bf16[256,1024]{1,0:T(8,128)(2,1)S(1)}, bf16[256,1024]{1,0:T(8,128)(2,1)S(1)}, u32[]{:S(2)}, u32[]{:S(2)}) collective-permute-start(bf16[256,1024]{1,0:T(8,128)(2,1)S(1)} %collective-permute-done.11.refs_6_), channel_id=1, source_target_pairs={{0,1},{1,2},{2,3},{3,0},{4,5},{5,6},{6,7},{7,4},{8,9},{9,10},{10,1... | collective-permute-start | bytes 1572872 | tf_op jit(solution)/shard_map/ppermute | solution.py:254
  122.5 13.7 %collective-permute-start.20 = (bf16[256,1024]{1,0:T(8,128)(2,1)}, bf16[256,1024]{1,0:T(8,128)(2,1)}, u32[]{:S(2)}, u32[]{:S(2)}) collective-permute-start(bf16[256,1024]{1,0:T(8,128)(2,1)} %collective-permute-done.13.refs_25_.refs_20_.refs_21_), channel_id=1, source_target_pairs={{0,16},{8,24},{16,32},{24,40},{32,48},{40,56},{48,0},{56,8},{64,80... | collective-permute-start | bytes 1572872 | tf_op jit(solution)/shard_map/ppermute | solution.py:245
  122.5 13.7 %collective-permute-start.21 = (bf16[256,1024]{1,0:T(8,128)(2,1)}, bf16[256,1024]{1,0:T(8,128)(2,1)}, u32[]{:S(2)}, u32[]{:S(2)}) collective-permute-start(bf16[256,1024]{1,0:T(8,128)(2,1)} %collective-permute-done.14.refs_30_.refs_25_.refs_26_), channel_id=1, source_target_pairs={{0,48},{8,56},{16,0},{24,8},{32,16},{40,24},{48,32},{56,40},{64,11... | collective-permute-start | bytes 1572872 | tf_op jit(solution)/shard_map/ppermute | solution.py:245
  158.1 15.1 %collective-permute-start.36 = (bf16[256,1024]{1,0:T(8,128)(2,1)}, bf16[256,1024]{1,0:T(8,128)(2,1)S(1)}, u32[]{:S(2)}, u32[]{:S(2)}) collective-permute-start(bf16[256,1024]{1,0:T(8,128)(2,1)} %get-tuple-element.106.refs_0_), channel_id=1, source_target_pairs={{0,3},{1,0},{2,1},{3,2},{4,7},{5,4},{6,5},{7,6},{8,11},{9,8},{10,9... | collective-permute-start | bytes 1572872 | tf_op jit(solution)/shard_map/ppermute | solution.py:254
  159.9 16.2 %collective-permute-start.35 = (bf16[256,1024]{1,0:T(8,128)(2,1)}, bf16[256,1024]{1,0:T(8,128)(2,1)S(1)}, u32[]{:S(2)}, u32[]{:S(2)}) collective-permute-start(bf16[256,1024]{1,0:T(8,128)(2,1)} %get-tuple-element.106.refs_0_), channel_id=1, source_target_pairs={{0,1},{1,2},{2,3},{3,0},{4,5},{5,6},{6,7},{7,4},{8,9},{9,10},{10,1... | collective-permute-start | bytes 1572872 | tf_op jit(solution)/shard_map/ppermute | solution.py:254
  160.2 23.4 %collective-permute-start.38 = (bf16[256,1024]{1,0:T(8,128)(2,1)}, bf16[256,1024]{1,0:T(8,128)(2,1)S(1)}, u32[]{:S(2)}, u32[]{:S(2)}) collective-permute-start(bf16[256,1024]{1,0:T(8,128)(2,1)} %get-tuple-element.108.refs_4_), channel_id=1, source_target_pairs={{0,3},{1,0},{2,1},{3,2},{4,7},{5,4},{6,5},{7,6},{8,11},{9,8},{10,9... | collective-permute-start | bytes 1572872 | tf_op jit(solution)/shard_map/ppermute | solution.py:254
  163.1 23.1 %collective-permute-start.37 = (bf16[256,1024]{1,0:T(8,128)(2,1)}, bf16[256,1024]{1,0:T(8,128)(2,1)S(1)}, u32[]{:S(2)}, u32[]{:S(2)}) collective-permute-start(bf16[256,1024]{1,0:T(8,128)(2,1)} %get-tuple-element.108.refs_4_), channel_id=1, source_target_pairs={{0,1},{1,2},{2,3},{3,0},{4,5},{5,6},{6,7},{7,4},{8,9},{9,10},{10,1... | collective-permute-start | bytes 1572872 | tf_op jit(solution)/shard_map/ppermute | solution.py:254
  163.2 26.5 %collective-permute-start.41 = (bf16[256,1024]{1,0:T(8,128)(2,1)}, bf16[256,1024]{1,0:T(8,128)(2,1)S(1)}, u32[]{:S(2)}, u32[]{:S(2)}) collective-permute-start(bf16[256,1024]{1,0:T(8,128)(2,1)} %get-tuple-element.106.refs_0_), channel_id=1, source_target_pairs={{0,4},{1,5},{2,6},{3,7},{4,0},{5,1},{6,2},{7,3},{8,12},{9,13},{10,... | collective-permute-start | bytes 1572872 | tf_op jit(solution)/shard_map/ppermute | solution.py:254
  173.1 18.0 %collective-permute-start.42 = (bf16[256,1024]{1,0:T(8,128)(2,1)}, bf16[256,1024]{1,0:T(8,128)(2,1)}, u32[]{:S(2)}, u32[]{:S(2)}) collective-permute-start(bf16[256,1024]{1,0:T(8,128)(2,1)} %get-tuple-element.108.refs_4_), channel_id=1, source_target_pairs={{0,4},{1,5},{2,6},{3,7},{4,0},{5,1},{6,2},{7,3},{8,12},{9,13},{10,... | collective-permute-start | bytes 1572872 | tf_op jit(solution)/shard_map/ppermute | solution.py:254
  187.0 12.8 %collective-permute-start.40 = (bf16[256,1024]{1,0:T(8,128)(2,1)S(1)}, bf16[256,1024]{1,0:T(8,128)(2,1)S(1)}, u32[]{:S(2)}, u32[]{:S(2)}) collective-permute-start(bf16[256,1024]{1,0:T(8,128)(2,1)S(1)} %collective-permute-done.38.refs_6_), channel_id=1, source_target_pairs={{0,3},{1,0},{2,1},{3,2},{4,7},{5,4},{6,5},{7,6},{8,11},{9,8},{10,9... | collective-permute-start | bytes 1572872 | tf_op jit(solution)/shard_map/ppermute | solution.py:254
  187.4 14.1 %collective-permute-start.39 = (bf16[256,1024]{1,0:T(8,128)(2,1)S(1)}, bf16[256,1024]{1,0:T(8,128)(2,1)S(1)}, u32[]{:S(2)}, u32[]{:S(2)}) collective-permute-start(bf16[256,1024]{1,0:T(8,128)(2,1)S(1)} %collective-permute-done.35.refs_1_), channel_id=1, source_target_pairs={{0,1},{1,2},{2,3},{3,0},{4,5},{5,6},{6,7},{7,4},{8,9},{9,10},{10,1... | collective-permute-start | bytes 1572872 | tf_op jit(solution)/shard_map/ppermute | solution.py:254
  189.1 26.2 %collective-permute-start.45 = (bf16[256,1024]{1,0:T(8,128)(2,1)S(1)}, bf16[256,1024]{1,0:T(8,128)(2,1)}, u32[]{:S(2)}, u32[]{:S(2)}) collective-permute-start(bf16[256,1024]{1,0:T(8,128)(2,1)S(1)} %collective-permute-done.35.refs_1_), channel_id=1, source_target_pairs={{0,4},{1,5},{2,6},{3,7},{4,0},{5,1},{6,2},{7,3},{8,12},{9,13},{10,... | collective-permute-start | bytes 1572872 | tf_op jit(solution)/shard_map/ppermute | solution.py:254
  189.6 25.7 %collective-permute-start.46 = (bf16[256,1024]{1,0:T(8,128)(2,1)S(1)}, bf16[256,1024]{1,0:T(8,128)(2,1)}, u32[]{:S(2)}, u32[]{:S(2)}) collective-permute-start(bf16[256,1024]{1,0:T(8,128)(2,1)S(1)} %collective-permute-done.36.refs_2_), channel_id=1, source_target_pairs={{0,4},{1,5},{2,6},{3,7},{4,0},{5,1},{6,2},{7,3},{8,12},{9,13},{10,... | collective-permute-start | bytes 1572872 | tf_op jit(solution)/shard_map/ppermute | solution.py:254
  201.4 13.8 %collective-permute-start.44 = (bf16[256,1024]{1,0:T(8,128)(2,1)}, bf16[256,1024]{1,0:T(8,128)(2,1)S(1)}, u32[]{:S(2)}, u32[]{:S(2)}) collective-permute-start(bf16[256,1024]{1,0:T(8,128)(2,1)} %collective-permute-done.42.refs_4_), channel_id=1, source_target_pairs={{0,3},{1,0},{2,1},{3,2},{4,7},{5,4},{6,5},{7,6},{8,11},{9,8},{10,9... | collective-permute-start | bytes 1572872 | tf_op jit(solution)/shard_map/ppermute | solution.py:254
  202.6 13.4 %collective-permute-start.43 = (bf16[256,1024]{1,0:T(8,128)(2,1)}, bf16[256,1024]{1,0:T(8,128)(2,1)S(1)}, u32[]{:S(2)}, u32[]{:S(2)}) collective-permute-start(bf16[256,1024]{1,0:T(8,128)(2,1)} %collective-permute-done.42.refs_4_), channel_id=1, source_target_pairs={{0,1},{1,2},{2,3},{3,0},{4,5},{5,6},{6,7},{7,4},{8,9},{9,10},{10,1... | collective-permute-start | bytes 1572872 | tf_op jit(solution)/shard_map/ppermute | solution.py:254
  204.1 19.8 %collective-permute-start.47 = (bf16[256,1024]{1,0:T(8,128)(2,1)S(1)}, bf16[256,1024]{1,0:T(8,128)(2,1)}, u32[]{:S(2)}, u32[]{:S(2)}) collective-permute-start(bf16[256,1024]{1,0:T(8,128)(2,1)S(1)} %collective-permute-done.39.refs_3_), channel_id=1, source_target_pairs={{0,4},{1,5},{2,6},{3,7},{4,0},{5,1},{6,2},{7,3},{8,12},{9,13},{10,... | collective-permute-start | bytes 1572872 | tf_op jit(solution)/shard_map/ppermute | solution.py:254
  (55 other events, 968.5 us)
